TPU v7x, 32 devices: a whole 2x2x4 slice. The times are simulated.
32 devices in a mesh: row: 4 (over x, core), col: 8 (over z, y).
Axes of the slice: x: 2, y: 2, z: 4, core: 2. Of those that a mesh axis runs over, the one named last changes fastest.
Arguments:
- first_slc: bfloat16 [2, 2048, 2048], P(None, ('row', 'col')), may hold values from -200 to 200, as said below
- second_slc: bfloat16 [2, 2048, 2048], P(None, ('row', 'col')), may hold values from -200 to 200, as said below
Outputs:
- solution: float32 [2048, 2048], P('row', 'col')
- residual: float32 [2048, 2048], P('row', 'col')
Inputs may be any that keep to these rules, and one draw needn't show every extreme that they name: `first_slc`: parts of a complex image. `second_slc`: parts of a complex image.
All inputs are finite; a program needn't handle non-finite values.
Results may differ from a plain program's by a relative error of at most 0.00155.
Values may be sent and summed in bfloat16 or wider, within the bound.
No kernel may reach another device: no remote copies, remote signals or barrier semaphores. Data moves between devices by JAX's collectives and lax.ppermute only.
A program may use at most 128 MiB of HBM per device.

v0:
```python
import functools
import math

import jax
import jax.numpy as jnp
import ml_dtypes
import numpy as np
from jax import lax
from jax.experimental import pallas as pl
from jax.experimental.pallas import tpu as pltpu
from jax.sharding import PartitionSpec as P

EPS = 1e-05
DAMPING = 0.0001
RADIUS = 4
LANES = 128
HALO = 8
TURN = 2.0 * math.pi
VMEM_LIMIT = 40 * 1024 * 1024

ATAN = (
    0.1591549409219458,
    -0.05305126669892651,
    0.03181993346630217,
    -0.022611352052724496,
    0.016957432021882463,
    -0.011990188139443825,
    0.0068498925926071,
    -0.002591499099089036,
    0.00046210915702298266,
)
COS = (
    0.9999999997806517,
    -4.934802137228286,
    4.0587091643402005,
    -1.3352120566397616,
    0.23493755882899706,
    -0.024396716411350872,
)


def taps():
    offsets = np.arange(-RADIUS, RADIUS + 1).astype(np.float64)
    weights = np.exp(-offsets * offsets / 8.0)
    weights = weights / weights.sum()
    return [float(weights[RADIUS + j]) for j in range(RADIUS + 1)]


def cosine_table(count):
    j = np.arange(count)[:, None].astype(np.float64)
    i = np.arange(count)[None, :].astype(np.float64)
    table = np.cos(np.pi * j * (i + 0.5) / count) * np.sqrt(2.0 / count)
    table[0] = np.sqrt(1.0 / count)
    return table


def two_parts(table):
    table = table.astype(np.float32)
    high = table.astype(ml_dtypes.bfloat16)
    low = (table - high.astype(np.float32)).astype(ml_dtypes.bfloat16)
    return np.ascontiguousarray(high), np.ascontiguousarray(low)


def inverse_eigen(count_az, count_rg):
    along_az = 2.0 - 2.0 * np.cos(np.pi * np.arange(count_az) / count_az)
    along_rg = 2.0 - 2.0 * np.cos(np.pi * np.arange(count_rg) / count_rg)
    return (1.0 / (DAMPING + along_az[:, None] + along_rg[None, :])).astype(np.float32)


def poly(coefficients, y):
    value = jnp.full_like(y, coefficients[-1])
    for c in coefficients[-2::-1]:
        value = value * y + c
    return value


def angle_turns(im, re):
    a, b = jnp.abs(im), jnp.abs(re)
    big, small = jnp.maximum(a, b), jnp.minimum(a, b)
    t = small / jnp.maximum(big, 1e-37)
    p = t * poly(ATAN, t * t)
    p = jnp.where(a > b, 0.25 - p, p)
    p = jnp.where(re < 0.0, 0.5 - p, p)
    return jnp.where(im < 0.0, -p, p)


def edge(phase_p, gain_p, phase_q, gain_q):
    delta = phase_q - phase_p
    delta = delta - jnp.round(delta)
    half = poly(COS, delta * delta)
    weight = gain_p * gain_q * (half * half)
    return weight, weight * delta


def split(value):
    high = value.astype(jnp.bfloat16)
    return high, (value - high.astype(jnp.float32)).astype(jnp.bfloat16)


def dot3(a, b):
    f = functools.partial(jnp.dot, preferred_element_type=jnp.float32)
    return f(a[0], b[1]) + f(a[1], b[0]) + f(a[0], b[0])


def lanes_of(shape):
    return lax.broadcasted_iota(jnp.int32, shape, 1)


def call(body, outs, args, scratch, name, smem_first=True, flops=1000000):
    specs = [pl.BlockSpec(memory_space=pltpu.VMEM)] * len(args)
    if smem_first:
        specs[0] = pl.BlockSpec(memory_space=pltpu.SMEM)
    return pl.pallas_call(
        body,
        out_shape=[jax.ShapeDtypeStruct(s, d) for s, d in outs],
        in_specs=specs,
        out_specs=[pl.BlockSpec(memory_space=pltpu.VMEM)] * len(outs),
        scratch_shapes=scratch,
        compiler_params=pltpu.CompilerParams(vmem_limit_bytes=VMEM_LIMIT),
        cost_estimate=pl.CostEstimate(flops=flops, bytes_accessed=4000000, transcendentals=0),
        name=name,
    )(*args)


def strip_kernel(lines, width, tile, columns, exchange, ids, first, second, above, below, *rest):
    n_out = len(rest) - 3
    outs, (prod, ranged, field) = rest[:n_out], rest[n_out:]
    k = taps()
    own = ids[1]
    inside_above = jnp.where(ids[2] == 0, 0.0, 1.0).astype(jnp.float32)
    inside_below = jnp.where(ids[2] == ids[3] - 1, 0.0, 1.0).astype(jnp.float32)
    height = lines + 2 * HALO

    def products(ar, ai, br, bi, scale=None):
        ar, ai, br, bi = (v.astype(jnp.float32) for v in (ar, ai, br, bi))
        if scale is not None:
            ar, ai, br, bi = (v * scale for v in (ar, ai, br, bi))
        return (ar * br + ai * bi, ai * br - ar * bi, ar * ar + ai * ai, br * br + bi * bi)

    zero = jnp.zeros((height, LANES), jnp.float32)
    for f in range(4):
        prod[f, :, 0:LANES] = zero
        prod[f, :, LANES + width :] = zero
    step = min(width, 512)
    for c in range(0, width, step):
        at = slice(LANES + c, LANES + c + step)
        cs = slice(c, c + step)
        rows = min(lines, 16)
        for r in range(0, lines, rows):
            rs = slice(r, r + rows)
            values = products(first[0, rs, cs], first[1, rs, cs], second[0, rs, cs], second[1, rs, cs])
            for f in range(4):
                prod[f, HALO + r : HALO + r + rows, at] = values[f]
        for ref, r, scale in ((above, 0, inside_above), (below, HALO + lines, inside_below)):
            values = products(ref[0, :, cs], ref[1, :, cs], ref[2, :, cs], ref[3, :, cs], scale)
            for f in range(4):
                prod[f, r : r + HALO, at] = values[f]

    step = min(width, 1024)
    for f in range(4):
        for r in range(0, height, 8):
            for c in range(0, width, step):
                x = prod[f, r : r + 8, c : c + step + 2 * LANES]
                n = step + 2 * LANES
                total = k[0] * x
                for j in range(1, RADIUS + 1):
                    total = total + k[j] * (pltpu.roll(x, j, 1) + pltpu.roll(x, n - j, 1))
                ranged[f, r : r + 8, c : c + step] = total[:, LANES : LANES + step]

    def phase_gain(smoothed):
        re, im, one, two = smoothed
        gain = jnp.sqrt(re * re + im * im) / (jnp.sqrt(one * two) + EPS)
        return angle_turns(im, re), gain

    for f in range(2):
        field[f, :, 0:LANES] = zero[:lines]
        field[f, :, LANES + width :] = zero[:lines]
    rows = min(lines, 32)
    sub = lax.broadcasted_iota(jnp.int32, (HALO, 1), 0)
    low = jnp.zeros((HALO, 1), jnp.float32)
    high = jnp.zeros((HALO, 1), jnp.float32)
    for j in range(RADIUS + 1):
        low = jnp.where(sub == HALO - 1 - j, k[j], low)
        high = jnp.where(sub == j - 1, k[j], high)
    top, bottom = [], []
    for c in range(0, width, LANES):
        cs = slice(c, c + LANES)
        for r in range(0, lines, rows):
            smoothed = []
            for f in range(4):
                b = HALO + r
                total = k[0] * ranged[f, b : b + rows, cs]
                for j in range(1, RADIUS + 1):
                    total = total + k[j] * (
                        ranged[f, b - j : b - j + rows, cs] + ranged[f, b + j : b + j + rows, cs]
                    )
                smoothed.append(total)
            phase, gain = phase_gain(smoothed)
            field[0, r : r + rows, LANES + c : 2 * LANES + c] = phase
            field[1, r : r + rows, LANES + c : 2 * LANES + c] = gain

    step = min(width, 1024)
    low = low + jnp.zeros((HALO, step), jnp.float32)
    high = high + jnp.zeros((HALO, step), jnp.float32)
    mirror_low = jnp.zeros((HALO, 1), jnp.float32)
    mirror_high = jnp.zeros((HALO, 1), jnp.float32)
    for j in range(RADIUS + 1):
        mirror_high = jnp.where(sub == j, k[j], mirror_high)
        mirror_low = jnp.where(sub == HALO - j, k[j], mirror_low)
    ends = []
    for c in range(0, width, step):
        cs = slice(c, c + step)
        up = [
            jnp.sum(low * ranged[f, 0:HALO, cs] + high * ranged[f, HALO : 2 * HALO, cs], axis=0, keepdims=True)
            for f in range(4)
        ]
        down = [
            jnp.sum(
                mirror_low * ranged[f, lines : lines + HALO, cs]
                + mirror_high * ranged[f, lines + HALO : lines + 2 * HALO, cs],
                axis=0,
                keepdims=True,
            )
            for f in range(4)
        ]
        up_phase, up_gain = phase_gain(up)
        down_phase, down_gain = phase_gain(down)
        ends.append((up_phase, down_phase, up_gain * inside_above, down_gain * inside_below))
    for i, (a, b, c_, d) in enumerate(ends):
        at = slice(i * step, (i + 1) * step)
        prod[0, 0:1, at] = a
        prod[0, 1:2, at] = b
        prod[0, 2:3, at] = c_
        prod[0, 3:4, at] = d

    groups = lines // 8
    lane = lanes_of((8, LANES))

    def pack(out, start, aligned):
        hint = pl.multiple_of if aligned else (lambda v, _: v)
        out[0:lines, :] = field[0, :, pl.ds(hint(start + LANES, LANES), tile)]
        out[lines : 2 * lines, :] = field[1, :, pl.ds(hint(start + LANES, LANES), tile)]
        block = jnp.zeros((8, LANES), jnp.float32)
        for f in range(2):
            for side in range(2):
                offset = start if side == 0 else start + LANES + tile
                for g in range(groups):
                    target = (f * 2 + side) * groups + g
                    x = field[f, 8 * g : 8 * g + 8, pl.ds(hint(offset, LANES), LANES)]
                    shift = (target - (LANES - 1 if side == 0 else 0)) % LANES
                    if shift:
                        x = pltpu.roll(x, shift, 1)
                    block = jnp.where(lane == target, x, block)
        base = 2 * lines
        out[base : base + 8, 0:LANES] = block
        for i in range(4):
            for h in range(tile // LANES):
                out[base + 2 * i + h : base + 2 * i + h + 1, LANES : 2 * LANES] = prod[
                    0, i : i + 1, pl.ds(hint(start + h * LANES, LANES), LANES)
                ]

    if exchange == "permute":
        for s in range(columns):
            pack(outs[s], (own ^ s) * tile, True)
    else:
        for s in range(columns):
            pack(outs[0].at[s], s * tile, False)


def precondition(field, tables, inverse):
    az, az_t, rg, rg_t = tables
    coef = dot3(az, split(field))
    coef = dot3(split(coef), rg_t)
    coef = coef * inverse[...]
    back = dot3(az_t, split(coef))
    return dot3(split(back), rg)


def line_groups(ref, tile_az, edge_lane):
    lane = lanes_of((8, LANES))
    first = (edge_lane // LANES) * LANES
    block = jnp.zeros((8, LANES), jnp.float32)
    for g in range(tile_az // 8):
        x = ref[8 * g : 8 * g + 8, first : first + LANES]
        shift = (g - edge_lane) % LANES
        if shift:
            x = pltpu.roll(x, shift, 1)
        block = jnp.where(lane == g, x, block)
    return block


def spread_groups(block, first_group, count, target_lane, base=0):
    parts = []
    for g in range(first_group, first_group + count):
        shift = (target_lane - (base + g)) % LANES
        parts.append(pltpu.roll(block, shift, 1) if shift else block)
    return jnp.concatenate(parts, axis=0) if count > 1 else parts[0]


def shifted_right(x, left):
    lane = lanes_of(x.shape)
    if left is None:
        return jnp.where(lane == 0, 0.0, pltpu.roll(x, 1, 1))
    wide = jnp.concatenate([left] * (x.shape[1] // LANES), axis=1)
    return jnp.where(lane == 0, wide, pltpu.roll(x, 1, 1))


def shifted_left(x, right):
    lane = lanes_of(x.shape)
    wide = jnp.concatenate([right] * (x.shape[1] // LANES), axis=1)
    return jnp.where(lane == x.shape[1] - 1, wide, pltpu.roll(x, x.shape[1] - 1, 1))


def divergence(tile_az, step, along_x, rim_x, along_y, r):
    rs = slice(r, r + step)
    x = along_x[rs, :]
    return (x - shifted_left(x, rim_x[rs, :])) + along_y[rs, :] - along_y[r + 1 : r + 1 + step, :]


def tile_kernel(lines, tile_az, tile, columns, exchange, ids, *rest):
    chunks = rest[: columns if exchange == "permute" else 1]
    rest = rest[len(chunks) :]
    tables, inverse = rest[:8], rest[8]
    residual, shaped, weight_x, rim_x, weight_y, rows_out, left_out, right_out = rest[9:17]
    phase, gain, sides, ends, flux_x, flux_rim, flux_y = rest[17:]
    own = ids[1]
    pairs = [(tables[2 * i][...], tables[2 * i + 1][...]) for i in range(4)]

    for s in range(columns):
        if exchange == "permute":
            src, strip = chunks[s], own ^ s
        else:
            src, strip = chunks[0].at[s], s
        row = strip * lines
        if exchange == "permute":
            row = pl.multiple_of(row, 8)
        phase[pl.ds(HALO + row, lines), :] = src[0:lines, :]
        gain[pl.ds(HALO + row, lines), :] = src[lines : 2 * lines, :]
        base = 2 * lines
        at = pl.ds(pl.multiple_of(strip * 8, 8), 8) if exchange == "permute" else pl.ds(strip * 8, 8)
        sides[at, :] = src[base : base + 8, 0:LANES]
        ends[at, :] = src[base : base + 8, LANES : 2 * LANES]
    last = 8 * (columns - 1)
    for h in range(tile // LANES):
        cs = slice(h * LANES, (h + 1) * LANES)
        phase[HALO - 1 : HALO, cs] = ends[h : h + 1, :]
        gain[HALO - 1 : HALO, cs] = ends[4 + h : 5 + h, :]
        phase[HALO + tile_az : HALO + tile_az + 1, cs] = ends[last + 2 + h : last + 3 + h, :]
        gain[HALO + tile_az : HALO + tile_az + 1, cs] = ends[last + 6 + h : last + 7 + h, :]

    step = min(tile_az, 32)
    groups = lines // 8
    for r in range(0, tile_az, step):
        rs = slice(r, r + step)
        b = HALO + r
        p, g = phase[b : b + step, :], gain[b : b + step, :]
        halo = []
        for f in range(2):
            for side in range(2):
                parts = []
                for line_group in range(r // 8, (r + step) // 8):
                    strip, inner = divmod(line_group, groups)
                    block = sides[8 * strip : 8 * strip + 8, :]
                    source_lane = (f * 2 + side) * groups + inner
                    shift = ((0 if side == 0 else LANES - 1) - source_lane) % LANES
                    parts.append(pltpu.roll(block, shift, 1) if shift else block)
                halo.append(jnp.concatenate(parts, axis=0) if len(parts) > 1 else parts[0])
        w, f = edge(shifted_right(p, halo[0]), shifted_right(g, halo[2]), p, g)
        weight_x[rs, :] = w
        flux_x[rs, :] = f
        w, f = edge(p[:, tile - LANES :], g[:, tile - LANES :], halo[1], halo[3])
        rim_x[rs, :] = w
        flux_rim[rs, :] = f
        w, f = edge(phase[b - 1 : b - 1 + step, :], gain[b - 1 : b - 1 + step, :], p, g)
        weight_y[rs, :] = w
        flux_y[rs, :] = f
    b = HALO + tile_az
    w, f = edge(
        phase[b - 1 : b, :], gain[b - 1 : b, :], phase[b : b + 1, :], gain[b : b + 1, :]
    )
    weight_y[tile_az : tile_az + 8, :] = jnp.broadcast_to(w, (8, tile))
    flux_y[tile_az : tile_az + 8, :] = jnp.broadcast_to(f, (8, tile))

    for r in range(0, tile_az, step):
        residual[r : r + step, :] = TURN * divergence(tile_az, step, flux_x, flux_rim, flux_y, r)
    shaped[...] = precondition(residual[...], pairs, inverse)
    rows_out[0, 0:1, :] = shaped[0:1, :]
    rows_out[1, 0:1, :] = shaped[tile_az - 1 : tile_az, :]
    left_out[...] = line_groups(shaped, tile_az, 0)
    right_out[...] = line_groups(shaped, tile_az, tile - 1)


def apply_operator(tile_az, tile, u, weight_x, rim_x, weight_y, flux_x, flux_rim, flux_y, left, right, out):
    step = min(tile_az, 32)
    for r in range(0, tile_az, step):
        rs = slice(r, r + step)
        b = HALO + r
        x = u[b : b + step, :]
        l = None if left is None else spread_groups(left, r // 8, step // 8, 0)
        flux_x[rs, :] = weight_x[rs, :] * (x - shifted_right(x, l))
        edge_x = x[:, tile - LANES :]
        if right is None:
            flux_rim[rs, :] = -rim_x[rs, :] * edge_x
        else:
            flux_rim[rs, :] = rim_x[rs, :] * (spread_groups(right, r // 8, step // 8, LANES - 1) - edge_x)
        flux_y[rs, :] = weight_y[rs, :] * (x - u[b - 1 : b - 1 + step, :])
    b = HALO + tile_az
    flux_y[tile_az : tile_az + 1, :] = weight_y[tile_az : tile_az + 1, :] * (u[b : b + 1, :] - u[b - 1 : b, :])
    for r in range(0, tile_az, step):
        out[r : r + step, :] = DAMPING * u[HALO + r : HALO + r + step, :] + divergence(
            tile_az, step, flux_x, flux_rim, flux_y, r
        )


def inner(a, b, tile_az, offset_a=0, offset_b=0):
    total = jnp.zeros((32, a.shape[1]), jnp.float32)
    for r in range(0, tile_az, 32):
        total = total + a[offset_a + r : offset_a + r + 32, :] * b[offset_b + r : offset_b + r + 32, :]
    return jnp.sum(jnp.sum(total, axis=0, keepdims=True), axis=1, keepdims=True)


def second_kernel(
    tile_az, tile, residual, shaped, weight_x, rim_x, weight_y, up, down, left, right, *rest
):
    tables, inverse = rest[:8], rest[8]
    operated, shaped2, operated2, chunk = rest[9:13]
    u, flux_x, flux_rim, flux_y = rest[13:]
    pairs = [(tables[2 * i][...], tables[2 * i + 1][...]) for i in range(4)]
    u[HALO : HALO + tile_az, :] = shaped[...]
    u[HALO - 1 : HALO, :] = up[0:1, :]
    u[HALO + tile_az : HALO + tile_az + 1, :] = down[0:1, :]
    apply_operator(
        tile_az, tile, u, weight_x, rim_x, weight_y, flux_x, flux_rim, flux_y, left[...], right[...], operated
    )
    image = precondition(operated[...], pairs, inverse)
    shaped2[...] = image
    u[HALO : HALO + tile_az, :] = image
    zero = jnp.zeros((1, tile), jnp.float32)
    u[HALO - 1 : HALO, :] = zero
    u[HALO + tile_az : HALO + tile_az + 1, :] = zero
    apply_operator(
        tile_az, tile, u, weight_x, rim_x, weight_y, flux_x, flux_rim, flux_y, None, None, operated2
    )
    lane = lanes_of((1, LANES))
    sums = jnp.zeros((1, LANES), jnp.float32)
    for i, (a, b) in enumerate(
        (
            (residual, shaped),
            (shaped, operated),
            (residual, shaped2),
            (operated, shaped2),
            (shaped2, operated2),
        )
    ):
        sums = jnp.where(lane == i, inner(a, b, tile_az), sums)
    chunk[8:16, :] = jnp.broadcast_to(sums, (8, LANES))
    top = jnp.sqrt(weight_y[0:1, :]) * shaped2[0:1, :]
    bottom = jnp.sqrt(weight_y[tile_az : tile_az + 1, :]) * shaped2[tile_az - 1 : tile_az, :]
    for h in range(tile // LANES):
        cs = slice(h * LANES, (h + 1) * LANES)
        chunk[8 + 2 + h : 8 + 3 + h, :] = top[:, cs]
        chunk[8 + 4 + h : 8 + 5 + h, :] = bottom[:, cs]
    half = tile_az // 8
    left_rim = jnp.sqrt(line_groups(weight_x, tile_az, 0)) * line_groups(shaped2, tile_az, 0)
    right_rim = jnp.sqrt(line_groups(rim_x, tile_az, LANES - 1)) * line_groups(shaped2, tile_az, tile - 1)
    wide = lanes_of((8, LANES))
    chunk[0:8, :] = jnp.where(wide < half, left_rim, pltpu.roll(right_rim, half, 1))


def last_kernel(
    tile_az, tile, rows, columns, ids, gathered, residual, shaped, operated, shaped2, operated2, weight_x, rim_x,
    weight_y, solution_out, residual_out
):
    half = tile_az // 8
    lane = lanes_of((8, LANES))
    total = jnp.zeros((8, LANES), jnp.float32)
    cross_x = jnp.zeros((8, LANES), jnp.float32)
    cross_y = jnp.zeros((2, LANES), jnp.float32)
    for r in range(rows):
        for c in range(columns):
            i = r * columns + c
            total = total + gathered[i, 8:16, :]
            if c + 1 < columns:
                right = pltpu.roll(gathered[i, 0:8, :], LANES - half, 1)
                cross_x = cross_x + right * gathered[i + 1, 0:8, :]
            if r + 1 < rows:
                cross_y = cross_y + gathered[i, 12:14, :] * gathered[i + columns, 10:12, :]
    cross = jnp.sum(jnp.where(lane < half, cross_x, 0.0), keepdims=True) + jnp.sum(cross_y, keepdims=True)
    wide = total[0:1, :]
    first_lane = lanes_of((1, LANES))
    pick = [
        jnp.sum(jnp.where(first_lane == i, wide, 0.0), axis=1, keepdims=True) for i in range(5)
    ]
    dot0, curve0, mixed, cross_dot, curve2 = pick
    curve2 = curve2 - 2.0 * cross
    alpha = dot0 / curve0
    fresh = dot0 - alpha * (mixed + curve0) + alpha * alpha * cross_dot
    beta = fresh / dot0
    grown = 1.0 + beta
    curve1 = grown * grown * curve0 - 2.0 * alpha * grown * cross_dot + alpha * alpha * curve2
    step1 = fresh / curve1
    on_first = alpha + step1 * grown
    on_second = step1 * alpha

    row, col = ids[0], ids[1]
    here = row * columns + col

    def neighbour(ok, index):
        return jnp.where(ok, index, here), jnp.where(ok, 1.0, 0.0).astype(jnp.float32)

    up, up_ok = neighbour(row > 0, here - columns)
    down, down_ok = neighbour(row < rows - 1, here + columns)
    left, left_ok = neighbour(col > 0, here - 1)
    right, right_ok = neighbour(col < columns - 1, here + 1)
    from_left = pltpu.roll(gathered[left, 0:8, :], LANES - half, 1) * left_ok
    from_right = gathered[right, 0:8, :] * right_ok
    top = jnp.concatenate([gathered[up, 12 + h : 13 + h, :] for h in range(tile // LANES)], axis=1) * up_ok
    bottom = jnp.concatenate([gathered[down, 10 + h : 11 + h, :] for h in range(tile // LANES)], axis=1) * down_ok
    top = top * jnp.sqrt(weight_y[0:1, :])
    bottom = bottom * jnp.sqrt(weight_y[tile_az : tile_az + 1, :])
    from_left = from_left * jnp.sqrt(line_groups(weight_x, tile_az, 0))
    from_right = from_right * jnp.sqrt(line_groups(rim_x, tile_az, LANES - 1))
    step = min(tile_az, 32)
    for r in range(0, tile_az, step):
        rs = slice(r, r + step)
        solution_out[rs, :] = on_first * shaped[rs, :] - on_second * shaped2[rs, :]
        q = operated2[rs, :]
        wide = lanes_of((step, tile))
        l = jnp.concatenate([spread_groups(from_left, r // 8, step // 8, 0)] * (tile // LANES), axis=1)
        q = q - jnp.where(wide == 0, l, 0.0)
        l = jnp.concatenate([spread_groups(from_right, r // 8, step // 8, LANES - 1)] * (tile // LANES), axis=1)
        q = q - jnp.where(wide == tile - 1, l, 0.0)
        deep = lax.broadcasted_iota(jnp.int32, (step, tile), 0)
        if r == 0:
            q = q - jnp.where(deep == 0, jnp.broadcast_to(top, (step, tile)), 0.0)
        if r + step == tile_az:
            q = q - jnp.where(deep == step - 1, jnp.broadcast_to(bottom, (step, tile)), 0.0)
        residual_out[rs, :] = residual[rs, :] - on_first * operated[rs, :] + on_second * q


def around(value, axis, steps):
    count = lax.axis_size(axis)
    return lax.ppermute(value, axis, [(i, (i + steps) % count) for i in range(count)])


def shards(rows, columns, first_slc, second_slc):
    lines, width = first_slc.shape[1:]
    tile = width // columns
    tile_az = lines * columns
    axes = ("row", "col")
    exchange = "permute" if columns <= 8 else "all_to_all"
    row, col = lax.axis_index("row"), lax.axis_index("col")
    ids = jnp.stack([row, col, row * columns + col, jnp.int32(rows * columns)]).astype(jnp.int32)
    f32 = jnp.float32
    height = lines + 2 * HALO

    above = around(jnp.concatenate([first_slc[:, -HALO:], second_slc[:, -HALO:]], 0), axes, 1)
    below = around(jnp.concatenate([first_slc[:, :HALO], second_slc[:, :HALO]], 0), axes, -1)
    depth = 2 * lines + 8
    if exchange == "permute":
        outs = [((depth, tile), f32)] * columns
    else:
        outs = [((columns, depth, tile), f32)]
    sent = call(
        functools.partial(strip_kernel, lines, width, tile, columns, exchange),
        outs,
        (ids, first_slc, second_slc, above, below),
        [
            pltpu.VMEM((4, height, width + 2 * LANES), f32),
            pltpu.VMEM((4, height, width), f32),
            pltpu.VMEM((2, lines, width + 2 * LANES), f32),
        ],
        "strips",
    )
    if exchange == "permute":
        order = [4, 5, 6, 7, 2, 3, 1]
        arrived = [sent[0]] + [None] * (columns - 1)
        for s in order:
            if s < columns:
                arrived[s] = lax.ppermute(sent[s], "col", [(i, i ^ s) for i in range(columns)])
    else:
        arrived = [lax.all_to_all(sent[0], "col", 0, 0, tiled=True)]

    az, rg = cosine_table(tile_az), cosine_table(tile)
    tables = []
    for table in (az, az.T, rg, rg.T):
        tables.extend(jnp.asarray(part) for part in two_parts(table))
    inverse = jnp.asarray(inverse_eigen(tile_az, tile))

    whole = ((tile_az, tile), f32)
    column = ((8, LANES), f32)
    padded = pltpu.VMEM((tile_az + 2 * HALO, tile), f32)
    fluxes = [
        pltpu.VMEM((tile_az, tile), f32),
        pltpu.VMEM((tile_az, LANES), f32),
        pltpu.VMEM((tile_az + 8, tile), f32),
    ]
    residual, shaped, weight_x, rim_x, weight_y, ends, left_col, right_col = call(
        functools.partial(tile_kernel, lines, tile_az, tile, columns, exchange),
        [whole, whole, whole, ((tile_az, LANES), f32), ((tile_az + 8, tile), f32), ((2, 1, tile), f32), column, column],
        (ids, *arrived, *tables, inverse),
        [padded, padded, pltpu.VMEM((8 * columns, LANES), f32), pltpu.VMEM((8 * columns, LANES), f32), *fluxes],
        "tiles",
    )
    down = around(ends[0], "row", -1)
    up = around(ends[1], "row", 1)
    right = around(left_col, "col", -1)
    left = around(right_col, "col", 1)
    operated, shaped2, operated2, chunk = call(
        functools.partial(second_kernel, tile_az, tile),
        [whole, whole, whole, ((16, LANES), f32)],
        (residual, shaped, weight_x, rim_x, weight_y, up, down, left, right, *tables, inverse),
        [padded, *fluxes],
        "operator",
        smem_first=False,
    )
    spread = jnp.broadcast_to(chunk[None], (rows * columns, 16, LANES))
    gathered = lax.all_to_all(spread, axes, 0, 0, tiled=True)
    return tuple(
        call(
            functools.partial(last_kernel, tile_az, tile, rows, columns),
            [whole, whole],
            (ids, gathered, residual, shaped, operated, shaped2, operated2, weight_x, rim_x, weight_y),
            [],
            "finish",
        )
    )


def solution(mesh):
    placed = P(None, ("row", "col"), None)
    return jax.shard_map(
        functools.partial(shards, mesh.shape["row"], mesh.shape["col"]),
        mesh=mesh,
        in_specs=(placed, placed),
        out_specs=(P("row", "col"), P("row", "col")),
        check_vma=False,
    )
```

profile of v0, /device:TPU:0, one launch (start us, length us, event | category | flops | bytes accessed | tf_op | source)
XLA Modules:
  0.0 87.4 jit_solution(1917858428306088816)
XLA Ops:
  0.6 1.0 %fusion = (bf16[2,8,2048]{2,1,0:T(8,128)(2,1)S(1)}, bf16[2,8,2048]{2,1,0:T(8,128)(2,1)S(1)}, bf16[2,8,2048]{2,1,0:T(8,128)(2,1)S(1)}, bf16[2,8,2048]{2,1,0:T(8,128)(2,1)S(1)}) fusion(bf16[2,64,2048]{2,1,0:T(8,128)(2,1)} %first.1, bf16[2,64,2048]{2,1,0:T(8,128)(2,1)} %second.1), kind=kLoop, calls=%fused_computation.5 | loop fusion | bytes 524288 | tf_op jit(solution)/shard_map/slice | solution.py:558
  1.7 3.0 %collective-permute-start = (bf16[4,8,2048]{2,1,0:T(8,128)(2,1)S(1)}, bf16[4,8,2048]{2,1,0:T(8,128)(2,1)S(1)}, u32[]{:S(2)}, u32[]{:S(2)}) collective-permute-start(bf16[4,8,2048]{2,1,0:T(8,128)(2,1)S(1)} %pad_maximum_fusion), channel_id=1, source_target_pairs={{0,1},{1,2},{2,3},{3,4},{4,5},{5,6},{6,7},{7,8},{8,9},{9,10},{10,1... | collective-permute-start | bytes 393224 | tf_op jit(solution)/shard_map/ppermute | solution.py:543
  4.8 3.5 %collective-permute-start.1 = (bf16[4,8,2048]{2,1,0:T(8,128)(2,1)S(1)}, bf16[4,8,2048]{2,1,0:T(8,128)(2,1)S(1)}, u32[]{:S(2)}, u32[]{:S(2)}) collective-permute-start(bf16[4,8,2048]{2,1,0:T(8,128)(2,1)S(1)} %pad_maximum_fusion.1), channel_id=1, source_target_pairs={{0,31},{1,0},{2,1},{3,2},{4,3},{5,4},{6,5},{7,6},{8,7},{9,8},{10,9... | collective-permute-start | bytes 393224 | tf_op jit(solution)/shard_map/ppermute | solution.py:543
  8.3 3.7 %collective-permute-done.above = bf16[4,8,2048]{2,1,0:T(8,128)(2,1)S(1)} collective-permute-done((bf16[4,8,2048]{2,1,0:T(8,128)(2,1)S(1)}, bf16[4,8,2048]{2,1,0:T(8,128)(2,1)S(1)}, u32[]{:S(2)}, u32[]{:S(2)}) %collective-permute-start) | collective-permute-done | bytes 131104 | tf_op jit(solution)/shard_map/ppermute | solution.py:543
  12.6 1.0 %copy-done.6 = bf16[2,64,2048]{2,1,0:T(8,128)(2,1)S(1)} copy-done((bf16[2,64,2048]{2,1,0:T(8,128)(2,1)S(1)}, bf16[2,64,2048]{2,1,0:T(8,128)(2,1)}, u32[]{:S(2)}) %copy-start.6) | copy-done | bytes 524312
  13.6 1.0 %copy-done.7 = bf16[2,64,2048]{2,1,0:T(8,128)(2,1)S(1)} copy-done((bf16[2,64,2048]{2,1,0:T(8,128)(2,1)S(1)}, bf16[2,64,2048]{2,1,0:T(8,128)(2,1)}, u32[]{:S(2)}) %copy-start.7) | copy-done | bytes 524312
  14.7 8.7 %strips.1 = (f32[136,256]{1,0:T(8,128)S(1)}, f32[136,256]{1,0:T(8,128)S(1)}, f32[136,256]{1,0:T(8,128)S(1)}, f32[136,256]{1,0:T(8,128)S(1)}, f32[136,256]{1,0:T(...) custom-call(s32[4]{0:T(128)S(1)} %pad_add_fusion.ids, ...), custom_call_target="tpu_custom_call" | custom-call | flops 1000000 | bytes 4000000 | tf_op jit(solution)/shard_map/strips/pallas_call | solution.py:113
  23.6 1.6 %collective-permute-start.3 = (f32[136,256]{1,0:T(8,128)S(1)}, f32[136,256]{1,0:T(8,128)S(1)}, u32[]{:S(2)}, u32[]{:S(2)}) collective-permute-start(f32[136,256]{1,0:T(8,128)S(1)} %get-tuple-element.24), channel_id=1, source_target_pairs={{0,2},{1,3},{2,0},{3,1},{4,6},{5,7},{6,4},{7,5},{8,10},{9,11},{10,... | collective-permute-start | bytes 417800 | tf_op jit(solution)/shard_map/ppermute | solution.py:580
  25.2 1.7 %collective-permute-start.4 = (f32[136,256]{1,0:T(8,128)S(1)}, f32[136,256]{1,0:T(8,128)S(1)}, u32[]{:S(2)}, u32[]{:S(2)}) collective-permute-start(f32[136,256]{1,0:T(8,128)S(1)} %get-tuple-element.25), channel_id=1, source_target_pairs={{0,3},{1,2},{2,1},{3,0},{4,7},{5,6},{6,5},{7,4},{8,11},{9,10},{10,... | collective-permute-start | bytes 417800 | tf_op jit(solution)/shard_map/ppermute | solution.py:580
  26.9 2.2 %collective-permute-start.5 = (f32[136,256]{1,0:T(8,128)S(1)}, f32[136,256]{1,0:T(8,128)S(1)}, u32[]{:S(2)}, u32[]{:S(2)}) collective-permute-start(f32[136,256]{1,0:T(8,128)S(1)} %get-tuple-element.26), channel_id=1, source_target_pairs={{0,4},{1,5},{2,6},{3,7},{4,0},{5,1},{6,2},{7,3},{8,12},{9,13},{10,... | collective-permute-start | bytes 417800 | tf_op jit(solution)/shard_map/ppermute | solution.py:580
  29.5 3.2 %collective-permute-start.7 = (f32[136,256]{1,0:T(8,128)S(1)}, f32[136,256]{1,0:T(8,128)S(1)}, u32[]{:S(2)}, u32[]{:S(2)}) collective-permute-start(f32[136,256]{1,0:T(8,128)S(1)} %get-tuple-element.28), channel_id=1, source_target_pairs={{0,6},{1,7},{2,4},{3,5},{4,2},{5,3},{6,0},{7,1},{8,14},{9,15},{10,... | collective-permute-start | bytes 417800 | tf_op jit(solution)/shard_map/ppermute | solution.py:580
  32.7 3.2 %collective-permute-start.8 = (f32[136,256]{1,0:T(8,128)S(1)}, f32[136,256]{1,0:T(8,128)S(1)}, u32[]{:S(2)}, u32[]{:S(2)}) collective-permute-start(f32[136,256]{1,0:T(8,128)S(1)} %get-tuple-element.29), channel_id=1, source_target_pairs={{0,7},{1,6},{2,5},{3,4},{4,3},{5,2},{6,1},{7,0},{8,15},{9,14},{10,... | collective-permute-start | bytes 417800 | tf_op jit(solution)/shard_map/ppermute | solution.py:580
  35.9 1.4 %collective-permute-done.4.rest_3_ = f32[136,256]{1,0:T(8,128)S(1)} collective-permute-done((f32[136,256]{1,0:T(8,128)S(1)}, f32[136,256]{1,0:T(8,128)S(1)}, u32[]{:S(2)}, u32[]{:S(2)}) %collective-permute-start.4) | collective-permute-done | bytes 139296 | tf_op jit(solution)/shard_map/ppermute | solution.py:580
  37.3 12.1 %collective-permute-done.6.rest_5_ = f32[136,256]{1,0:T(8,128)S(1)} collective-permute-done((f32[136,256]{1,0:T(8,128)S(1)}, f32[136,256]{1,0:T(8,128)S(1)}, u32[]{:S(2)}, u32[]{:S(2)}) %collective-permute-start.6) | collective-permute-done | bytes 139296 | tf_op jit(solution)/shard_map/ppermute | solution.py:580
  49.5 1.0 %copy-done.4 = bf16[512,512]{1,0:T(8,128)(2,1)S(1)} copy-done((bf16[512,512]{1,0:T(8,128)(2,1)S(1)}, bf16[512,512]{1,0:T(8,128)(2,1)}, u32[]{:S(2)}) %copy-start.4) | copy-done | bytes 524312
  50.5 0.9 %copy-done.10 = bf16[256,256]{1,0:T(8,128)(2,1)S(1)} copy-done((bf16[256,256]{1,0:T(8,128)(2,1)S(1)}, bf16[256,256]{1,0:T(8,128)(2,1)}, u32[]{:S(2)}) %copy-start.10) | copy-done | bytes 131096
  51.4 0.9 %copy-done.11 = bf16[256,256]{1,0:T(8,128)(2,1)S(1)} copy-done((bf16[256,256]{1,0:T(8,128)(2,1)S(1)}, bf16[256,256]{1,0:T(8,128)(2,1)}, u32[]{:S(2)}) %copy-start.11) | copy-done | bytes 131096
  52.3 4.4 %tiles.1 = (f32[512,256]{1,0:T(8,128)S(1)}, f32[512,256]{1,0:T(8,128)S(1)}, f32[512,256]{1,0:T(8,128)S(1)}, f32[512,128]{1,0:T(8,128)S(1)}, f32[520,256]{1,0:T(8...) custom-call(s32[4]{0:T(128)S(1)} %pad_add_fusion.ids, ...), custom_call_target="tpu_custom_call" | custom-call | flops 1000000 | bytes 4000000 | tf_op jit(solution)/shard_map/tiles/pallas_call | solution.py:113
  57.3 4.2 %collective-permute-start.12 = (f32[8,128]{1,0:T(8,128)S(1)}, f32[8,128]{1,0:T(8,128)S(1)}, u32[]{:S(2)}, u32[]{:S(2)}) collective-permute-start(f32[8,128]{1,0:T(8,128)S(1)} %get-tuple-element.37), channel_id=1, source_target_pairs={{0,7},{1,0},{2,1},{3,2},{4,3},{5,4},{6,5},{7,6},{8,15},{9,8},{10,9... | collective-permute-start | bytes 12296 | tf_op jit(solution)/shard_map/ppermute | solution.py:543
  62.0 0.8 collective-permute-done.10.down
  62.8 1.7 %collective-permute-done.9.up = f32[1,256]{1,0:T(1,128)S(1)} collective-permute-done((f32[1,256]{1,0:T(1,128)S(1)}, f32[1,256]{1,0:T(1,128)S(1)}, u32[]{:S(2)}, u32[]{:S(2)}) %collective-permute-start.9) | collective-permute-done | bytes 1056 | tf_op jit(solution)/shard_map/ppermute | solution.py:543
  65.2 3.8 %operator.1 = (f32[512,256]{1,0:T(8,128)S(1)}, f32[512,256]{1,0:T(8,128)S(1)}, f32[512,256]{1,0:T(8,128)S(1)}, f32[16,128]{1,0:T(8,128)S(1)}) custom-call(f32[512,256]{1,0:T(8,128)S(1)} %get-tuple-element.30.residual, f32[512,256]{1,0:T(8,128)S(1)} %get-tuple-element.31.shaped, f32[512,256]{1,0:T(8,128)S(1)} %get-tuple-element.32.weight_x, ...), custom_call_target="tpu_custom_call" | custom-call | flops 1000000 | bytes 4000000 | tf_op jit(solution)/shard_map/operator/pallas_call | solution.py:113
  69.0 16.5 %all_to_all.5.gathered = f32[32,16,128]{2,1,0:T(8,128)S(1)} all-to-all(f32[32,16,128]{2,1,0:T(8,128)S(1)} %broadcast_in_dim.2), channel_id=1, replica_groups=mesh['row'=4,'col'=8] {'row','col'}, dimensions={0} | all-to-all | bytes 524288 | tf_op jit(solution)/shard_map/all_to_all | solution.py:618
  85.5 1.9 %finish.1 = (f32[512,256]{1,0:T(8,128)}, f32[512,256]{1,0:T(8,128)}) custom-call(s32[4]{0:T(128)S(1)} %pad_add_fusion.ids, f32[32,16,128]{2,1,0:T(8,128)S(1)} %all_to_all.5.gathered, f32[512,256]{1,0:T(8,128)S(1)} %get-tuple-element.30.residual, f32[512,256]{1,0:T(8,128)S(1)} %get-tuple-element.31.shaped, f32[512,256]{1,0:T(8,128)S(1)} %get-tuple-element.39.operated, ...), custom_call_target="tpu_custom_call" | custom-call | flops 1000000 | bytes 4000000 | tf_op jit(solution)/shard_map/finish/pallas_call | solution.py:113
  (37 shorter events, 3.1 us)
Async XLA Ops:
  0.6 48.8 %copy-start.3 = (bf16[512,512]{1,0:T(8,128)(2,1)S(1)}, bf16[512,512]{1,0:T(8,128)(2,1)}, u32[]{:S(2)}) copy-start(bf16[512,512]{1,0:T(8,128)(2,1)} %constant.31.clone.rest_9_.rest_1_) | copy-start | bytes 1572868
  1.7 47.8 %copy-start.8 = (bf16[256,256]{1,0:T(8,128)(2,1)S(1)}, bf16[256,256]{1,0:T(8,128)(2,1)}, u32[]{:S(2)}) copy-start(bf16[256,256]{1,0:T(8,128)(2,1)} %constant.37.clone.rest_15_.rest_7_) | copy-start | bytes 393220
  1.7 47.8 %copy-start.9 = (bf16[256,256]{1,0:T(8,128)(2,1)S(1)}, bf16[256,256]{1,0:T(8,128)(2,1)}, u32[]{:S(2)}) copy-start(bf16[256,256]{1,0:T(8,128)(2,1)} %constant.36.clone.rest_14_.rest_6_) | copy-start | bytes 393220
  1.7 10.4 %collective-permute-start = (bf16[4,8,2048]{2,1,0:T(8,128)(2,1)S(1)}, bf16[4,8,2048]{2,1,0:T(8,128)(2,1)S(1)}, u32[]{:S(2)}, u32[]{:S(2)}) collective-permute-start(bf16[4,8,2048]{2,1,0:T(8,128)(2,1)S(1)} %pad_maximum_fusion), channel_id=1, source_target_pairs={{0,1},{1,2},{2,3},{3,4},{4,5},{5,6},{6,7},{7,8},{8,9},{9,10},{10,1... | collective-permute-start | bytes 393224 | tf_op jit(solution)/shard_map/ppermute | solution.py:543
  4.7 44.7 %copy-start.2 = (bf16[512,512]{1,0:T(8,128)(2,1)S(1)}, bf16[512,512]{1,0:T(8,128)(2,1)}, u32[]{:S(2)}) copy-start(bf16[512,512]{1,0:T(8,128)(2,1)} %constant.32.clone.rest_10_.rest_2_) | copy-start | bytes 1572868
  4.8 7.8 %collective-permute-start.1 = (bf16[4,8,2048]{2,1,0:T(8,128)(2,1)S(1)}, bf16[4,8,2048]{2,1,0:T(8,128)(2,1)S(1)}, u32[]{:S(2)}, u32[]{:S(2)}) collective-permute-start(bf16[4,8,2048]{2,1,0:T(8,128)(2,1)S(1)} %pad_maximum_fusion.1), channel_id=1, source_target_pairs={{0,31},{1,0},{2,1},{3,2},{4,3},{5,4},{6,5},{7,6},{8,7},{9,8},{10,9... | collective-permute-start | bytes 393224 | tf_op jit(solution)/shard_map/ppermute | solution.py:543
  8.3 41.1 %copy-start = (f32[512,256]{1,0:T(8,128)S(1)}, f32[512,256]{1,0:T(8,128)}, u32[]{:S(2)}) copy-start(f32[512,256]{1,0:T(8,128)} %constant.38.clone.rest_16_.rest_8_) | copy-start | bytes 1572868
  8.3 41.2 %copy-start.1 = (bf16[512,512]{1,0:T(8,128)(2,1)S(1)}, bf16[512,512]{1,0:T(8,128)(2,1)}, u32[]{:S(2)}) copy-start(bf16[512,512]{1,0:T(8,128)(2,1)} %constant.33.clone.rest_11_.rest_3_) | copy-start | bytes 1572868
  12.6 1.0 %copy-start.6 = (bf16[2,64,2048]{2,1,0:T(8,128)(2,1)S(1)}, bf16[2,64,2048]{2,1,0:T(8,128)(2,1)}, u32[]{:S(2)}) copy-start(bf16[2,64,2048]{2,1,0:T(8,128)(2,1)} %first.1) | copy-start | bytes 1572868
  13.6 1.0 %copy-start.7 = (bf16[2,64,2048]{2,1,0:T(8,128)(2,1)S(1)}, bf16[2,64,2048]{2,1,0:T(8,128)(2,1)}, u32[]{:S(2)}) copy-start(bf16[2,64,2048]{2,1,0:T(8,128)(2,1)} %second.1) | copy-start | bytes 1572868
  23.4 6.1 %collective-permute-start.2 = (f32[136,256]{1,0:T(8,128)S(1)}, f32[136,256]{1,0:T(8,128)S(1)}, u32[]{:S(2)}, u32[]{:S(2)}) collective-permute-start(f32[136,256]{1,0:T(8,128)S(1)} %get-tuple-element.23), channel_id=1, source_target_pairs={{0,1},{1,0},{2,3},{3,2},{4,5},{5,4},{6,7},{7,6},{8,9},{9,8},{10,11... | collective-permute-start | bytes 417800 | tf_op jit(solution)/shard_map/ppermute | solution.py:580
  23.6 9.1 %collective-permute-start.3 = (f32[136,256]{1,0:T(8,128)S(1)}, f32[136,256]{1,0:T(8,128)S(1)}, u32[]{:S(2)}, u32[]{:S(2)}) collective-permute-start(f32[136,256]{1,0:T(8,128)S(1)} %get-tuple-element.24), channel_id=1, source_target_pairs={{0,2},{1,3},{2,0},{3,1},{4,6},{5,7},{6,4},{7,5},{8,10},{9,11},{10,... | collective-permute-start | bytes 417800 | tf_op jit(solution)/shard_map/ppermute | solution.py:580
  25.2 12.1 %collective-permute-start.4 = (f32[136,256]{1,0:T(8,128)S(1)}, f32[136,256]{1,0:T(8,128)S(1)}, u32[]{:S(2)}, u32[]{:S(2)}) collective-permute-start(f32[136,256]{1,0:T(8,128)S(1)} %get-tuple-element.25), channel_id=1, source_target_pairs={{0,3},{1,2},{2,1},{3,0},{4,7},{5,6},{6,5},{7,4},{8,11},{9,10},{10,... | collective-permute-start | bytes 417800 | tf_op jit(solution)/shard_map/ppermute | solution.py:580
  26.9 10.4 %collective-permute-start.5 = (f32[136,256]{1,0:T(8,128)S(1)}, f32[136,256]{1,0:T(8,128)S(1)}, u32[]{:S(2)}, u32[]{:S(2)}) collective-permute-start(f32[136,256]{1,0:T(8,128)S(1)} %get-tuple-element.26), channel_id=1, source_target_pairs={{0,4},{1,5},{2,6},{3,7},{4,0},{5,1},{6,2},{7,3},{8,12},{9,13},{10,... | collective-permute-start | bytes 417800 | tf_op jit(solution)/shard_map/ppermute | solution.py:580
  29.1 20.3 %collective-permute-start.6 = (f32[136,256]{1,0:T(8,128)S(1)}, f32[136,256]{1,0:T(8,128)S(1)}, u32[]{:S(2)}, u32[]{:S(2)}) collective-permute-start(f32[136,256]{1,0:T(8,128)S(1)} %get-tuple-element.27), channel_id=1, source_target_pairs={{0,5},{1,4},{2,7},{3,6},{4,1},{5,0},{6,3},{7,2},{8,13},{9,12},{10,... | collective-permute-start | bytes 417800 | tf_op jit(solution)/shard_map/ppermute | solution.py:580
  29.5 19.9 %collective-permute-start.7 = (f32[136,256]{1,0:T(8,128)S(1)}, f32[136,256]{1,0:T(8,128)S(1)}, u32[]{:S(2)}, u32[]{:S(2)}) collective-permute-start(f32[136,256]{1,0:T(8,128)S(1)} %get-tuple-element.28), channel_id=1, source_target_pairs={{0,6},{1,7},{2,4},{3,5},{4,2},{5,3},{6,0},{7,1},{8,14},{9,15},{10,... | collective-permute-start | bytes 417800 | tf_op jit(solution)/shard_map/ppermute | solution.py:580
  32.7 16.7 %collective-permute-start.8 = (f32[136,256]{1,0:T(8,128)S(1)}, f32[136,256]{1,0:T(8,128)S(1)}, u32[]{:S(2)}, u32[]{:S(2)}) collective-permute-start(f32[136,256]{1,0:T(8,128)S(1)} %get-tuple-element.29), channel_id=1, source_target_pairs={{0,7},{1,6},{2,5},{3,4},{4,3},{5,2},{6,1},{7,0},{8,15},{9,14},{10,... | collective-permute-start | bytes 417800 | tf_op jit(solution)/shard_map/ppermute | solution.py:580
  49.5 1.0 %copy-start.4 = (bf16[512,512]{1,0:T(8,128)(2,1)S(1)}, bf16[512,512]{1,0:T(8,128)(2,1)}, u32[]{:S(2)}) copy-start(bf16[512,512]{1,0:T(8,128)(2,1)} %constant.30.clone.rest_8_.rest_0_) | copy-start | bytes 1572868
  50.5 0.9 %copy-start.10 = (bf16[256,256]{1,0:T(8,128)(2,1)S(1)}, bf16[256,256]{1,0:T(8,128)(2,1)}, u32[]{:S(2)}) copy-start(bf16[256,256]{1,0:T(8,128)(2,1)} %constant.35.clone.rest_13_.rest_5_) | copy-start | bytes 393220
  52.3 12.8 %copy-start.5 = (bf16[512,512]{1,0:T(8,128)(2,1)S(1)}, bf16[512,512]{1,0:T(8,128)(2,1)}, u32[]{:S(2)}) copy-start(bf16[512,512]{1,0:T(8,128)(2,1)} %constant.30.clone.rest_8_.rest_0_) | copy-start | bytes 1572868
  56.7 7.8 %collective-permute-start.11 = (f32[8,128]{1,0:T(8,128)S(1)}, f32[8,128]{1,0:T(8,128)S(1)}, u32[]{:S(2)}, u32[]{:S(2)}) collective-permute-start(f32[8,128]{1,0:T(8,128)S(1)} %get-tuple-element.36), channel_id=1, source_target_pairs={{0,1},{1,2},{2,3},{3,4},{4,5},{5,6},{6,7},{7,0},{8,9},{9,10},{10,1... | collective-permute-start | bytes 12296 | tf_op jit(solution)/shard_map/ppermute | solution.py:543
  57.3 7.8 %collective-permute-start.12 = (f32[8,128]{1,0:T(8,128)S(1)}, f32[8,128]{1,0:T(8,128)S(1)}, u32[]{:S(2)}, u32[]{:S(2)}) collective-permute-start(f32[8,128]{1,0:T(8,128)S(1)} %get-tuple-element.37), channel_id=1, source_target_pairs={{0,7},{1,0},{2,1},{3,2},{4,3},{5,4},{6,5},{7,6},{8,15},{9,8},{10,9... | collective-permute-start | bytes 12296 | tf_op jit(solution)/shard_map/ppermute | solution.py:543
  61.5 1.3 %collective-permute-start.10 = (f32[1,256]{1,0:T(1,128)S(1)}, f32[1,256]{1,0:T(1,128)S(1)}, u32[]{:S(2)}, u32[]{:S(2)}) collective-permute-start(f32[1,256]{1,0:T(1,128)S(1)} %get-tuple-element.46), channel_id=1, source_target_pairs={{0,24},{8,0},{16,8},{24,16},{1,25},{9,1},{17,9},{25,17},{2,26},{10... | collective-permute-start | bytes 3080 | tf_op jit(solution)/shard_map/ppermute | solution.py:543
  61.5 3.0 %collective-permute-start.9 = (f32[1,256]{1,0:T(1,128)S(1)}, f32[1,256]{1,0:T(1,128)S(1)}, u32[]{:S(2)}, u32[]{:S(2)}) collective-permute-start(f32[1,256]{1,0:T(1,128)S(1)} %get-tuple-element.47), channel_id=1, source_target_pairs={{0,8},{8,16},{16,24},{24,0},{1,9},{9,17},{17,25},{25,1},{2,10},{10... | collective-permute-start | bytes 3080 | tf_op jit(solution)/shard_map/ppermute | solution.py:543
  (1 other events, 0.9 us)
where the time goes:
time: 87.8 us; the launch traced here: 87.4 us
  starting transfers between devices  24.3 us (28%)
  waiting for transfers between devices  21 us (24%)
  Pallas kernels  18.8 us (21%)
  blocking collectives  16.5 us (19%)
  local copies, waits for them, and re-layouts  6 us (7%)
    pallas_call x4, Pallas kernels, call(): pl.pallas_call(body, out_shape=[jax.ShapeDtypeStruct(s, d) for s, d in ou...  18.8 us
    all_to_all x1, blocking collectives, shards(): gathered = lax.all_to_all(spread, axes, 0, 0, tiled=True)  16.5 us
    ppermute x7, waiting for transfers between devices, shards(): lax.ppermute(sent[s], 'col', [(i, i ^ s) for i in range(columns)])  13.6 us
    ppermute x7, starting transfers between devices, shards(): lax.ppermute(sent[s], 'col', [(i, i ^ s) for i in range(columns)])  12.5 us
    ppermute x6, starting transfers between devices, around(): lax.ppermute(value, axis, [(i, (i + steps) % count) for i in range(count)])  11.8 us
    ppermute x6, waiting for transfers between devices, around(): lax.ppermute(value, axis, [(i, (i + steps) % count) for i in range(count)])  7.4 us
    unnamed x24, local copies, waits for them, and re-layouts  4.96 us
  transfers between devices with their start and end apart: 13, of which 7 were waited for; matrix products, arithmetic and copies ran while one was open for 0% of the time, Pallas kernels for 0%

commit v1 on v0

--- a/solution.py
+++ b/solution.py
@@ -15,7 +15,9 @@
 RADIUS = 4
 LANES = 128
 HALO = 8
+EDGE = 16
 TURN = 2.0 * math.pi
+CODE_SPAN = 248.0
 VMEM_LIMIT = 40 * 1024 * 1024
 
 ATAN = (
@@ -87,9 +89,17 @@
 def edge(phase_p, gain_p, phase_q, gain_q):
     delta = phase_q - phase_p
     delta = delta - jnp.round(delta)
-    half = poly(COS, delta * delta)
-    weight = gain_p * gain_q * (half * half)
+    half = gain_p * gain_q * poly(COS, delta * delta)
+    weight = half * half
     return weight, weight * delta
+
+
+def encode_gain(value):
+    return jnp.exp2(value * CODE_SPAN - 0.5 * CODE_SPAN).astype(jnp.bfloat16)
+
+
+def decode_gain(code):
+    return (jnp.log2(code.astype(jnp.float32)) + 0.5 * CODE_SPAN) * (1.0 / CODE_SPAN)
 
 
 def split(value):
@@ -122,6 +132,216 @@
     )(*args)
 
 
+def interior(body, outs, args, scratch):
+    return pl.pallas_call(
+        body,
+        out_shape=[jax.ShapeDtypeStruct(s, d) for s, d in outs],
+        in_specs=[pl.BlockSpec(memory_space=pl.ANY)] * 2,
+        out_specs=[pl.BlockSpec(memory_space=pltpu.VMEM)] * len(outs),
+        scratch_shapes=scratch,
+        compiler_params=pltpu.CompilerParams(vmem_limit_bytes=VMEM_LIMIT),
+        cost_estimate=pl.CostEstimate(flops=8000000, bytes_accessed=4000000, transcendentals=0),
+        name="interior",
+    )(*args)
+
+
+def phase_gain(smoothed):
+    re, im, one, two = smoothed
+    gain = jnp.sqrt(re * re + im * im) / (jnp.sqrt(one * two) + EPS)
+    return angle_turns(im, re), jnp.sqrt(gain)
+
+
+def products(ar, ai, br, bi, scale=None):
+    ar, ai, br, bi = (v.astype(jnp.float32) for v in (ar, ai, br, bi))
+    if scale is not None:
+        ar, ai, br, bi = (v * scale for v in (ar, ai, br, bi))
+    return (ar * br + ai * bi, ai * br - ar * bi, ar * ar + ai * ai, br * br + bi * bi)
+
+
+def along_range(x):
+    k = taps()
+    n = x.shape[1]
+    total = k[0] * x
+    for j in range(1, RADIUS + 1):
+        total = total + k[j] * (pltpu.roll(x, j, 1) + pltpu.roll(x, n - j, 1))
+    return total
+
+
+def along_azimuth(ref, f, row, rows, cs):
+    k = taps()
+    total = k[0] * ref[f, row : row + rows, cs]
+    for j in range(1, RADIUS + 1):
+        total = total + k[j] * (ref[f, row - j : row - j + rows, cs] + ref[f, row + j : row + j + rows, cs])
+    return total
+
+
+def end_weights(before):
+    k = taps()
+    sub = lax.broadcasted_iota(jnp.int32, (HALO, 1), 0)
+    low = jnp.zeros((HALO, 1), jnp.float32)
+    high = jnp.zeros((HALO, 1), jnp.float32)
+    for j in range(RADIUS + 1):
+        low = jnp.where(sub == (HALO - 1 - j if before else HALO - j), k[j], low)
+        high = jnp.where(sub == (j - 1 if before else j), k[j], high)
+    return low, high
+
+
+def interior_kernel(lines, width, tile, columns, first, second, ranged, codes, rims, raw, prod, field, sems):
+    chunk = 16
+    copies = []
+    for i in range(lines // chunk):
+        rs = pl.ds(i * chunk, chunk)
+        for a, ref in enumerate((first, second)):
+            copy = pltpu.make_async_copy(ref.at[:, rs, :], raw.at[a, :, rs, :], sems.at[2 * i + a])
+            copy.start()
+            copies.append(copy)
+    zero = jnp.zeros((lines, LANES), jnp.float32)
+    for f in range(4):
+        prod[f, :, 0:LANES] = zero[:chunk]
+        prod[f, :, LANES + width :] = zero[:chunk]
+        ranged[f, :, 0:LANES] = zero
+        ranged[f, :, LANES + width :] = zero
+    wide = min(width, 1024)
+    for i in range(lines // chunk):
+        copies[2 * i].wait()
+        copies[2 * i + 1].wait()
+        rs = slice(i * chunk, (i + 1) * chunk)
+        for c in range(0, width, 512):
+            cs = slice(c, c + 512)
+            values = products(raw[0, 0, rs, cs], raw[0, 1, rs, cs], raw[1, 0, rs, cs], raw[1, 1, rs, cs])
+            for f in range(4):
+                prod[f, :, LANES + c : LANES + c + 512] = values[f]
+        for f in range(4):
+            for r in range(0, chunk, 8):
+                for c in range(0, width, wide):
+                    total = along_range(prod[f, r : r + 8, c : c + wide + 2 * LANES])
+                    row = i * chunk + r
+                    ranged[f, row : row + 8, LANES + c : LANES + c + wide] = total[:, LANES : LANES + wide]
+    inner = lines - 2 * EDGE
+    for f in range(2):
+        field[f, :, 0:LANES] = zero[:inner]
+        field[f, :, LANES + width :] = zero[:inner]
+    for c in range(0, width, LANES):
+        cs = slice(LANES + c, 2 * LANES + c)
+        out = slice(c, c + LANES)
+        for r in range(0, inner, 16):
+            smoothed = [along_azimuth(ranged, f, EDGE + r, 16, cs) for f in range(4)]
+            phase, gain = phase_gain(smoothed)
+            field[0, r : r + 16, cs] = phase
+            field[1, r : r + 16, cs] = gain
+            codes[0, r : r + 16, out], codes[1, r : r + 16, out] = split(phase)
+            codes[2, r : r + 16, out] = encode_gain(gain)
+    groups = lines // 8
+    for t in range(columns):
+        rims[t] = rim_block(field, groups, range(EDGE // 8, (lines - EDGE) // 8), EDGE // 8, t * tile, tile, None)
+
+
+def rim_block(field, groups, which, first_group, start, tile, block, hint=None):
+    lane = lanes_of((8, LANES))
+    if block is None:
+        block = jnp.zeros((8, LANES), jnp.float32)
+    for f in range(2):
+        for side in range(2):
+            offset = start if side == 0 else start + LANES + tile
+            at = slice(offset, offset + LANES) if hint is None else pl.ds(hint(offset, LANES), LANES)
+            for g in which:
+                target = (f * 2 + side) * groups + g
+                row = 8 * (g - first_group)
+                x = field[f, row : row + 8, at]
+                shift = (target - (LANES - 1 if side == 0 else 0)) % LANES
+                if shift:
+                    x = pltpu.roll(x, shift, 1)
+                block = jnp.where(lane == target, x, block)
+    return block
+
+
+def border_kernel(lines, width, tile, columns, across, ids, ranged, codes, rims, from_pair, from_next, *rest):
+    half = columns // 2
+    outs, (prod, seg, field, ends) = rest[:half], rest[half:]
+    own = ids[1]
+    odd = ids[4]
+    first_tile = (own & half) ^ (half if across else 0)
+    span = half * tile + 2 * LANES
+    start = pl.multiple_of(first_tile * tile, LANES)
+    inside = (
+        jnp.where(ids[2] == 0, 0.0, 1.0).astype(jnp.float32),
+        jnp.where(ids[2] == ids[3] - 1, 0.0, 1.0).astype(jnp.float32),
+    )
+    zero = jnp.zeros((HALO, 2 * LANES), jnp.float32)
+    own_rows = EDGE + HALO
+    pixel = lanes_of((HALO, span)) + (start - LANES)
+    in_image = jnp.logical_and(pixel >= 0, pixel < width)
+    for e in range(2):
+        flag = odd if e == 0 else 1 - odd
+        keep = flag.astype(jnp.float32)
+        for f in range(4):
+            prod[f, :, 0 : 2 * LANES] = zero
+            prod[f, :, 2 * LANES + width :] = zero
+        for c in range(0, width, 512):
+            cs = slice(c, c + 512)
+            parts = [
+                from_pair[i, :, cs].astype(jnp.float32) * keep + from_next[i, :, cs].astype(jnp.float32) * (1.0 - keep)
+                for i in range(4)
+            ]
+            values = products(*parts, inside[e])
+            for f in range(4):
+                prod[f, :, 2 * LANES + c : 2 * LANES + c + 512] = values[f]
+        for f in range(4):
+            total = along_range(prod[f, :, pl.ds(start, span + 2 * LANES)])[:, LANES : LANES + span]
+            total = jnp.where(in_image, total, 0.0)
+            if e == 0:
+                seg[e, f, 0:HALO, :] = total
+                seg[e, f, HALO:, :] = ranged[f, 0:own_rows, pl.ds(start, span)]
+            else:
+                seg[e, f, own_rows:, :] = total
+                seg[e, f, 0:own_rows, :] = ranged[f, lines - own_rows :, pl.ds(start, span)]
+    for e in range(2):
+        ref = seg.at[e]
+        for c in range(0, span, LANES):
+            cs = slice(c, c + LANES)
+            smoothed = [along_azimuth(ref, f, HALO, EDGE, cs) for f in range(4)]
+            phase, gain = phase_gain(smoothed)
+            field[0, e * EDGE : (e + 1) * EDGE, cs] = phase
+            field[1, e * EDGE : (e + 1) * EDGE, cs] = gain
+        low, high = end_weights(e == 0)
+        r = 0 if e == 0 else own_rows - HALO
+        smoothed = [
+            jnp.sum(low * ref[f, r : r + HALO, :] + high * ref[f, r + HALO : r + 2 * HALO, :], axis=0, keepdims=True)
+            for f in range(4)
+        ]
+        phase, gain = phase_gain(smoothed)
+        ends[e : e + 1, :] = phase
+        ends[2 + e : 3 + e, :] = gain * inside[e]
+    groups = lines // 8
+    edge_groups = EDGE // 8
+    inner = lines - 2 * EDGE
+    for n, s in enumerate(range(half, columns) if across else range(half)):
+        out = outs[n]
+        target = own ^ s
+        local = pl.multiple_of((target - first_tile) * tile, LANES)
+        cs = pl.ds(pl.multiple_of(local + LANES, LANES), tile)
+        wide = pl.ds(pl.multiple_of(target * tile, LANES), tile)
+        for i in range(3):
+            out[i * lines + EDGE : i * lines + EDGE + inner, :] = codes[i, :, wide]
+        for e in range(2):
+            row = 0 if e == 0 else lines - EDGE
+            rs = slice(e * EDGE, (e + 1) * EDGE)
+            out[row : row + EDGE, :], out[lines + row : lines + row + EDGE, :] = split(field[0, rs, cs])
+            out[2 * lines + row : 2 * lines + row + EDGE, :] = encode_gain(field[1, rs, cs])
+        block = rims[target]
+        block = rim_block(field, groups, range(edge_groups), 0, local, tile, block, pl.multiple_of)
+        block = rim_block(
+            field, groups, range(groups - edge_groups, groups), groups - 2 * edge_groups, local, tile, block,
+            pl.multiple_of,
+        )
+        rows = []
+        for i in range(4):
+            for h in range(tile // LANES):
+                rows.append(ends[i : i + 1, pl.ds(pl.multiple_of(local + (h + 1) * LANES, LANES), LANES)])
+        block = jnp.concatenate([block, jnp.concatenate(rows, axis=0)], axis=1)
+        out[3 * lines :, :] = jnp.concatenate(split(block), axis=0)
+
+
 def strip_kernel(lines, width, tile, columns, exchange, ids, first, second, above, below, *rest):
     n_out = len(rest) - 3
     outs, (prod, ranged, field) = rest[:n_out], rest[n_out:]
@@ -130,12 +350,6 @@
     inside_above = jnp.where(ids[2] == 0, 0.0, 1.0).astype(jnp.float32)
     inside_below = jnp.where(ids[2] == ids[3] - 1, 0.0, 1.0).astype(jnp.float32)
     height = lines + 2 * HALO
-
-    def products(ar, ai, br, bi, scale=None):
-        ar, ai, br, bi = (v.astype(jnp.float32) for v in (ar, ai, br, bi))
-        if scale is not None:
-            ar, ai, br, bi = (v * scale for v in (ar, ai, br, bi))
-        return (ar * br + ai * bi, ai * br - ar * bi, ar * ar + ai * ai, br * br + bi * bi)
 
     zero = jnp.zeros((height, LANES), jnp.float32)
     for f in range(4):
@@ -166,11 +380,6 @@
                 for j in range(1, RADIUS + 1):
                     total = total + k[j] * (pltpu.roll(x, j, 1) + pltpu.roll(x, n - j, 1))
                 ranged[f, r : r + 8, c : c + step] = total[:, LANES : LANES + step]
-
-    def phase_gain(smoothed):
-        re, im, one, two = smoothed
-        gain = jnp.sqrt(re * re + im * im) / (jnp.sqrt(one * two) + EPS)
-        return angle_turns(im, re), gain
 
     for f in range(2):
         field[f, :, 0:LANES] = zero[:lines]
@@ -276,6 +485,15 @@
     return dot3(split(back), rg)
 
 
+def table_pairs(tables):
+    pairs = []
+    for ref in tables:
+        n = ref.shape[1]
+        parts = [ref[i * n : (i + 1) * n, :] for i in range(4)]
+        pairs += [(parts[0], parts[1]), (parts[2], parts[3])]
+    return pairs
+
+
 def line_groups(ref, tile_az, edge_lane):
     lane = lanes_of((8, LANES))
     first = (edge_lane // LANES) * LANES
@@ -320,11 +538,11 @@
 def tile_kernel(lines, tile_az, tile, columns, exchange, ids, *rest):
     chunks = rest[: columns if exchange == "permute" else 1]
     rest = rest[len(chunks) :]
-    tables, inverse = rest[:8], rest[8]
-    residual, shaped, weight_x, rim_x, weight_y, rows_out, left_out, right_out = rest[9:17]
-    phase, gain, sides, ends, flux_x, flux_rim, flux_y = rest[17:]
+    tables, inverse = rest[:2], rest[2]
+    residual, shaped, weight_x, rim_x, weight_y, row_pair, row_next, col_pair, col_next = rest[3:12]
+    phase, gain, sides, ends, flux_x, flux_rim, flux_y = rest[12:]
     own = ids[1]
-    pairs = [(tables[2 * i][...], tables[2 * i + 1][...]) for i in range(4)]
+    pairs = table_pairs(tables)
 
     for s in range(columns):
         if exchange == "permute":
@@ -334,12 +552,20 @@
         row = strip * lines
         if exchange == "permute":
             row = pl.multiple_of(row, 8)
-        phase[pl.ds(HALO + row, lines), :] = src[0:lines, :]
-        gain[pl.ds(HALO + row, lines), :] = src[lines : 2 * lines, :]
-        base = 2 * lines
         at = pl.ds(pl.multiple_of(strip * 8, 8), 8) if exchange == "permute" else pl.ds(strip * 8, 8)
-        sides[at, :] = src[base : base + 8, 0:LANES]
-        ends[at, :] = src[base : base + 8, LANES : 2 * LANES]
+        if exchange == "permute":
+            phase[pl.ds(HALO + row, lines), :] = src[0:lines, :].astype(jnp.float32) + src[
+                lines : 2 * lines, :
+            ].astype(jnp.float32)
+            gain[pl.ds(HALO + row, lines), :] = decode_gain(src[2 * lines : 3 * lines, :])
+            both = src[3 * lines :, :].astype(jnp.float32)
+            block = both[0:8, :] + both[8:16, :]
+        else:
+            phase[pl.ds(HALO + row, lines), :] = src[0:lines, :]
+            gain[pl.ds(HALO + row, lines), :] = src[lines : 2 * lines, :]
+            block = src[2 * lines : 2 * lines + 8, :]
+        sides[at, :] = block[:, 0:LANES]
+        ends[at, :] = block[:, LANES : 2 * LANES]
     last = 8 * (columns - 1)
     for h in range(tile // LANES):
         cs = slice(h * LANES, (h + 1) * LANES)
@@ -384,10 +610,15 @@
     for r in range(0, tile_az, step):
         residual[r : r + step, :] = TURN * divergence(tile_az, step, flux_x, flux_rim, flux_y, r)
     shaped[...] = precondition(residual[...], pairs, inverse)
-    rows_out[0, 0:1, :] = shaped[0:1, :]
-    rows_out[1, 0:1, :] = shaped[tile_az - 1 : tile_az, :]
-    left_out[...] = line_groups(shaped, tile_az, 0)
-    right_out[...] = line_groups(shaped, tile_az, tile - 1)
+    row_odd, col_odd = ids[5] == 1, ids[4] == 1
+    top = jnp.concatenate([shaped[0:1, h : h + LANES] for h in range(0, tile, LANES)], axis=0)
+    bottom = jnp.concatenate([shaped[tile_az - 1 : tile_az, h : h + LANES] for h in range(0, tile, LANES)], axis=0)
+    row_pair[0:2, :] = jnp.where(row_odd, top, bottom)
+    row_next[0:2, :] = jnp.where(row_odd, bottom, top)
+    left = line_groups(shaped, tile_az, 0)
+    right = line_groups(shaped, tile_az, tile - 1)
+    col_pair[...] = jnp.where(col_odd, left, right)
+    col_next[...] = jnp.where(col_odd, right, left)
 
 
 def apply_operator(tile_az, tile, u, weight_x, rim_x, weight_y, flux_x, flux_rim, flux_y, left, right, out):
@@ -420,17 +651,24 @@
 
 
 def second_kernel(
-    tile_az, tile, residual, shaped, weight_x, rim_x, weight_y, up, down, left, right, *rest
+    tile_az, tile, ids, residual, shaped, weight_x, rim_x, weight_y, row_pair, row_next, col_pair, col_next, *rest
 ):
-    tables, inverse = rest[:8], rest[8]
-    operated, shaped2, operated2, chunk = rest[9:13]
-    u, flux_x, flux_rim, flux_y = rest[13:]
-    pairs = [(tables[2 * i][...], tables[2 * i + 1][...]) for i in range(4)]
+    tables, inverse = rest[:2], rest[2]
+    operated, shaped2, operated2, chunk = rest[3:7]
+    u, flux_x, flux_rim, flux_y = rest[7:]
+    pairs = table_pairs(tables)
+    row_odd, col_odd = ids[5] == 1, ids[4] == 1
+    up = jnp.where(row_odd, row_pair[0:2, :], row_next[0:2, :])
+    down = jnp.where(row_odd, row_next[0:2, :], row_pair[0:2, :])
+    left = jnp.where(col_odd, col_pair[...], col_next[...])
+    right = jnp.where(col_odd, col_next[...], col_pair[...])
     u[HALO : HALO + tile_az, :] = shaped[...]
-    u[HALO - 1 : HALO, :] = up[0:1, :]
-    u[HALO + tile_az : HALO + tile_az + 1, :] = down[0:1, :]
+    for h in range(tile // LANES):
+        cs = slice(h * LANES, (h + 1) * LANES)
+        u[HALO - 1 : HALO, cs] = up[h : h + 1, :]
+        u[HALO + tile_az : HALO + tile_az + 1, cs] = down[h : h + 1, :]
     apply_operator(
-        tile_az, tile, u, weight_x, rim_x, weight_y, flux_x, flux_rim, flux_y, left[...], right[...], operated
+        tile_az, tile, u, weight_x, rim_x, weight_y, flux_x, flux_rim, flux_y, left, right, operated
     )
     image = precondition(operated[...], pairs, inverse)
     shaped2[...] = image
@@ -538,9 +776,12 @@
         residual_out[rs, :] = residual[rs, :] - on_first * operated[rs, :] + on_second * q
 
 
-def around(value, axis, steps):
-    count = lax.axis_size(axis)
-    return lax.ppermute(value, axis, [(i, (i + steps) % count) for i in range(count)])
+def swapped(value, axis, count, step):
+    if step == 0:
+        pairs = [(i, i ^ 1) for i in range(count)]
+    else:
+        pairs = [(i, (i + 1 if i % 2 else i - 1) % count) for i in range(count)]
+    return lax.ppermute(value, axis, pairs)
 
 
 def shards(rows, columns, first_slc, second_slc):
@@ -548,71 +789,96 @@
     tile = width // columns
     tile_az = lines * columns
     axes = ("row", "col")
-    exchange = "permute" if columns <= 8 else "all_to_all"
+    exchange = "permute" if lines >= 4 * EDGE and columns <= 8 else "all_to_all"
     row, col = lax.axis_index("row"), lax.axis_index("col")
-    ids = jnp.stack([row, col, row * columns + col, jnp.int32(rows * columns)]).astype(jnp.int32)
-    f32 = jnp.float32
-    height = lines + 2 * HALO
-
-    above = around(jnp.concatenate([first_slc[:, -HALO:], second_slc[:, -HALO:]], 0), axes, 1)
-    below = around(jnp.concatenate([first_slc[:, :HALO], second_slc[:, :HALO]], 0), axes, -1)
-    depth = 2 * lines + 8
+    ids = jnp.stack([row, col, row * columns + col, jnp.int32(rows * columns), col % 2, row % 2]).astype(jnp.int32)
+    f32, bf16 = jnp.float32, jnp.bfloat16
+
+    head = jnp.concatenate([first_slc[:, :HALO], second_slc[:, :HALO]], 0)
+    tail = jnp.concatenate([first_slc[:, -HALO:], second_slc[:, -HALO:]], 0)
+    odd = col % 2 == 1
+    from_pair = swapped(jnp.where(odd, head, tail), axes, rows * columns, 0)
+    from_next = swapped(jnp.where(odd, tail, head), axes, rows * columns, 1)
+    wide = width + 2 * LANES
     if exchange == "permute":
-        outs = [((depth, tile), f32)] * columns
+        ranged, codes, rims = interior(
+            functools.partial(interior_kernel, lines, width, tile, columns),
+            [((4, lines, wide), f32), ((3, lines - 2 * EDGE, width), bf16), ((columns, 8, LANES), f32)],
+            (first_slc, second_slc),
+            [
+                pltpu.VMEM((2, 2, lines, width), bf16),
+                pltpu.VMEM((4, 16, wide), f32),
+                pltpu.VMEM((2, lines - 2 * EDGE, wide), f32),
+                pltpu.SemaphoreType.DMA((lines // 8,)),
+            ],
+        )
+        half = columns // 2
+        span = half * tile + 2 * LANES
+        sent = [None] * columns
+        for across in (True, False):
+            part = call(
+                functools.partial(border_kernel, lines, width, tile, columns, across),
+                [((3 * lines + 16, tile), bf16)] * half,
+                (ids, ranged, codes, rims, from_pair, from_next),
+                [
+                    pltpu.VMEM((4, HALO, width + 4 * LANES), f32),
+                    pltpu.VMEM((2, 4, EDGE + 2 * HALO, span), f32),
+                    pltpu.VMEM((2, 2 * EDGE, span), f32),
+                    pltpu.VMEM((8, span), f32),
+                ],
+                "borders",
+            )
+            for i, value in enumerate(part):
+                sent[i + (half if across else 0)] = value
+        arrived = [sent[0]] + [
+            lax.ppermute(sent[s], "col", [(i, i ^ s) for i in range(columns)]) for s in range(1, columns)
+        ]
     else:
-        outs = [((columns, depth, tile), f32)]
-    sent = call(
-        functools.partial(strip_kernel, lines, width, tile, columns, exchange),
-        outs,
-        (ids, first_slc, second_slc, above, below),
-        [
-            pltpu.VMEM((4, height, width + 2 * LANES), f32),
-            pltpu.VMEM((4, height, width), f32),
-            pltpu.VMEM((2, lines, width + 2 * LANES), f32),
-        ],
-        "strips",
-    )
-    if exchange == "permute":
-        order = [4, 5, 6, 7, 2, 3, 1]
-        arrived = [sent[0]] + [None] * (columns - 1)
-        for s in order:
-            if s < columns:
-                arrived[s] = lax.ppermute(sent[s], "col", [(i, i ^ s) for i in range(columns)])
-    else:
+        above = jnp.where(odd, from_pair, from_next)
+        below = jnp.where(odd, from_next, from_pair)
+        height = lines + 2 * HALO
+        sent = call(
+            functools.partial(strip_kernel, lines, width, tile, columns, exchange),
+            [((columns, 2 * lines + 8, tile), f32)],
+            (ids, first_slc, second_slc, above, below),
+            [pltpu.VMEM((4, height, wide), f32), pltpu.VMEM((4, height, width), f32), pltpu.VMEM((2, lines, wide), f32)],
+            "strips",
+        )
         arrived = [lax.all_to_all(sent[0], "col", 0, 0, tiled=True)]
 
-    az, rg = cosine_table(tile_az), cosine_table(tile)
     tables = []
-    for table in (az, az.T, rg, rg.T):
-        tables.extend(jnp.asarray(part) for part in two_parts(table))
+    for table in (cosine_table(tile_az), cosine_table(tile)):
+        parts = [*two_parts(table), *two_parts(table.T)]
+        tables.append(jnp.asarray(np.concatenate(parts, axis=0)))
     inverse = jnp.asarray(inverse_eigen(tile_az, tile))
 
     whole = ((tile_az, tile), f32)
-    column = ((8, LANES), f32)
+    block = ((8, LANES), f32)
     padded = pltpu.VMEM((tile_az + 2 * HALO, tile), f32)
     fluxes = [
         pltpu.VMEM((tile_az, tile), f32),
         pltpu.VMEM((tile_az, LANES), f32),
         pltpu.VMEM((tile_az + 8, tile), f32),
     ]
-    residual, shaped, weight_x, rim_x, weight_y, ends, left_col, right_col = call(
+    residual, shaped, weight_x, rim_x, weight_y, row_pair, row_next, col_pair, col_next = call(
         functools.partial(tile_kernel, lines, tile_az, tile, columns, exchange),
-        [whole, whole, whole, ((tile_az, LANES), f32), ((tile_az + 8, tile), f32), ((2, 1, tile), f32), column, column],
+        [whole, whole, whole, ((tile_az, LANES), f32), ((tile_az + 8, tile), f32), block, block, block, block],
         (ids, *arrived, *tables, inverse),
         [padded, padded, pltpu.VMEM((8 * columns, LANES), f32), pltpu.VMEM((8 * columns, LANES), f32), *fluxes],
         "tiles",
     )
-    down = around(ends[0], "row", -1)
-    up = around(ends[1], "row", 1)
-    right = around(left_col, "col", -1)
-    left = around(right_col, "col", 1)
+    rims = (
+        swapped(row_pair, "row", rows, 0),
+        swapped(row_next, "row", rows, 1),
+        swapped(col_pair, "col", columns, 0),
+        swapped(col_next, "col", columns, 1),
+    )
     operated, shaped2, operated2, chunk = call(
         functools.partial(second_kernel, tile_az, tile),
         [whole, whole, whole, ((16, LANES), f32)],
-        (residual, shaped, weight_x, rim_x, weight_y, up, down, left, right, *tables, inverse),
+        (ids, residual, shaped, weight_x, rim_x, weight_y, *rims, *tables, inverse),
         [padded, *fluxes],
         "operator",
-        smem_first=False,
     )
     spread = jnp.broadcast_to(chunk[None], (rows * columns, 16, LANES))
     gathered = lax.all_to_all(spread, axes, 0, 0, tiled=True)

time: 87.8 us -> 76.8 us (0.87)
  waiting for transfers between devices: 21 us -> 12.9 us
  Pallas kernels: 18.8 us -> 23.5 us
  local copies, waits for them, and re-layouts: 6 us -> 3.17 us
  blocking collectives: 16.5 us -> 14.2 us
  starting transfers between devices: 24.3 us -> 22 us
    pallas_call x0 -> x1, Pallas kernels: none -> 7.21 us  [interior(): pl.pallas_call(body, out_shape=[jax.ShapeDtypeStruct(s, d) for s, d in ou...]
    ppermute x6, waiting for transfers between devices: 7.4 us -> 2.91 us  [swapped(): return lax.ppermute(value, axis, pairs)]
    ppermute x7, waiting for transfers between devices: 13.6 us -> 9.95 us  [shards(): lax.ppermute(sent[s], 'col', [(i, i ^ s) for i in range(columns)])]
    unnamed x24 -> x10, local copies, waits for them, and re-layouts: 4.96 us -> 2.11 us
    ppermute x7, starting transfers between devices: 12.5 us -> 9.81 us  [shards(): lax.ppermute(sent[s], 'col', [(i, i ^ s) for i in range(columns)])]
    pallas_call x4 -> x5, Pallas kernels: 18.8 us -> 16.3 us  [call(): pl.pallas_call(body, out_shape=[jax.ShapeDtypeStruct(s, d) for s, d in ou...]
    all_to_all x1, blocking collectives: 16.5 us -> 14.2 us  [shards(): gathered = lax.all_to_all(spread, axes, 0, 0, tiled=True)]
  transfers between devices with their start and end apart: 13 -> 13, of which waited for: 7 -> 5; matrix products, arithmetic and copies ran while one was open for 0% -> 0% of each run, Pallas kernels for 0% -> 13%
where the time goes in v1:
time: 76.8 us; the launch traced here: 76.6 us
  Pallas kernels  23.5 us (31%)
  starting transfers between devices  22 us (29%)
  blocking collectives  14.2 us (18%)
  waiting for transfers between devices  12.9 us (17%)
  local copies, waits for them, and re-layouts  3.17 us (4%)
    pallas_call x5, Pallas kernels, call(): pl.pallas_call(body, out_shape=[jax.ShapeDtypeStruct(s, d) for s, d in ou...  16.3 us
    all_to_all x1, blocking collectives, shards(): gathered = lax.all_to_all(spread, axes, 0, 0, tiled=True)  14.2 us
    ppermute x6, starting transfers between devices, swapped(): return lax.ppermute(value, axis, pairs)  12.2 us
    ppermute x7, waiting for transfers between devices, shards(): lax.ppermute(sent[s], 'col', [(i, i ^ s) for i in range(columns)])  9.95 us
    ppermute x7, starting transfers between devices, shards(): lax.ppermute(sent[s], 'col', [(i, i ^ s) for i in range(columns)])  9.81 us
    pallas_call x1, Pallas kernels, interior(): pl.pallas_call(body, out_shape=[jax.ShapeDtypeStruct(s, d) for s, d in ou...  7.21 us
    ppermute x6, waiting for transfers between devices, swapped(): return lax.ppermute(value, axis, pairs)  2.91 us
    unnamed x10, local copies, waits for them, and re-layouts  2.11 us
  transfers between devices with their start and end apart: 13, of which 5 were waited for; matrix products, arithmetic and copies ran while one was open for 0% of the time, Pallas kernels for 13%

profile of v1, /device:TPU:0, one launch (start us, length us, event | category | flops | bytes accessed | tf_op | source)
XLA Modules:
  0.0 76.6 jit_solution(5468216011123609066)
XLA Ops:
  0.6 1.0 %fusion = (bf16[2,8,2048]{2,1,0:T(8,128)(2,1)S(1)}, bf16[2,8,2048]{2,1,0:T(8,128)(2,1)S(1)}, bf16[2,8,2048]{2,1,0:T(8,128)(2,1)S(1)}, bf16[2,8,2048]{2,1,0:T(8,128)(2,1)S(1)}) fusion(bf16[2,64,2048]{2,1,0:T(8,128)(2,1)} %first.1, bf16[2,64,2048]{2,1,0:T(8,128)(2,1)} %second.1), kind=kLoop, calls=%fused_computation.4 | loop fusion | bytes 524288 | tf_op jit(solution)/shard_map/slice | solution.py:797
  1.6 6.4 %collective-permute-start.1 = (bf16[4,8,2048]{2,1,0:T(8,128)(2,1)S(1)}, bf16[4,8,2048]{2,1,0:T(8,128)(2,1)S(1)}, u32[]{:S(2)}, u32[]{:S(2)}) collective-permute-start(bf16[4,8,2048]{2,1,0:T(8,128)(2,1)S(1)} %get-tuple-element.54), channel_id=1, source_target_pairs={{0,31},{1,2},{2,1},{3,4},{4,3},{5,6},{6,5},{7,8},{8,7},{9,10},{10,... | collective-permute-start | bytes 393224 | tf_op jit(solution)/shard_map/ppermute | solution.py:784
  8.1 0.1 stack.23.ids
  8.2 1.0 %copy-done.3 = bf16[2,64,2048]{2,1,0:T(8,128)(2,1)S(1)} copy-done((bf16[2,64,2048]{2,1,0:T(8,128)(2,1)S(1)}, bf16[2,64,2048]{2,1,0:T(8,128)(2,1)}, u32[]{:S(2)}) %copy-start.3) | copy-done | bytes 524312
  9.2 1.0 %copy-done.4 = bf16[2,64,2048]{2,1,0:T(8,128)(2,1)S(1)} copy-done((bf16[2,64,2048]{2,1,0:T(8,128)(2,1)S(1)}, bf16[2,64,2048]{2,1,0:T(8,128)(2,1)}, u32[]{:S(2)}) %copy-start.4) | copy-done | bytes 524312
  10.3 7.2 %interior.1 = (f32[4,64,2304]{2,1,0:T(8,128)S(1)}, bf16[3,32,2048]{2,1,0:T(8,128)(2,1)S(1)}, f32[8,8,128]{2,1,0:T(8,128)S(1)}) custom-call(bf16[2,64,2048]{2,1,0:T(8,128)(2,1)S(1)} %copy-done.3, bf16[2,64,2048]{2,1,0:T(8,128)(2,1)S(1)} %copy-done.4), custom_call_target="tpu_custom_call" | custom-call | flops 8000000 | bytes 4000000 | tf_op jit(solution)/shard_map/interior/pallas_call | solution.py:136
  17.5 2.7 %borders.3 = (bf16[208,256]{1,0:T(8,128)(2,1)S(1)}, bf16[208,256]{1,0:T(8,128)(2,1)S(1)}, bf16[208,256]{1,0:T(8,128)(2,1)S(1)}, bf16[208,256]{1,0:T(8,128)(2,1)S(1)}) custom-call(s32[6]{0:T(128)S(1)} %stack.23.ids, f32[4,64,2304]{2,1,0:T(8,128)S(1)} %get-tuple-element.26.ranged, bf16[3,32,2048]{2,1,0:T(8,128)(2,1)S(1)} %get-tuple-element.27.codes, ...), custom_call_target="tpu_custom_call" | custom-call | flops 1000000 | bytes 4000000 | tf_op jit(solution)/shard_map/borders/pallas_call | solution.py:123
  20.2 0.8 %collective-permute-start.5 = (bf16[208,256]{1,0:T(8,128)(2,1)S(1)}, bf16[208,256]{1,0:T(8,128)(2,1)S(1)}, u32[]{:S(2)}, u32[]{:S(2)}) collective-permute-start(bf16[208,256]{1,0:T(8,128)(2,1)S(1)} %get-tuple-element.33), channel_id=1, source_target_pairs={{0,4},{1,5},{2,6},{3,7},{4,0},{5,1},{6,2},{7,3},{8,12},{9,13},{10,... | collective-permute-start | bytes 319496 | tf_op jit(solution)/shard_map/ppermute | solution.py:834
  21.0 3.7 %collective-permute-start.6 = (bf16[208,256]{1,0:T(8,128)(2,1)S(1)}, bf16[208,256]{1,0:T(8,128)(2,1)S(1)}, u32[]{:S(2)}, u32[]{:S(2)}) collective-permute-start(bf16[208,256]{1,0:T(8,128)(2,1)S(1)} %get-tuple-element.34), channel_id=1, source_target_pairs={{0,5},{1,4},{2,7},{3,6},{4,1},{5,0},{6,3},{7,2},{8,13},{9,12},{10,... | collective-permute-start | bytes 319496 | tf_op jit(solution)/shard_map/ppermute | solution.py:834
  24.7 3.2 %collective-permute-start.8 = (bf16[208,256]{1,0:T(8,128)(2,1)S(1)}, bf16[208,256]{1,0:T(8,128)(2,1)S(1)}, u32[]{:S(2)}, u32[]{:S(2)}) collective-permute-start(bf16[208,256]{1,0:T(8,128)(2,1)S(1)} %get-tuple-element.36), channel_id=1, source_target_pairs={{0,7},{1,6},{2,5},{3,4},{4,3},{5,2},{6,1},{7,0},{8,15},{9,14},{10,... | collective-permute-start | bytes 319496 | tf_op jit(solution)/shard_map/ppermute | solution.py:834
  27.9 2.7 %borders.2 = (bf16[208,256]{1,0:T(8,128)(2,1)S(1)}, bf16[208,256]{1,0:T(8,128)(2,1)S(1)}, bf16[208,256]{1,0:T(8,128)(2,1)S(1)}, bf16[208,256]{1,0:T(8,128)(2,1)S(1)}) custom-call(s32[6]{0:T(128)S(1)} %stack.23.ids, f32[4,64,2304]{2,1,0:T(8,128)S(1)} %get-tuple-element.26.ranged, bf16[3,32,2048]{2,1,0:T(8,128)(2,1)S(1)} %get-tuple-element.27.codes, ...), custom_call_target="tpu_custom_call" | custom-call | flops 1000000 | bytes 4000000 | tf_op jit(solution)/shard_map/borders/pallas_call | solution.py:123
  30.6 2.1 %collective-permute-start.2 = (bf16[208,256]{1,0:T(8,128)(2,1)S(1)}, bf16[208,256]{1,0:T(8,128)(2,1)S(1)}, u32[]{:S(2)}, u32[]{:S(2)}) collective-permute-start(bf16[208,256]{1,0:T(8,128)(2,1)S(1)} %get-tuple-element.30), channel_id=1, source_target_pairs={{0,1},{1,0},{2,3},{3,2},{4,5},{5,4},{6,7},{7,6},{8,9},{9,8},{10,11... | collective-permute-start | bytes 319496 | tf_op jit(solution)/shard_map/ppermute | solution.py:834
  32.7 1.5 %collective-permute-done.5.rest_4_ = bf16[208,256]{1,0:T(8,128)(2,1)S(1)} collective-permute-done((bf16[208,256]{1,0:T(8,128)(2,1)S(1)}, bf16[208,256]{1,0:T(8,128)(2,1)S(1)}, u32[]{:S(2)}, u32[]{:S(2)}) %collective-permute-start.5) | collective-permute-done | bytes 106528 | tf_op jit(solution)/shard_map/ppermute | solution.py:834
  34.3 2.8 %collective-permute-done.6.rest_5_ = bf16[208,256]{1,0:T(8,128)(2,1)S(1)} collective-permute-done((bf16[208,256]{1,0:T(8,128)(2,1)S(1)}, bf16[208,256]{1,0:T(8,128)(2,1)S(1)}, u32[]{:S(2)}, u32[]{:S(2)}) %collective-permute-start.6) | collective-permute-done | bytes 106528 | tf_op jit(solution)/shard_map/ppermute | solution.py:834
  37.1 1.8 %collective-permute-done.3.rest_2_ = bf16[208,256]{1,0:T(8,128)(2,1)S(1)} collective-permute-done((bf16[208,256]{1,0:T(8,128)(2,1)S(1)}, bf16[208,256]{1,0:T(8,128)(2,1)S(1)}, u32[]{:S(2)}, u32[]{:S(2)}) %collective-permute-start.3) | collective-permute-done | bytes 106528 | tf_op jit(solution)/shard_map/ppermute | solution.py:834
  39.0 3.7 %collective-permute-done.4.rest_3_ = bf16[208,256]{1,0:T(8,128)(2,1)S(1)} collective-permute-done((bf16[208,256]{1,0:T(8,128)(2,1)S(1)}, bf16[208,256]{1,0:T(8,128)(2,1)S(1)}, u32[]{:S(2)}, u32[]{:S(2)}) %collective-permute-start.4) | collective-permute-done | bytes 106528 | tf_op jit(solution)/shard_map/ppermute | solution.py:834
  42.7 4.6 %tiles.1 = (f32[512,256]{1,0:T(8,128)S(1)}, f32[512,256]{1,0:T(8,128)S(1)}, f32[512,256]{1,0:T(8,128)S(1)}, f32[512,128]{1,0:T(8,128)S(1)}, f32[520,256]{1,0:T(8...) custom-call(s32[6]{0:T(128)S(1)} %stack.23.ids, ...), custom_call_target="tpu_custom_call" | custom-call | flops 1000000 | bytes 4000000 | tf_op jit(solution)/shard_map/tiles/pallas_call | solution.py:123
  47.4 1.0 %collective-permute-start.10 = (f32[8,128]{1,0:T(8,128)S(1)}, f32[8,128]{1,0:T(8,128)S(1)}, u32[]{:S(2)}, u32[]{:S(2)}) collective-permute-start(f32[8,128]{1,0:T(8,128)S(1)} %get-tuple-element.43), channel_id=1, source_target_pairs={{0,24},{8,16},{16,8},{24,0},{1,25},{9,17},{17,9},{25,1},{2,26},{10... | collective-permute-start | bytes 12296 | tf_op jit(solution)/shard_map/ppermute | solution.py:784
  48.4 1.3 %collective-permute-start.11 = (f32[8,128]{1,0:T(8,128)S(1)}, f32[8,128]{1,0:T(8,128)S(1)}, u32[]{:S(2)}, u32[]{:S(2)}) collective-permute-start(f32[8,128]{1,0:T(8,128)S(1)} %get-tuple-element.44), channel_id=1, source_target_pairs={{0,1},{1,0},{2,3},{3,2},{4,5},{5,4},{6,7},{7,6},{8,9},{9,8},{10,11... | collective-permute-start | bytes 12296 | tf_op jit(solution)/shard_map/ppermute | solution.py:784
  49.7 3.4 %collective-permute-start.12 = (f32[8,128]{1,0:T(8,128)S(1)}, f32[8,128]{1,0:T(8,128)S(1)}, u32[]{:S(2)}, u32[]{:S(2)}) collective-permute-start(f32[8,128]{1,0:T(8,128)S(1)} %get-tuple-element.45), channel_id=1, source_target_pairs={{0,7},{1,2},{2,1},{3,4},{4,3},{5,6},{6,5},{7,0},{8,15},{9,10},{10,... | collective-permute-start | bytes 12296 | tf_op jit(solution)/shard_map/ppermute | solution.py:784
  53.1 2.9 %collective-permute-done.12.col_next = f32[8,128]{1,0:T(8,128)S(1)} collective-permute-done((f32[8,128]{1,0:T(8,128)S(1)}, f32[8,128]{1,0:T(8,128)S(1)}, u32[]{:S(2)}, u32[]{:S(2)}) %collective-permute-start.12) | collective-permute-done | bytes 4128 | tf_op jit(solution)/shard_map/ppermute | solution.py:784
  56.0 4.3 %operator.1 = (f32[512,256]{1,0:T(8,128)S(1)}, f32[512,256]{1,0:T(8,128)S(1)}, f32[512,256]{1,0:T(8,128)S(1)}, f32[16,128]{1,0:T(8,128)S(1)}) custom-call(s32[6]{0:T(128)S(1)} %stack.23.ids, f32[512,256]{1,0:T(8,128)S(1)} %get-tuple-element.37.residual, f32[512,256]{1,0:T(8,128)S(1)} %get-tuple-element.38.shaped, f32[512,256]{1,0:T(8,128)S(1)} %get-tuple-element.39.weight_x, ...), custom_call_target="tpu_custom_call" | custom-call | flops 1000000 | bytes 4000000 | tf_op jit(solution)/shard_map/operator/pallas_call | solution.py:123
  60.4 14.2 %all_to_all.5.gathered = f32[32,16,128]{2,1,0:T(8,128)S(1)} all-to-all(f32[32,16,128]{2,1,0:T(8,128)S(1)} %broadcast_in_dim.2), channel_id=1, replica_groups=mesh['row'=4,'col'=8] {'row','col'}, dimensions={0} | all-to-all | bytes 524288 | tf_op jit(solution)/shard_map/all_to_all | solution.py:884
  74.6 1.9 %finish.1 = (f32[512,256]{1,0:T(8,128)}, f32[512,256]{1,0:T(8,128)}) custom-call(s32[6]{0:T(128)S(1)} %stack.23.ids, f32[32,16,128]{2,1,0:T(8,128)S(1)} %all_to_all.5.gathered, f32[512,256]{1,0:T(8,128)S(1)} %get-tuple-element.37.residual, f32[512,256]{1,0:T(8,128)S(1)} %get-tuple-element.38.shaped, f32[512,256]{1,0:T(8,128)S(1)} %get-tuple-element.47.operated, ...), custom_call_target="tpu_custom_call" | custom-call | flops 1000000 | bytes 4000000 | tf_op jit(solution)/shard_map/finish/pallas_call | solution.py:123
  (23 shorter events, 0.3 us)
Async XLA Ops:
  1.6 15.8 %collective-permute-start.1 = (bf16[4,8,2048]{2,1,0:T(8,128)(2,1)S(1)}, bf16[4,8,2048]{2,1,0:T(8,128)(2,1)S(1)}, u32[]{:S(2)}, u32[]{:S(2)}) collective-permute-start(bf16[4,8,2048]{2,1,0:T(8,128)(2,1)S(1)} %get-tuple-element.54), channel_id=1, source_target_pairs={{0,31},{1,2},{2,1},{3,4},{4,3},{5,6},{6,5},{7,8},{8,7},{9,10},{10,... | collective-permute-start | bytes 393224 | tf_op jit(solution)/shard_map/ppermute | solution.py:784
  8.1 9.4 %collective-permute-start = (bf16[4,8,2048]{2,1,0:T(8,128)(2,1)S(1)}, bf16[4,8,2048]{2,1,0:T(8,128)(2,1)S(1)}, u32[]{:S(2)}, u32[]{:S(2)}) collective-permute-start(bf16[4,8,2048]{2,1,0:T(8,128)(2,1)S(1)} %get-tuple-element.55), channel_id=1, source_target_pairs={{0,1},{1,0},{2,3},{3,2},{4,5},{5,4},{6,7},{7,6},{8,9},{9,8},{10,11... | collective-permute-start | bytes 393224 | tf_op jit(solution)/shard_map/ppermute | solution.py:784
  8.2 1.0 %copy-start.3 = (bf16[2,64,2048]{2,1,0:T(8,128)(2,1)S(1)}, bf16[2,64,2048]{2,1,0:T(8,128)(2,1)}, u32[]{:S(2)}) copy-start(bf16[2,64,2048]{2,1,0:T(8,128)(2,1)} %first.1) | copy-start | bytes 1572868
  9.2 1.0 %copy-start.4 = (bf16[2,64,2048]{2,1,0:T(8,128)(2,1)S(1)}, bf16[2,64,2048]{2,1,0:T(8,128)(2,1)}, u32[]{:S(2)}) copy-start(bf16[2,64,2048]{2,1,0:T(8,128)(2,1)} %second.1) | copy-start | bytes 1572868
  17.5 25.2 %copy-start = (bf16[2048,512]{1,0:T(8,128)(2,1)S(1)}, bf16[2048,512]{1,0:T(8,128)(2,1)}, u32[]{:S(2)}) copy-start(bf16[2048,512]{1,0:T(8,128)(2,1)} %constant.38.clone.rest_8_.rest_0_) | copy-start | bytes 6291460
  17.5 25.2 %copy-start.1 = (f32[512,256]{1,0:T(8,128)S(1)}, f32[512,256]{1,0:T(8,128)}, u32[]{:S(2)}) copy-start(f32[512,256]{1,0:T(8,128)} %constant.40.clone.rest_10_.rest_2_) | copy-start | bytes 1572868
  17.5 25.2 %copy-start.2 = (bf16[1024,256]{1,0:T(8,128)(2,1)S(1)}, bf16[1024,256]{1,0:T(8,128)(2,1)}, u32[]{:S(2)}) copy-start(bf16[1024,256]{1,0:T(8,128)(2,1)} %constant.39.clone.rest_9_.rest_1_) | copy-start | bytes 1572868
  20.2 14.0 %collective-permute-start.5 = (bf16[208,256]{1,0:T(8,128)(2,1)S(1)}, bf16[208,256]{1,0:T(8,128)(2,1)S(1)}, u32[]{:S(2)}, u32[]{:S(2)}) collective-permute-start(bf16[208,256]{1,0:T(8,128)(2,1)S(1)} %get-tuple-element.33), channel_id=1, source_target_pairs={{0,4},{1,5},{2,6},{3,7},{4,0},{5,1},{6,2},{7,3},{8,12},{9,13},{10,... | collective-permute-start | bytes 319496 | tf_op jit(solution)/shard_map/ppermute | solution.py:834
  21.0 16.1 %collective-permute-start.6 = (bf16[208,256]{1,0:T(8,128)(2,1)S(1)}, bf16[208,256]{1,0:T(8,128)(2,1)S(1)}, u32[]{:S(2)}, u32[]{:S(2)}) collective-permute-start(bf16[208,256]{1,0:T(8,128)(2,1)S(1)} %get-tuple-element.34), channel_id=1, source_target_pairs={{0,5},{1,4},{2,7},{3,6},{4,1},{5,0},{6,3},{7,2},{8,13},{9,12},{10,... | collective-permute-start | bytes 319496 | tf_op jit(solution)/shard_map/ppermute | solution.py:834
  24.7 12.4 %collective-permute-start.7 = (bf16[208,256]{1,0:T(8,128)(2,1)S(1)}, bf16[208,256]{1,0:T(8,128)(2,1)S(1)}, u32[]{:S(2)}, u32[]{:S(2)}) collective-permute-start(bf16[208,256]{1,0:T(8,128)(2,1)S(1)} %get-tuple-element.35), channel_id=1, source_target_pairs={{0,6},{1,7},{2,4},{3,5},{4,2},{5,3},{6,0},{7,1},{8,14},{9,15},{10,... | collective-permute-start | bytes 319496 | tf_op jit(solution)/shard_map/ppermute | solution.py:834
  24.7 12.4 %collective-permute-start.8 = (bf16[208,256]{1,0:T(8,128)(2,1)S(1)}, bf16[208,256]{1,0:T(8,128)(2,1)S(1)}, u32[]{:S(2)}, u32[]{:S(2)}) collective-permute-start(bf16[208,256]{1,0:T(8,128)(2,1)S(1)} %get-tuple-element.36), channel_id=1, source_target_pairs={{0,7},{1,6},{2,5},{3,4},{4,3},{5,2},{6,1},{7,0},{8,15},{9,14},{10,... | collective-permute-start | bytes 319496 | tf_op jit(solution)/shard_map/ppermute | solution.py:834
  30.6 6.5 %collective-permute-start.2 = (bf16[208,256]{1,0:T(8,128)(2,1)S(1)}, bf16[208,256]{1,0:T(8,128)(2,1)S(1)}, u32[]{:S(2)}, u32[]{:S(2)}) collective-permute-start(bf16[208,256]{1,0:T(8,128)(2,1)S(1)} %get-tuple-element.30), channel_id=1, source_target_pairs={{0,1},{1,0},{2,3},{3,2},{4,5},{5,4},{6,7},{7,6},{8,9},{9,8},{10,11... | collective-permute-start | bytes 319496 | tf_op jit(solution)/shard_map/ppermute | solution.py:834
  34.3 4.7 %collective-permute-start.3 = (bf16[208,256]{1,0:T(8,128)(2,1)S(1)}, bf16[208,256]{1,0:T(8,128)(2,1)S(1)}, u32[]{:S(2)}, u32[]{:S(2)}) collective-permute-start(bf16[208,256]{1,0:T(8,128)(2,1)S(1)} %get-tuple-element.31), channel_id=1, source_target_pairs={{0,2},{1,3},{2,0},{3,1},{4,6},{5,7},{6,4},{7,5},{8,10},{9,11},{10,... | collective-permute-start | bytes 319496 | tf_op jit(solution)/shard_map/ppermute | solution.py:834
  37.1 5.6 %collective-permute-start.4 = (bf16[208,256]{1,0:T(8,128)(2,1)S(1)}, bf16[208,256]{1,0:T(8,128)(2,1)S(1)}, u32[]{:S(2)}, u32[]{:S(2)}) collective-permute-start(bf16[208,256]{1,0:T(8,128)(2,1)S(1)} %get-tuple-element.32), channel_id=1, source_target_pairs={{0,3},{1,2},{2,1},{3,0},{4,7},{5,6},{6,5},{7,4},{8,11},{9,10},{10,... | collective-permute-start | bytes 319496 | tf_op jit(solution)/shard_map/ppermute | solution.py:834
  47.3 5.8 %collective-permute-start.9 = (f32[8,128]{1,0:T(8,128)S(1)}, f32[8,128]{1,0:T(8,128)S(1)}, u32[]{:S(2)}, u32[]{:S(2)}) collective-permute-start(f32[8,128]{1,0:T(8,128)S(1)} %get-tuple-element.42), channel_id=1, source_target_pairs={{0,8},{8,0},{16,24},{24,16},{1,9},{9,1},{17,25},{25,17},{2,10},{10... | collective-permute-start | bytes 12296 | tf_op jit(solution)/shard_map/ppermute | solution.py:784
  47.4 5.7 %collective-permute-start.10 = (f32[8,128]{1,0:T(8,128)S(1)}, f32[8,128]{1,0:T(8,128)S(1)}, u32[]{:S(2)}, u32[]{:S(2)}) collective-permute-start(f32[8,128]{1,0:T(8,128)S(1)} %get-tuple-element.43), channel_id=1, source_target_pairs={{0,24},{8,16},{16,8},{24,0},{1,25},{9,17},{17,9},{25,1},{2,26},{10... | collective-permute-start | bytes 12296 | tf_op jit(solution)/shard_map/ppermute | solution.py:784
  48.4 4.7 %collective-permute-start.11 = (f32[8,128]{1,0:T(8,128)S(1)}, f32[8,128]{1,0:T(8,128)S(1)}, u32[]{:S(2)}, u32[]{:S(2)}) collective-permute-start(f32[8,128]{1,0:T(8,128)S(1)} %get-tuple-element.44), channel_id=1, source_target_pairs={{0,1},{1,0},{2,3},{3,2},{4,5},{5,4},{6,7},{7,6},{8,9},{9,8},{10,11... | collective-permute-start | bytes 12296 | tf_op jit(solution)/shard_map/ppermute | solution.py:784
  49.7 6.3 %collective-permute-start.12 = (f32[8,128]{1,0:T(8,128)S(1)}, f32[8,128]{1,0:T(8,128)S(1)}, u32[]{:S(2)}, u32[]{:S(2)}) collective-permute-start(f32[8,128]{1,0:T(8,128)S(1)} %get-tuple-element.45), channel_id=1, source_target_pairs={{0,7},{1,2},{2,1},{3,4},{4,3},{5,6},{6,5},{7,0},{8,15},{9,10},{10,... | collective-permute-start | bytes 12296 | tf_op jit(solution)/shard_map/ppermute | solution.py:784

commit v2 on v1

--- a/solution.py
+++ b/solution.py
@@ -18,6 +18,9 @@
 EDGE = 16
 TURN = 2.0 * math.pi
 CODE_SPAN = 248.0
+POWER_BASE = 2.0**7.5
+TINY = 1e-30
+SCALE_LANE = 5
 VMEM_LIMIT = 40 * 1024 * 1024
 
 ATAN = (
@@ -102,6 +105,21 @@
     return (jnp.log2(code.astype(jnp.float32)) + 0.5 * CODE_SPAN) * (1.0 / CODE_SPAN)
 
 
+def encode_power(value, scale):
+    share = jnp.minimum(jnp.abs(value) / jnp.maximum(scale, TINY), 1.0) * POWER_BASE
+    for _ in range(4):
+        share = share * share
+    return jnp.where(value < 0.0, -share, share)
+
+
+def decode_power(code, scale):
+    share = jnp.abs(code)
+    for _ in range(4):
+        share = jnp.sqrt(share)
+    share = share * (scale * (1.0 / POWER_BASE))
+    return jnp.where(code < 0.0, -share, share)
+
+
 def split(value):
     high = value.astype(jnp.bfloat16)
     return high, (value - high.astype(jnp.float32)).astype(jnp.bfloat16)
@@ -116,7 +134,7 @@
     return lax.broadcasted_iota(jnp.int32, shape, 1)
 
 
-def call(body, outs, args, scratch, name, smem_first=True, flops=1000000):
+def call(body, outs, args, scratch, name, smem_first=True, flops=1000000, out_space=pltpu.VMEM):
     specs = [pl.BlockSpec(memory_space=pltpu.VMEM)] * len(args)
     if smem_first:
         specs[0] = pl.BlockSpec(memory_space=pltpu.SMEM)
@@ -124,7 +142,7 @@
         body,
         out_shape=[jax.ShapeDtypeStruct(s, d) for s, d in outs],
         in_specs=specs,
-        out_specs=[pl.BlockSpec(memory_space=pltpu.VMEM)] * len(outs),
+        out_specs=[pl.BlockSpec(memory_space=out_space)] * len(outs),
         scratch_shapes=scratch,
         compiler_params=pltpu.CompilerParams(vmem_limit_bytes=VMEM_LIMIT),
         cost_estimate=pl.CostEstimate(flops=flops, bytes_accessed=4000000, transcendentals=0),
@@ -136,7 +154,7 @@
     return pl.pallas_call(
         body,
         out_shape=[jax.ShapeDtypeStruct(s, d) for s, d in outs],
-        in_specs=[pl.BlockSpec(memory_space=pl.ANY)] * 2,
+        in_specs=[pl.BlockSpec(memory_space=pltpu.SMEM)] + [pl.BlockSpec(memory_space=pltpu.HBM)] * 2,
         out_specs=[pl.BlockSpec(memory_space=pltpu.VMEM)] * len(outs),
         scratch_shapes=scratch,
         compiler_params=pltpu.CompilerParams(vmem_limit_bytes=VMEM_LIMIT),
@@ -186,53 +204,66 @@
     return low, high
 
 
-def interior_kernel(lines, width, tile, columns, first, second, ranged, codes, rims, raw, prod, field, sems):
+def first_of_half(own, half, across):
+    return (own & half) ^ (half if across else 0)
+
+
+def window(lines, width, tile, columns, across, own, rows):
+    half = columns // 2
+    span = half * tile + 2 * LANES
+    first_tile = first_of_half(own, half, across)
+    start = pl.multiple_of(first_tile * tile, LANES)
+    pixel = lanes_of((rows, span)) + (start - LANES)
+    return first_tile, start, span, jnp.logical_and(pixel >= 0, pixel < width)
+
+
+def interior_kernel(lines, width, tile, columns, across, ids, first, second, ranged, codes, rims, raw, prod, field, sems):
+    half = columns // 2
     chunk = 16
+    first_tile, start, span, in_image = window(lines, width, tile, columns, across, ids[1], 8)
+    upper = jnp.where(first_tile == 0, 0, 1)
+    source = pl.multiple_of(upper * (width // 2 - 2 * LANES), LANES)
+    target = pl.multiple_of((1 - upper) * 2 * LANES, LANES)
+    size = width // 2 + 2 * LANES
+    blank = pl.multiple_of(upper * size, LANES)
     copies = []
     for i in range(lines // chunk):
         rs = pl.ds(i * chunk, chunk)
         for a, ref in enumerate((first, second)):
-            copy = pltpu.make_async_copy(ref.at[:, rs, :], raw.at[a, :, rs, :], sems.at[2 * i + a])
+            copy = pltpu.make_async_copy(
+                ref.at[:, rs, pl.ds(source, size)], raw.at[a, :, rs, pl.ds(target, size)], sems.at[2 * i + a]
+            )
             copy.start()
             copies.append(copy)
-    zero = jnp.zeros((lines, LANES), jnp.float32)
-    for f in range(4):
-        prod[f, :, 0:LANES] = zero[:chunk]
-        prod[f, :, LANES + width :] = zero[:chunk]
-        ranged[f, :, 0:LANES] = zero
-        ranged[f, :, LANES + width :] = zero
-    wide = min(width, 1024)
+    for a in range(2):
+        for part in range(2):
+            raw[a, part, :, pl.ds(blank, 2 * LANES)] = jnp.zeros((lines, 2 * LANES), jnp.bfloat16)
     for i in range(lines // chunk):
         copies[2 * i].wait()
         copies[2 * i + 1].wait()
         rs = slice(i * chunk, (i + 1) * chunk)
-        for c in range(0, width, 512):
+        for c in range(0, span + 2 * LANES, 512):
             cs = slice(c, c + 512)
             values = products(raw[0, 0, rs, cs], raw[0, 1, rs, cs], raw[1, 0, rs, cs], raw[1, 1, rs, cs])
             for f in range(4):
-                prod[f, :, LANES + c : LANES + c + 512] = values[f]
+                prod[f, :, cs] = values[f]
         for f in range(4):
             for r in range(0, chunk, 8):
-                for c in range(0, width, wide):
-                    total = along_range(prod[f, r : r + 8, c : c + wide + 2 * LANES])
-                    row = i * chunk + r
-                    ranged[f, row : row + 8, LANES + c : LANES + c + wide] = total[:, LANES : LANES + wide]
+                total = along_range(prod[f, r : r + 8, :])[:, LANES : LANES + span]
+                row = i * chunk + r
+                ranged[f, row : row + 8, :] = jnp.where(in_image, total, 0.0)
     inner = lines - 2 * EDGE
-    for f in range(2):
-        field[f, :, 0:LANES] = zero[:inner]
-        field[f, :, LANES + width :] = zero[:inner]
-    for c in range(0, width, LANES):
-        cs = slice(LANES + c, 2 * LANES + c)
-        out = slice(c, c + LANES)
+    for c in range(0, span, LANES):
+        cs = slice(c, c + LANES)
         for r in range(0, inner, 16):
             smoothed = [along_azimuth(ranged, f, EDGE + r, 16, cs) for f in range(4)]
             phase, gain = phase_gain(smoothed)
             field[0, r : r + 16, cs] = phase
             field[1, r : r + 16, cs] = gain
-            codes[0, r : r + 16, out], codes[1, r : r + 16, out] = split(phase)
-            codes[2, r : r + 16, out] = encode_gain(gain)
+            codes[0, r : r + 16, cs], codes[1, r : r + 16, cs] = split(phase)
+            codes[2, r : r + 16, cs] = encode_gain(gain)
     groups = lines // 8
-    for t in range(columns):
+    for t in range(half):
         rims[t] = rim_block(field, groups, range(EDGE // 8, (lines - EDGE) // 8), EDGE // 8, t * tile, tile, None)
 
 
@@ -260,17 +291,13 @@
     outs, (prod, seg, field, ends) = rest[:half], rest[half:]
     own = ids[1]
     odd = ids[4]
-    first_tile = (own & half) ^ (half if across else 0)
-    span = half * tile + 2 * LANES
-    start = pl.multiple_of(first_tile * tile, LANES)
+    first_tile, start, span, in_image = window(lines, width, tile, columns, across, own, HALO)
     inside = (
         jnp.where(ids[2] == 0, 0.0, 1.0).astype(jnp.float32),
         jnp.where(ids[2] == ids[3] - 1, 0.0, 1.0).astype(jnp.float32),
     )
     zero = jnp.zeros((HALO, 2 * LANES), jnp.float32)
     own_rows = EDGE + HALO
-    pixel = lanes_of((HALO, span)) + (start - LANES)
-    in_image = jnp.logical_and(pixel >= 0, pixel < width)
     for e in range(2):
         flag = odd if e == 0 else 1 - odd
         keep = flag.astype(jnp.float32)
@@ -291,10 +318,10 @@
             total = jnp.where(in_image, total, 0.0)
             if e == 0:
                 seg[e, f, 0:HALO, :] = total
-                seg[e, f, HALO:, :] = ranged[f, 0:own_rows, pl.ds(start, span)]
+                seg[e, f, HALO:, :] = ranged[f, 0:own_rows, :]
             else:
                 seg[e, f, own_rows:, :] = total
-                seg[e, f, 0:own_rows, :] = ranged[f, lines - own_rows :, pl.ds(start, span)]
+                seg[e, f, 0:own_rows, :] = ranged[f, lines - own_rows :, :]
     for e in range(2):
         ref = seg.at[e]
         for c in range(0, span, LANES):
@@ -320,15 +347,14 @@
         target = own ^ s
         local = pl.multiple_of((target - first_tile) * tile, LANES)
         cs = pl.ds(pl.multiple_of(local + LANES, LANES), tile)
-        wide = pl.ds(pl.multiple_of(target * tile, LANES), tile)
         for i in range(3):
-            out[i * lines + EDGE : i * lines + EDGE + inner, :] = codes[i, :, wide]
+            out[i * lines + EDGE : i * lines + EDGE + inner, :] = codes[i, :, cs]
         for e in range(2):
             row = 0 if e == 0 else lines - EDGE
             rs = slice(e * EDGE, (e + 1) * EDGE)
             out[row : row + EDGE, :], out[lines + row : lines + row + EDGE, :] = split(field[0, rs, cs])
             out[2 * lines + row : 2 * lines + row + EDGE, :] = encode_gain(field[1, rs, cs])
-        block = rims[target]
+        block = rims[target - first_tile]
         block = rim_block(field, groups, range(edge_groups), 0, local, tile, block, pl.multiple_of)
         block = rim_block(
             field, groups, range(groups - edge_groups, groups), groups - 2 * edge_groups, local, tile, block,
@@ -654,8 +680,8 @@
     tile_az, tile, ids, residual, shaped, weight_x, rim_x, weight_y, row_pair, row_next, col_pair, col_next, *rest
 ):
     tables, inverse = rest[:2], rest[2]
-    operated, shaped2, operated2, chunk = rest[3:7]
-    u, flux_x, flux_rim, flux_y = rest[7:]
+    operated, shaped2, operated2, chunk, roots = rest[3:8]
+    u, flux_x, flux_rim, flux_y = rest[8:]
     pairs = table_pairs(tables)
     row_odd, col_odd = ids[5] == 1, ids[4] == 1
     up = jnp.where(row_odd, row_pair[0:2, :], row_next[0:2, :])
@@ -673,11 +699,8 @@
     image = precondition(operated[...], pairs, inverse)
     shaped2[...] = image
     u[HALO : HALO + tile_az, :] = image
-    zero = jnp.zeros((1, tile), jnp.float32)
-    u[HALO - 1 : HALO, :] = zero
-    u[HALO + tile_az : HALO + tile_az + 1, :] = zero
     apply_operator(
-        tile_az, tile, u, weight_x, rim_x, weight_y, flux_x, flux_rim, flux_y, None, None, operated2
+        tile_az, tile, u, weight_x, rim_x, weight_y, flux_x, flux_rim, flux_y, left, right, operated2
     )
     lane = lanes_of((1, LANES))
     sums = jnp.zeros((1, LANES), jnp.float32)
@@ -691,43 +714,77 @@
         )
     ):
         sums = jnp.where(lane == i, inner(a, b, tile_az), sums)
-    chunk[8:16, :] = jnp.broadcast_to(sums, (8, LANES))
-    top = jnp.sqrt(weight_y[0:1, :]) * shaped2[0:1, :]
-    bottom = jnp.sqrt(weight_y[tile_az : tile_az + 1, :]) * shaped2[tile_az - 1 : tile_az, :]
-    for h in range(tile // LANES):
-        cs = slice(h * LANES, (h + 1) * LANES)
-        chunk[8 + 2 + h : 8 + 3 + h, :] = top[:, cs]
-        chunk[8 + 4 + h : 8 + 5 + h, :] = bottom[:, cs]
+    def rows_of(x):
+        return jnp.concatenate([x[:, h : h + LANES] for h in range(0, tile, LANES)], axis=0)
+
+    weight_t, weight_b = rows_of(weight_y[0:1, :]), rows_of(weight_y[tile_az : tile_az + 1, :])
+    weight_l, weight_r = line_groups(weight_x, tile_az, 0), line_groups(rim_x, tile_az, LANES - 1)
+    top = rows_of(image_row(shaped2, shaped, 0))
+    bottom = rows_of(image_row(shaped2, shaped, tile_az - 1))
+    left_rim = line_groups(shaped2, tile_az, 0) - line_groups(shaped, tile_az, 0)
+    right_rim = line_groups(shaped2, tile_az, tile - 1) - line_groups(shaped, tile_az, tile - 1)
+    known = jnp.sum(weight_t * up * top + weight_b * down * bottom, keepdims=True) + jnp.sum(
+        weight_l * left * left_rim + weight_r * right * right_rim, keepdims=True
+    )
+    sums = jnp.where(lane == 4, sums - known, sums)
     half = tile_az // 8
-    left_rim = jnp.sqrt(line_groups(weight_x, tile_az, 0)) * line_groups(shaped2, tile_az, 0)
-    right_rim = jnp.sqrt(line_groups(rim_x, tile_az, LANES - 1)) * line_groups(shaped2, tile_az, tile - 1)
     wide = lanes_of((8, LANES))
-    chunk[0:8, :] = jnp.where(wide < half, left_rim, pltpu.roll(right_rim, half, 1))
+    root_sides = jnp.sqrt(jnp.where(wide < half, weight_l, pltpu.roll(weight_r, half, 1)))
+    sides = root_sides * jnp.where(wide < half, left_rim, pltpu.roll(right_rim, half, 1))
+    root_ends = jnp.sqrt(jnp.concatenate([weight_t, weight_b], axis=0))
+    ends = root_ends * jnp.concatenate([top, bottom], axis=0)
+    scale = jnp.maximum(jnp.max(jnp.abs(sides), keepdims=True), jnp.max(jnp.abs(ends), keepdims=True))
+    scale = (scale * 1.01).astype(jnp.bfloat16).astype(jnp.float32)
+    sums = jnp.where(lane == SCALE_LANE, scale, sums)
+    high = sums.astype(jnp.bfloat16).astype(jnp.float32)
+    middle = (sums - high).astype(jnp.bfloat16).astype(jnp.float32)
+    rest_ = sums - high - middle
+    sums = high + pltpu.roll(middle, 8, 1) + pltpu.roll(rest_, 16, 1)
+    chunk[...] = jnp.concatenate(
+        [encode_power(sides, scale), encode_power(ends, scale), jnp.broadcast_to(sums, (4, LANES))], axis=0
+    ).astype(jnp.bfloat16)
+    roots[...] = jnp.concatenate([root_sides, root_ends, root_ends], axis=0)
+
+
+def image_row(a, b, row):
+    return a[row : row + 1, :] - b[row : row + 1, :]
 
 
 def last_kernel(
-    tile_az, tile, rows, columns, ids, gathered, residual, shaped, operated, shaped2, operated2, weight_x, rim_x,
-    weight_y, solution_out, residual_out
+    tile_az, tile, rows, columns, ids, gathered, residual, shaped, operated, shaped2, operated2, roots,
+    solution_hbm, residual_hbm, solution_out, residual_out, sems
 ):
     half = tile_az // 8
     lane = lanes_of((8, LANES))
-    total = jnp.zeros((8, LANES), jnp.float32)
+    total = jnp.zeros((4, LANES), jnp.float32)
     cross_x = jnp.zeros((8, LANES), jnp.float32)
     cross_y = jnp.zeros((2, LANES), jnp.float32)
+    values = {}
+
+    def decoded(i):
+        x = gathered[i].astype(jnp.float32)
+        return jnp.concatenate([decode_power(x[0:12, :], x[12:13, SCALE_LANE : SCALE_LANE + 1]), x[12:16, :]], axis=0)
+
+    def value_of(i):
+        if i not in values:
+            values[i] = decoded(i)
+        return values[i]
+
     for r in range(rows):
         for c in range(columns):
             i = r * columns + c
-            total = total + gathered[i, 8:16, :]
+            here = value_of(i)
+            total = total + here[12:16, :]
             if c + 1 < columns:
-                right = pltpu.roll(gathered[i, 0:8, :], LANES - half, 1)
-                cross_x = cross_x + right * gathered[i + 1, 0:8, :]
+                cross_x = cross_x + pltpu.roll(here[0:8, :], LANES - half, 1) * value_of(i + 1)[0:8, :]
             if r + 1 < rows:
-                cross_y = cross_y + gathered[i, 12:14, :] * gathered[i + columns, 10:12, :]
+                cross_y = cross_y + here[10:12, :] * value_of(i + columns)[8:10, :]
     cross = jnp.sum(jnp.where(lane < half, cross_x, 0.0), keepdims=True) + jnp.sum(cross_y, keepdims=True)
     wide = total[0:1, :]
     first_lane = lanes_of((1, LANES))
     pick = [
-        jnp.sum(jnp.where(first_lane == i, wide, 0.0), axis=1, keepdims=True) for i in range(5)
+        jnp.sum(jnp.where(first_lane % 8 == i, jnp.where(first_lane < 24, wide, 0.0), 0.0), axis=1, keepdims=True)
+        for i in range(5)
     ]
     dot0, curve0, mixed, cross_dot, curve2 = pick
     curve2 = curve2 - 2.0 * cross
@@ -750,15 +807,17 @@
     down, down_ok = neighbour(row < rows - 1, here + columns)
     left, left_ok = neighbour(col > 0, here - 1)
     right, right_ok = neighbour(col < columns - 1, here + 1)
-    from_left = pltpu.roll(gathered[left, 0:8, :], LANES - half, 1) * left_ok
-    from_right = gathered[right, 0:8, :] * right_ok
-    top = jnp.concatenate([gathered[up, 12 + h : 13 + h, :] for h in range(tile // LANES)], axis=1) * up_ok
-    bottom = jnp.concatenate([gathered[down, 10 + h : 11 + h, :] for h in range(tile // LANES)], axis=1) * down_ok
-    top = top * jnp.sqrt(weight_y[0:1, :])
-    bottom = bottom * jnp.sqrt(weight_y[tile_az : tile_az + 1, :])
-    from_left = from_left * jnp.sqrt(line_groups(weight_x, tile_az, 0))
-    from_right = from_right * jnp.sqrt(line_groups(rim_x, tile_az, LANES - 1))
-    step = min(tile_az, 32)
+    near = [decoded(i) for i in (left, right, up, down)]
+    from_left = pltpu.roll(near[0][0:8, :], LANES - half, 1) * left_ok
+    from_right = pltpu.roll(near[1][0:8, :], half, 1) * right_ok
+    top = jnp.concatenate([near[2][10 + h : 11 + h, :] for h in range(tile // LANES)], axis=1) * up_ok
+    bottom = jnp.concatenate([near[3][8 + h : 9 + h, :] for h in range(tile // LANES)], axis=1) * down_ok
+    top = top * jnp.concatenate([roots[8 + h : 9 + h, :] for h in range(tile // LANES)], axis=1)
+    bottom = bottom * jnp.concatenate([roots[10 + h : 11 + h, :] for h in range(tile // LANES)], axis=1)
+    from_left = from_left * roots[0:8, :]
+    from_right = from_right * roots[0:8, :]
+    step = min(tile_az, 64)
+    copies = []
     for r in range(0, tile_az, step):
         rs = slice(r, r + step)
         solution_out[rs, :] = on_first * shaped[rs, :] - on_second * shaped2[rs, :]
@@ -766,14 +825,21 @@
         wide = lanes_of((step, tile))
         l = jnp.concatenate([spread_groups(from_left, r // 8, step // 8, 0)] * (tile // LANES), axis=1)
         q = q - jnp.where(wide == 0, l, 0.0)
-        l = jnp.concatenate([spread_groups(from_right, r // 8, step // 8, LANES - 1)] * (tile // LANES), axis=1)
+        l = jnp.concatenate([spread_groups(from_right, r // 8, step // 8, LANES - 1, half)] * (tile // LANES), axis=1)
         q = q - jnp.where(wide == tile - 1, l, 0.0)
-        deep = lax.broadcasted_iota(jnp.int32, (step, tile), 0)
+        if r == 0 or r + step == tile_az:
+            deep = lax.broadcasted_iota(jnp.int32, (step, tile), 0)
         if r == 0:
             q = q - jnp.where(deep == 0, jnp.broadcast_to(top, (step, tile)), 0.0)
         if r + step == tile_az:
             q = q - jnp.where(deep == step - 1, jnp.broadcast_to(bottom, (step, tile)), 0.0)
         residual_out[rs, :] = residual[rs, :] - on_first * operated[rs, :] + on_second * q
+        for n, (src, dst) in enumerate(((solution_out, solution_hbm), (residual_out, residual_hbm))):
+            copy = pltpu.make_async_copy(src.at[rs, :], dst.at[rs, :], sems.at[2 * (r // step) + n])
+            copy.start()
+            copies.append(copy)
+    for copy in copies:
+        copy.wait()
 
 
 def swapped(value, axis, count, step):
@@ -801,21 +867,22 @@
     from_next = swapped(jnp.where(odd, tail, head), axes, rows * columns, 1)
     wide = width + 2 * LANES
     if exchange == "permute":
-        ranged, codes, rims = interior(
-            functools.partial(interior_kernel, lines, width, tile, columns),
-            [((4, lines, wide), f32), ((3, lines - 2 * EDGE, width), bf16), ((columns, 8, LANES), f32)],
-            (first_slc, second_slc),
-            [
-                pltpu.VMEM((2, 2, lines, width), bf16),
-                pltpu.VMEM((4, 16, wide), f32),
-                pltpu.VMEM((2, lines - 2 * EDGE, wide), f32),
-                pltpu.SemaphoreType.DMA((lines // 8,)),
-            ],
-        )
         half = columns // 2
         span = half * tile + 2 * LANES
         sent = [None] * columns
+        sources = (first_slc, second_slc)
         for across in (True, False):
+            ranged, codes, rims = interior(
+                functools.partial(interior_kernel, lines, width, tile, columns, across),
+                [((4, lines, span), f32), ((3, lines - 2 * EDGE, span), bf16), ((half, 8, LANES), f32)],
+                (ids, *sources),
+                [
+                    pltpu.VMEM((2, 2, lines, span + 2 * LANES), bf16),
+                    pltpu.VMEM((4, 16, span + 2 * LANES), f32),
+                    pltpu.VMEM((2, lines - 2 * EDGE, span), f32),
+                    pltpu.SemaphoreType.DMA((lines // 8,)),
+                ],
+            )
             part = call(
                 functools.partial(border_kernel, lines, width, tile, columns, across),
                 [((3 * lines + 16, tile), bf16)] * half,
@@ -830,6 +897,11 @@
             )
             for i, value in enumerate(part):
                 sent[i + (half if across else 0)] = value
+            if across:
+                *part, first_slc, second_slc = lax.optimization_barrier((*part, first_slc, second_slc))
+                sources = (first_slc, second_slc)
+                for i, value in enumerate(part):
+                    sent[i + half] = value
         arrived = [sent[0]] + [
             lax.ppermute(sent[s], "col", [(i, i ^ s) for i in range(columns)]) for s in range(1, columns)
         ]
@@ -873,9 +945,9 @@
         swapped(col_pair, "col", columns, 0),
         swapped(col_next, "col", columns, 1),
     )
-    operated, shaped2, operated2, chunk = call(
+    operated, shaped2, operated2, chunk, roots = call(
         functools.partial(second_kernel, tile_az, tile),
-        [whole, whole, whole, ((16, LANES), f32)],
+        [whole, whole, whole, ((16, LANES), bf16), ((16, LANES), f32)],
         (ids, residual, shaped, weight_x, rim_x, weight_y, *rims, *tables, inverse),
         [padded, *fluxes],
         "operator",
@@ -886,9 +958,14 @@
         call(
             functools.partial(last_kernel, tile_az, tile, rows, columns),
             [whole, whole],
-            (ids, gathered, residual, shaped, operated, shaped2, operated2, weight_x, rim_x, weight_y),
-            [],
+            (ids, gathered, residual, shaped, operated, shaped2, operated2, roots),
+            [
+                pltpu.VMEM((tile_az, tile), f32),
+                pltpu.VMEM((tile_az, tile), f32),
+                pltpu.SemaphoreType.DMA((2 * (tile_az // min(tile_az, 64)),)),
+            ],
             "finish",
+            out_space=pltpu.HBM,
         )
     )
 

time: 76.8 us -> 71.9 us (0.936)
  Pallas kernels: 23.5 us -> 27.2 us
  blocking collectives: 14.2 us -> 10.7 us
  waiting for transfers between devices: 12.9 us -> 9.66 us
  local copies, waits for them, and re-layouts: 3.17 us -> 1.17 us
    ppermute x7, waiting for transfers between devices: 9.95 us -> 4.64 us  [shards(): lax.ppermute(sent[s], 'col', [(i, i ^ s) for i in range(columns)])]
    all_to_all x1, blocking collectives: 14.2 us -> 10.7 us  [shards(): gathered = lax.all_to_all(spread, axes, 0, 0, tiled=True)]
    pallas_call x1 -> x2, Pallas kernels: 7.21 us -> 10.5 us  [interior(): pl.pallas_call(body, out_shape=[jax.ShapeDtypeStruct(s, d) for s, d in ou...]
    ppermute x6, waiting for transfers between devices: 2.91 us -> 5.02 us  [swapped(): return lax.ppermute(value, axis, pairs)]
    unnamed x10, local copies, waits for them, and re-layouts: 2.11 us -> 0.03 us
    ppermute x6, starting transfers between devices: 12.2 us -> 11.1 us  [swapped(): return lax.ppermute(value, axis, pairs)]
    ppermute x7, starting transfers between devices: 9.81 us -> 10.9 us  [shards(): lax.ppermute(sent[s], 'col', [(i, i ^ s) for i in range(columns)])]
  transfers between devices with their start and end apart: 13 -> 13, of which waited for: 5 -> 6; matrix products, arithmetic and copies ran while one was open for 0% -> 0% of each run, Pallas kernels for 13% -> 18%
where the time goes in v2:
time: 71.9 us; the launch traced here: 71.8 us
  Pallas kernels  27.2 us (38%)
  starting transfers between devices  22 us (31%)
  blocking collectives  10.7 us (15%)
  waiting for transfers between devices  9.66 us (13%)
  local copies, waits for them, and re-layouts  1.17 us (2%)
  between operations  0.93 us (1%)
    pallas_call x5, Pallas kernels, call(): pl.pallas_call(body, out_shape=[jax.ShapeDtypeStruct(s, d) for s, d in ou...  16.8 us
    ppermute x6, starting transfers between devices, swapped(): return lax.ppermute(value, axis, pairs)  11.1 us
    ppermute x7, starting transfers between devices, shards(): lax.ppermute(sent[s], 'col', [(i, i ^ s) for i in range(columns)])  10.9 us
    all_to_all x1, blocking collectives, shards(): gathered = lax.all_to_all(spread, axes, 0, 0, tiled=True)  10.7 us
    pallas_call x2, Pallas kernels, interior(): pl.pallas_call(body, out_shape=[jax.ShapeDtypeStruct(s, d) for s, d in ou...  10.5 us
    ppermute x6, waiting for transfers between devices, swapped(): return lax.ppermute(value, axis, pairs)  5.02 us
    ppermute x7, waiting for transfers between devices, shards(): lax.ppermute(sent[s], 'col', [(i, i ^ s) for i in range(columns)])  4.64 us
  transfers between devices with their start and end apart: 13, of which 6 were waited for; matrix products, arithmetic and copies ran while one was open for 0% of the time, Pallas kernels for 18%

profile of v2, /device:TPU:0, one launch (start us, length us, event | category | flops | bytes accessed | tf_op | source)
XLA Modules:
  0.0 71.8 jit_solution(14250261814937986208)
XLA Ops:
  0.7 1.0 %fusion = (bf16[2,8,2048]{2,1,0:T(8,128)(2,1)S(1)}, bf16[2,8,2048]{2,1,0:T(8,128)(2,1)S(1)}, bf16[2,8,2048]{2,1,0:T(8,128)(2,1)S(1)}, bf16[2,8,2048]{2,1,0:T(8,128)(2,1)S(1)}) fusion(bf16[2,64,2048]{2,1,0:T(8,128)(2,1)} %first.2, bf16[2,64,2048]{2,1,0:T(8,128)(2,1)} %second.2), kind=kLoop, calls=%fused_computation.4 | loop fusion | bytes 524288 | tf_op jit(solution)/shard_map/slice | solution.py:863
  1.7 6.4 %collective-permute-start.1 = (bf16[4,8,2048]{2,1,0:T(8,128)(2,1)S(1)}, bf16[4,8,2048]{2,1,0:T(8,128)(2,1)S(1)}, u32[]{:S(2)}, u32[]{:S(2)}) collective-permute-start(bf16[4,8,2048]{2,1,0:T(8,128)(2,1)S(1)} %get-tuple-element.74), channel_id=1, source_target_pairs={{0,31},{1,2},{2,1},{3,4},{4,3},{5,6},{6,5},{7,8},{8,7},{9,10},{10,... | collective-permute-start | bytes 393224 | tf_op jit(solution)/shard_map/ppermute | solution.py:850
  8.3 5.2 %interior.2 = (f32[4,64,1280]{2,1,0:T(8,128)S(1)}, bf16[3,32,1280]{2,1,0:T(8,128)(2,1)S(1)}, f32[4,8,128]{2,1,0:T(8,128)S(1)}) custom-call(s32[6]{0:T(128)S(1)} %stack.23.ids, bf16[2,64,2048]{2,1,0:T(8,128)(2,1)S(1)} %copy-done.1, bf16[2,64,2048]{2,1,0:T(8,128)(2,1)S(1)} %copy-done.2), custom_call_target="tpu_custom_call" | custom-call | flops 8000000 | bytes 4000000 | tf_op jit(solution)/shard_map/interior/pallas_call | solution.py:154
  13.4 1.5 %collective-permute-done.from_pair = bf16[4,8,2048]{2,1,0:T(8,128)(2,1)S(1)} collective-permute-done((bf16[4,8,2048]{2,1,0:T(8,128)(2,1)S(1)}, bf16[4,8,2048]{2,1,0:T(8,128)(2,1)S(1)}, u32[]{:S(2)}, u32[]{:S(2)}) %collective-permute-start) | collective-permute-done | bytes 131104 | tf_op jit(solution)/shard_map/ppermute | solution.py:850
  15.0 2.7 %borders.2 = (bf16[208,256]{1,0:T(8,128)(2,1)S(1)}, bf16[208,256]{1,0:T(8,128)(2,1)S(1)}, bf16[208,256]{1,0:T(8,128)(2,1)S(1)}, bf16[208,256]{1,0:T(8,128)(2,1)S(1)}) custom-call(s32[6]{0:T(128)S(1)} %stack.23.ids, f32[4,64,1280]{2,1,0:T(8,128)S(1)} %get-tuple-element.36.ranged, bf16[3,32,1280]{2,1,0:T(8,128)(2,1)S(1)} %get-tuple-element.37.codes, ...), custom_call_target="tpu_custom_call" | custom-call | flops 1000000 | bytes 4000000 | tf_op jit(solution)/shard_map/borders/pallas_call | solution.py:141
  17.8 2.9 %collective-permute-start.6 = (bf16[208,256]{1,0:T(8,128)(2,1)S(1)}, bf16[208,256]{1,0:T(8,128)(2,1)S(1)}, u32[]{:S(2)}, u32[]{:S(2)}) collective-permute-start(bf16[208,256]{1,0:T(8,128)(2,1)S(1)} %get-tuple-element.53), channel_id=1, source_target_pairs={{0,5},{1,4},{2,7},{3,6},{4,1},{5,0},{6,3},{7,2},{8,13},{9,12},{10,... | collective-permute-start | bytes 319496 | tf_op jit(solution)/shard_map/ppermute | solution.py:906
  20.6 1.7 %collective-permute-start.7 = (bf16[208,256]{1,0:T(8,128)(2,1)S(1)}, bf16[208,256]{1,0:T(8,128)(2,1)S(1)}, u32[]{:S(2)}, u32[]{:S(2)}) collective-permute-start(bf16[208,256]{1,0:T(8,128)(2,1)S(1)} %get-tuple-element.54), channel_id=1, source_target_pairs={{0,6},{1,7},{2,4},{3,5},{4,2},{5,3},{6,0},{7,1},{8,14},{9,15},{10,... | collective-permute-start | bytes 319496 | tf_op jit(solution)/shard_map/ppermute | solution.py:906
  22.3 3.1 %collective-permute-start.8 = (bf16[208,256]{1,0:T(8,128)(2,1)S(1)}, bf16[208,256]{1,0:T(8,128)(2,1)S(1)}, u32[]{:S(2)}, u32[]{:S(2)}) collective-permute-start(bf16[208,256]{1,0:T(8,128)(2,1)S(1)} %get-tuple-element.55), channel_id=1, source_target_pairs={{0,7},{1,6},{2,5},{3,4},{4,3},{5,2},{6,1},{7,0},{8,15},{9,14},{10,... | collective-permute-start | bytes 319496 | tf_op jit(solution)/shard_map/ppermute | solution.py:906
  25.4 5.3 %interior.3 = (f32[4,64,1280]{2,1,0:T(8,128)S(1)}, bf16[3,32,1280]{2,1,0:T(8,128)(2,1)S(1)}, f32[4,8,128]{2,1,0:T(8,128)S(1)}) custom-call(s32[6]{0:T(128)S(1)} %stack.23.ids, bf16[2,64,2048]{2,1,0:T(8,128)(2,1)S(1)} %copy-done.1, bf16[2,64,2048]{2,1,0:T(8,128)(2,1)S(1)} %copy-done.2), custom_call_target="tpu_custom_call" | custom-call | flops 8000000 | bytes 4000000 | tf_op jit(solution)/shard_map/interior/pallas_call | solution.py:154
  30.7 2.7 %borders.3 = (bf16[208,256]{1,0:T(8,128)(2,1)S(1)}, bf16[208,256]{1,0:T(8,128)(2,1)S(1)}, bf16[208,256]{1,0:T(8,128)(2,1)S(1)}, bf16[208,256]{1,0:T(8,128)(2,1)S(1)}) custom-call(s32[6]{0:T(128)S(1)} %stack.23.ids, f32[4,64,1280]{2,1,0:T(8,128)S(1)} %get-tuple-element.45.ranged, bf16[3,32,1280]{2,1,0:T(8,128)(2,1)S(1)} %get-tuple-element.46.codes, ...), custom_call_target="tpu_custom_call" | custom-call | flops 1000000 | bytes 4000000 | tf_op jit(solution)/shard_map/borders/pallas_call | solution.py:141
  33.5 0.6 collective-permute-start.2
  34.1 0.4 collective-permute-done.6.rest_5_
  34.4 2.6 %collective-permute-start.4 = (bf16[208,256]{1,0:T(8,128)(2,1)S(1)}, bf16[208,256]{1,0:T(8,128)(2,1)S(1)}, u32[]{:S(2)}, u32[]{:S(2)}) collective-permute-start(bf16[208,256]{1,0:T(8,128)(2,1)S(1)} %get-tuple-element.51), channel_id=1, source_target_pairs={{0,3},{1,2},{2,1},{3,0},{4,7},{5,6},{6,5},{7,4},{8,11},{9,10},{10,... | collective-permute-start | bytes 319496 | tf_op jit(solution)/shard_map/ppermute | solution.py:906
  37.0 2.2 %collective-permute-done.2.rest_1_ = bf16[208,256]{1,0:T(8,128)(2,1)S(1)} collective-permute-done((bf16[208,256]{1,0:T(8,128)(2,1)S(1)}, bf16[208,256]{1,0:T(8,128)(2,1)S(1)}, u32[]{:S(2)}, u32[]{:S(2)}) %collective-permute-start.2) | collective-permute-done | bytes 106528 | tf_op jit(solution)/shard_map/ppermute | solution.py:906
  39.3 2.0 %collective-permute-done.4.rest_3_ = bf16[208,256]{1,0:T(8,128)(2,1)S(1)} collective-permute-done((bf16[208,256]{1,0:T(8,128)(2,1)S(1)}, bf16[208,256]{1,0:T(8,128)(2,1)S(1)}, u32[]{:S(2)}, u32[]{:S(2)}) %collective-permute-start.4) | collective-permute-done | bytes 106528 | tf_op jit(solution)/shard_map/ppermute | solution.py:906
  41.3 4.5 %tiles.1 = (f32[512,256]{1,0:T(8,128)S(1)}, f32[512,256]{1,0:T(8,128)S(1)}, f32[512,256]{1,0:T(8,128)S(1)}, f32[512,128]{1,0:T(8,128)S(1)}, f32[520,256]{1,0:T(8...) custom-call(s32[6]{0:T(128)S(1)} %stack.23.ids, ...), custom_call_target="tpu_custom_call" | custom-call | flops 1000000 | bytes 4000000 | tf_op jit(solution)/shard_map/tiles/pallas_call | solution.py:141
  45.8 1.5 %collective-permute-start.10 = (f32[8,128]{1,0:T(8,128)S(1)}, f32[8,128]{1,0:T(8,128)S(1)}, u32[]{:S(2)}, u32[]{:S(2)}) collective-permute-start(f32[8,128]{1,0:T(8,128)S(1)} %get-tuple-element.62), channel_id=1, source_target_pairs={{0,24},{8,16},{16,8},{24,0},{1,25},{9,17},{17,9},{25,1},{2,26},{10... | collective-permute-start | bytes 12296 | tf_op jit(solution)/shard_map/ppermute | solution.py:850
  47.3 0.3 collective-permute-start.11
  47.6 2.8 %collective-permute-start.12 = (f32[8,128]{1,0:T(8,128)S(1)}, f32[8,128]{1,0:T(8,128)S(1)}, u32[]{:S(2)}, u32[]{:S(2)}) collective-permute-start(f32[8,128]{1,0:T(8,128)S(1)} %get-tuple-element.64), channel_id=1, source_target_pairs={{0,7},{1,2},{2,1},{3,4},{4,3},{5,6},{6,5},{7,0},{8,15},{9,10},{10,... | collective-permute-start | bytes 12296 | tf_op jit(solution)/shard_map/ppermute | solution.py:850
  50.5 0.5 collective-permute-done.11.col_pair
  50.9 3.0 %collective-permute-done.12.col_next = f32[8,128]{1,0:T(8,128)S(1)} collective-permute-done((f32[8,128]{1,0:T(8,128)S(1)}, f32[8,128]{1,0:T(8,128)S(1)}, u32[]{:S(2)}, u32[]{:S(2)}) %collective-permute-start.12) | collective-permute-done | bytes 4128 | tf_op jit(solution)/shard_map/ppermute | solution.py:850
  54.0 4.6 %operator.1 = (f32[512,256]{1,0:T(8,128)S(1)}, f32[512,256]{1,0:T(8,128)S(1)}, f32[512,256]{1,0:T(8,128)S(1)}, bf16[16,128]{1,0:T(8,128)(2,1)S(1)}, f32[16,128]{1,0:T(8,128)S(1)}) custom-call(s32[6]{0:T(128)S(1)} %stack.23.ids, f32[512,256]{1,0:T(8,128)S(1)} %get-tuple-element.56.residual, f32[512,256]{1,0:T(8,128)S(1)} %get-tuple-element.57.shaped, ...), custom_call_target="tpu_custom_call" | custom-call | flops 1000000 | bytes 4000000 | tf_op jit(solution)/shard_map/operator/pallas_call | solution.py:141
  58.5 10.7 %all_to_all.5.gathered = bf16[32,16,128]{2,1,0:T(8,128)(2,1)S(1)} all-to-all(bf16[32,16,128]{2,1,0:T(8,128)(2,1)S(1)} %broadcast_in_dim.2), channel_id=1, replica_groups=mesh['row'=4,'col'=8] {'row','col'}, dimensions={0} | all-to-all | bytes 262144 | tf_op jit(solution)/shard_map/all_to_all | solution.py:956
  69.3 2.3 %finish.1 = (f32[512,256]{1,0:T(8,128)}, f32[512,256]{1,0:T(8,128)}) custom-call(s32[6]{0:T(128)S(1)} %stack.23.ids, bf16[32,16,128]{2,1,0:T(8,128)(2,1)S(1)} %all_to_all.5.gathered, f32[512,256]{1,0:T(8,128)S(1)} %get-tuple-element.56.residual, f32[512,256]{1,0:T(8,128)S(1)} %get-tuple-element.57.shaped, f32[512,256]{1,0:T(8,128)S(1)} %get-tuple-element.66.operated, ...), custom_call_target="tpu_custom_call" | custom-call | flops 1000000 | bytes 4000000 | tf_op jit(solution)/shard_map/finish/pallas_call | solution.py:141
  (24 shorter events, 0.3 us)
Async XLA Ops:
  0.6 7.6 %copy-start.2 = (bf16[2,64,2048]{2,1,0:T(8,128)(2,1)S(1)}, bf16[2,64,2048]{2,1,0:T(8,128)(2,1)}, u32[]{:S(2)}) copy-start(bf16[2,64,2048]{2,1,0:T(8,128)(2,1)} %second.2) | copy-start | bytes 1572868
  0.6 7.6 %copy-start.1 = (bf16[2,64,2048]{2,1,0:T(8,128)(2,1)S(1)}, bf16[2,64,2048]{2,1,0:T(8,128)(2,1)}, u32[]{:S(2)}) copy-start(bf16[2,64,2048]{2,1,0:T(8,128)(2,1)} %first.2) | copy-start | bytes 1572868
  1.7 11.7 %collective-permute-start.1 = (bf16[4,8,2048]{2,1,0:T(8,128)(2,1)S(1)}, bf16[4,8,2048]{2,1,0:T(8,128)(2,1)S(1)}, u32[]{:S(2)}, u32[]{:S(2)}) collective-permute-start(bf16[4,8,2048]{2,1,0:T(8,128)(2,1)S(1)} %get-tuple-element.74), channel_id=1, source_target_pairs={{0,31},{1,2},{2,1},{3,4},{4,3},{5,6},{6,5},{7,8},{8,7},{9,10},{10,... | collective-permute-start | bytes 393224 | tf_op jit(solution)/shard_map/ppermute | solution.py:850
  8.2 6.8 %collective-permute-start = (bf16[4,8,2048]{2,1,0:T(8,128)(2,1)S(1)}, bf16[4,8,2048]{2,1,0:T(8,128)(2,1)S(1)}, u32[]{:S(2)}, u32[]{:S(2)}) collective-permute-start(bf16[4,8,2048]{2,1,0:T(8,128)(2,1)S(1)} %get-tuple-element.75), channel_id=1, source_target_pairs={{0,1},{1,0},{2,3},{3,2},{4,5},{5,4},{6,7},{7,6},{8,9},{9,8},{10,11... | collective-permute-start | bytes 393224 | tf_op jit(solution)/shard_map/ppermute | solution.py:850
  15.0 26.3 %copy-start.4 = (bf16[1024,256]{1,0:T(8,128)(2,1)S(1)}, bf16[1024,256]{1,0:T(8,128)(2,1)}, u32[]{:S(2)}) copy-start(bf16[1024,256]{1,0:T(8,128)(2,1)} %constant.39.clone.rest_9_.rest_1_) | copy-start | bytes 1572868
  17.7 23.6 %copy-start = (bf16[2048,512]{1,0:T(8,128)(2,1)S(1)}, bf16[2048,512]{1,0:T(8,128)(2,1)}, u32[]{:S(2)}) copy-start(bf16[2048,512]{1,0:T(8,128)(2,1)} %constant.38.clone.rest_8_.rest_0_) | copy-start | bytes 6291460
  17.7 23.6 %copy-start.3 = (f32[512,256]{1,0:T(8,128)S(1)}, f32[512,256]{1,0:T(8,128)}, u32[]{:S(2)}) copy-start(f32[512,256]{1,0:T(8,128)} %constant.40.clone.rest_10_.rest_2_) | copy-start | bytes 1572868
  17.7 16.4 %collective-permute-start.5 = (bf16[208,256]{1,0:T(8,128)(2,1)S(1)}, bf16[208,256]{1,0:T(8,128)(2,1)S(1)}, u32[]{:S(2)}, u32[]{:S(2)}) collective-permute-start(bf16[208,256]{1,0:T(8,128)(2,1)S(1)} %get-tuple-element.52), channel_id=1, source_target_pairs={{0,4},{1,5},{2,6},{3,7},{4,0},{5,1},{6,2},{7,3},{8,12},{9,13},{10,... | collective-permute-start | bytes 319496 | tf_op jit(solution)/shard_map/ppermute | solution.py:906
  17.8 16.7 %collective-permute-start.6 = (bf16[208,256]{1,0:T(8,128)(2,1)S(1)}, bf16[208,256]{1,0:T(8,128)(2,1)S(1)}, u32[]{:S(2)}, u32[]{:S(2)}) collective-permute-start(bf16[208,256]{1,0:T(8,128)(2,1)S(1)} %get-tuple-element.53), channel_id=1, source_target_pairs={{0,5},{1,4},{2,7},{3,6},{4,1},{5,0},{6,3},{7,2},{8,13},{9,12},{10,... | collective-permute-start | bytes 319496 | tf_op jit(solution)/shard_map/ppermute | solution.py:906
  20.6 16.4 %collective-permute-start.7 = (bf16[208,256]{1,0:T(8,128)(2,1)S(1)}, bf16[208,256]{1,0:T(8,128)(2,1)S(1)}, u32[]{:S(2)}, u32[]{:S(2)}) collective-permute-start(bf16[208,256]{1,0:T(8,128)(2,1)S(1)} %get-tuple-element.54), channel_id=1, source_target_pairs={{0,6},{1,7},{2,4},{3,5},{4,2},{5,3},{6,0},{7,1},{8,14},{9,15},{10,... | collective-permute-start | bytes 319496 | tf_op jit(solution)/shard_map/ppermute | solution.py:906
  22.3 14.7 %collective-permute-start.8 = (bf16[208,256]{1,0:T(8,128)(2,1)S(1)}, bf16[208,256]{1,0:T(8,128)(2,1)S(1)}, u32[]{:S(2)}, u32[]{:S(2)}) collective-permute-start(bf16[208,256]{1,0:T(8,128)(2,1)S(1)} %get-tuple-element.55), channel_id=1, source_target_pairs={{0,7},{1,6},{2,5},{3,4},{4,3},{5,2},{6,1},{7,0},{8,15},{9,14},{10,... | collective-permute-start | bytes 319496 | tf_op jit(solution)/shard_map/ppermute | solution.py:906
  33.5 5.8 %collective-permute-start.2 = (bf16[208,256]{1,0:T(8,128)(2,1)S(1)}, bf16[208,256]{1,0:T(8,128)(2,1)S(1)}, u32[]{:S(2)}, u32[]{:S(2)}) collective-permute-start(bf16[208,256]{1,0:T(8,128)(2,1)S(1)} %get-tuple-element.49), channel_id=1, source_target_pairs={{0,1},{1,0},{2,3},{3,2},{4,5},{5,4},{6,7},{7,6},{8,9},{9,8},{10,11... | collective-permute-start | bytes 319496 | tf_op jit(solution)/shard_map/ppermute | solution.py:906
  34.1 5.2 %collective-permute-start.3 = (bf16[208,256]{1,0:T(8,128)(2,1)S(1)}, bf16[208,256]{1,0:T(8,128)(2,1)S(1)}, u32[]{:S(2)}, u32[]{:S(2)}) collective-permute-start(bf16[208,256]{1,0:T(8,128)(2,1)S(1)} %get-tuple-element.50), channel_id=1, source_target_pairs={{0,2},{1,3},{2,0},{3,1},{4,6},{5,7},{6,4},{7,5},{8,10},{9,11},{10,... | collective-permute-start | bytes 319496 | tf_op jit(solution)/shard_map/ppermute | solution.py:906
  34.4 6.8 %collective-permute-start.4 = (bf16[208,256]{1,0:T(8,128)(2,1)S(1)}, bf16[208,256]{1,0:T(8,128)(2,1)S(1)}, u32[]{:S(2)}, u32[]{:S(2)}) collective-permute-start(bf16[208,256]{1,0:T(8,128)(2,1)S(1)} %get-tuple-element.51), channel_id=1, source_target_pairs={{0,3},{1,2},{2,1},{3,0},{4,7},{5,6},{6,5},{7,4},{8,11},{9,10},{10,... | collective-permute-start | bytes 319496 | tf_op jit(solution)/shard_map/ppermute | solution.py:906
  45.8 4.7 %collective-permute-start.9 = (f32[8,128]{1,0:T(8,128)S(1)}, f32[8,128]{1,0:T(8,128)S(1)}, u32[]{:S(2)}, u32[]{:S(2)}) collective-permute-start(f32[8,128]{1,0:T(8,128)S(1)} %get-tuple-element.61), channel_id=1, source_target_pairs={{0,8},{8,0},{16,24},{24,16},{1,9},{9,1},{17,25},{25,17},{2,10},{10... | collective-permute-start | bytes 12296 | tf_op jit(solution)/shard_map/ppermute | solution.py:850
  45.8 4.6 %collective-permute-start.10 = (f32[8,128]{1,0:T(8,128)S(1)}, f32[8,128]{1,0:T(8,128)S(1)}, u32[]{:S(2)}, u32[]{:S(2)}) collective-permute-start(f32[8,128]{1,0:T(8,128)S(1)} %get-tuple-element.62), channel_id=1, source_target_pairs={{0,24},{8,16},{16,8},{24,0},{1,25},{9,17},{17,9},{25,1},{2,26},{10... | collective-permute-start | bytes 12296 | tf_op jit(solution)/shard_map/ppermute | solution.py:850
  47.3 3.6 %collective-permute-start.11 = (f32[8,128]{1,0:T(8,128)S(1)}, f32[8,128]{1,0:T(8,128)S(1)}, u32[]{:S(2)}, u32[]{:S(2)}) collective-permute-start(f32[8,128]{1,0:T(8,128)S(1)} %get-tuple-element.63), channel_id=1, source_target_pairs={{0,1},{1,0},{2,3},{3,2},{4,5},{5,4},{6,7},{7,6},{8,9},{9,8},{10,11... | collective-permute-start | bytes 12296 | tf_op jit(solution)/shard_map/ppermute | solution.py:850
  47.6 6.3 %collective-permute-start.12 = (f32[8,128]{1,0:T(8,128)S(1)}, f32[8,128]{1,0:T(8,128)S(1)}, u32[]{:S(2)}, u32[]{:S(2)}) collective-permute-start(f32[8,128]{1,0:T(8,128)S(1)} %get-tuple-element.64), channel_id=1, source_target_pairs={{0,7},{1,2},{2,1},{3,4},{4,3},{5,6},{6,5},{7,0},{8,15},{9,10},{10,... | collective-permute-start | bytes 12296 | tf_op jit(solution)/shard_map/ppermute | solution.py:850

commit v3 on v2

--- a/solution.py
+++ b/solution.py
@@ -113,10 +113,7 @@
 
 
 def decode_power(code, scale):
-    share = jnp.abs(code)
-    for _ in range(4):
-        share = jnp.sqrt(share)
-    share = share * (scale * (1.0 / POWER_BASE))
+    share = jnp.exp2(jnp.log2(jnp.abs(code)) * (1.0 / 16.0)) * (scale * (1.0 / POWER_BASE))
     return jnp.where(code < 0.0, -share, share)
 
 
@@ -154,7 +151,8 @@
     return pl.pallas_call(
         body,
         out_shape=[jax.ShapeDtypeStruct(s, d) for s, d in outs],
-        in_specs=[pl.BlockSpec(memory_space=pltpu.SMEM)] + [pl.BlockSpec(memory_space=pltpu.HBM)] * 2,
+        in_specs=[pl.BlockSpec(memory_space=pltpu.SMEM)] + [pl.BlockSpec(memory_space=pltpu.HBM)] * 2
+        + [pl.BlockSpec(memory_space=pltpu.VMEM)],
         out_specs=[pl.BlockSpec(memory_space=pltpu.VMEM)] * len(outs),
         scratch_shapes=scratch,
         compiler_params=pltpu.CompilerParams(vmem_limit_bytes=VMEM_LIMIT),
@@ -217,10 +215,22 @@
     return first_tile, start, span, jnp.logical_and(pixel >= 0, pixel < width)
 
 
-def interior_kernel(lines, width, tile, columns, across, ids, first, second, ranged, codes, rims, raw, prod, field, sems):
+def range_table(tile_pair, out):
+    k = taps()
+    margin = (tile_pair - out) // 2
+    table = np.zeros((tile_pair, out))
+    for n in range(out):
+        for j in range(-RADIUS, RADIUS + 1):
+            table[n + margin + j, n] = k[abs(j)]
+    return table
+
+
+def interior_kernel(
+    lines, width, tile, columns, across, ids, first, second, table, ranged, field, codes, rims, raw, high, low, sems
+):
     half = columns // 2
     chunk = 16
-    first_tile, start, span, in_image = window(lines, width, tile, columns, across, ids[1], 8)
+    first_tile, start, span, _ = window(lines, width, tile, columns, across, ids[1], 8)
     upper = jnp.where(first_tile == 0, 0, 1)
     source = pl.multiple_of(upper * (width // 2 - 2 * LANES), LANES)
     target = pl.multiple_of((1 - upper) * 2 * LANES, LANES)
@@ -242,29 +252,37 @@
         copies[2 * i].wait()
         copies[2 * i + 1].wait()
         rs = slice(i * chunk, (i + 1) * chunk)
-        for c in range(0, span + 2 * LANES, 512):
-            cs = slice(c, c + 512)
+        for c in range(0, span + 2 * LANES, 2 * LANES):
+            cs = slice(c, c + 2 * LANES)
             values = products(raw[0, 0, rs, cs], raw[0, 1, rs, cs], raw[1, 0, rs, cs], raw[1, 1, rs, cs])
             for f in range(4):
-                prod[f, :, cs] = values[f]
+                row = f * lines + i * chunk
+                high[row : row + chunk, cs], low[row : row + chunk, cs] = split(values[f])
+    block = 2 * LANES
+    weights = table[0 : 2 * block, :], table[2 * block :, :]
+    for c in range(0, span, block):
+        cs = slice(c, c + 2 * block)
+        total = dot3((high[:, cs], low[:, cs]), weights)
+        if c == 0 or c + block == span:
+            pixel = lanes_of(total.shape) + (start - LANES + c)
+            total = jnp.where(jnp.logical_and(pixel >= 0, pixel < width), total, 0.0)
         for f in range(4):
-            for r in range(0, chunk, 8):
-                total = along_range(prod[f, r : r + 8, :])[:, LANES : LANES + span]
-                row = i * chunk + r
-                ranged[f, row : row + 8, :] = jnp.where(in_image, total, 0.0)
-    inner = lines - 2 * EDGE
+            ranged[f, :, c : c + block] = total[f * lines : (f + 1) * lines, :]
     for c in range(0, span, LANES):
         cs = slice(c, c + LANES)
-        for r in range(0, inner, 16):
-            smoothed = [along_azimuth(ranged, f, EDGE + r, 16, cs) for f in range(4)]
+        steps = [(HALO, HALO)] + [(r, 16) for r in range(EDGE, lines - EDGE, 16)] + [(lines - EDGE, HALO)]
+        for r, rows in steps:
+            smoothed = [along_azimuth(ranged, f, r, rows, cs) for f in range(4)]
             phase, gain = phase_gain(smoothed)
-            field[0, r : r + 16, cs] = phase
-            field[1, r : r + 16, cs] = gain
-            codes[0, r : r + 16, cs], codes[1, r : r + 16, cs] = split(phase)
-            codes[2, r : r + 16, cs] = encode_gain(gain)
+            field[0, r - HALO : r - HALO + rows, cs] = phase
+            field[1, r - HALO : r - HALO + rows, cs] = gain
+            if rows == 16:
+                at = slice(r - EDGE, r - EDGE + rows)
+                codes[0, at, cs], codes[1, at, cs] = split(phase)
+                codes[2, at, cs] = encode_gain(gain)
     groups = lines // 8
     for t in range(half):
-        rims[t] = rim_block(field, groups, range(EDGE // 8, (lines - EDGE) // 8), EDGE // 8, t * tile, tile, None)
+        rims[t] = rim_block(field, groups, range(1, groups - 1), 1, t * tile, tile, None)
 
 
 def rim_block(field, groups, which, first_group, start, tile, block, hint=None):
@@ -286,7 +304,7 @@
     return block
 
 
-def border_kernel(lines, width, tile, columns, across, ids, ranged, codes, rims, from_pair, from_next, *rest):
+def border_kernel(lines, width, tile, columns, across, ids, ranged, inside_field, codes, rims, from_pair, from_next, *rest):
     half = columns // 2
     outs, (prod, seg, field, ends) = rest[:half], rest[half:]
     own = ids[1]
@@ -297,7 +315,7 @@
         jnp.where(ids[2] == ids[3] - 1, 0.0, 1.0).astype(jnp.float32),
     )
     zero = jnp.zeros((HALO, 2 * LANES), jnp.float32)
-    own_rows = EDGE + HALO
+    own_rows = 2 * HALO
     for e in range(2):
         flag = odd if e == 0 else 1 - odd
         keep = flag.astype(jnp.float32)
@@ -326,10 +344,10 @@
         ref = seg.at[e]
         for c in range(0, span, LANES):
             cs = slice(c, c + LANES)
-            smoothed = [along_azimuth(ref, f, HALO, EDGE, cs) for f in range(4)]
+            smoothed = [along_azimuth(ref, f, HALO, HALO, cs) for f in range(4)]
             phase, gain = phase_gain(smoothed)
-            field[0, e * EDGE : (e + 1) * EDGE, cs] = phase
-            field[1, e * EDGE : (e + 1) * EDGE, cs] = gain
+            field[0, e * HALO : (e + 1) * HALO, cs] = phase
+            field[1, e * HALO : (e + 1) * HALO, cs] = gain
         low, high = end_weights(e == 0)
         r = 0 if e == 0 else own_rows - HALO
         smoothed = [
@@ -340,7 +358,6 @@
         ends[e : e + 1, :] = phase
         ends[2 + e : 3 + e, :] = gain * inside[e]
     groups = lines // 8
-    edge_groups = EDGE // 8
     inner = lines - 2 * EDGE
     for n, s in enumerate(range(half, columns) if across else range(half)):
         out = outs[n]
@@ -351,15 +368,15 @@
             out[i * lines + EDGE : i * lines + EDGE + inner, :] = codes[i, :, cs]
         for e in range(2):
             row = 0 if e == 0 else lines - EDGE
-            rs = slice(e * EDGE, (e + 1) * EDGE)
-            out[row : row + EDGE, :], out[lines + row : lines + row + EDGE, :] = split(field[0, rs, cs])
-            out[2 * lines + row : 2 * lines + row + EDGE, :] = encode_gain(field[1, rs, cs])
+            rs = slice(e * HALO, (e + 1) * HALO)
+            inner_rows = slice(0, HALO) if e == 0 else slice(lines - 3 * HALO, lines - 2 * HALO)
+            pairs = [(field[i, rs, cs], inside_field[i, inner_rows, cs]) for i in range(2)]
+            phase, gain = (jnp.concatenate(p if e == 0 else p[::-1], axis=0) for p in pairs)
+            out[row : row + EDGE, :], out[lines + row : lines + row + EDGE, :] = split(phase)
+            out[2 * lines + row : 2 * lines + row + EDGE, :] = encode_gain(gain)
         block = rims[target - first_tile]
-        block = rim_block(field, groups, range(edge_groups), 0, local, tile, block, pl.multiple_of)
-        block = rim_block(
-            field, groups, range(groups - edge_groups, groups), groups - 2 * edge_groups, local, tile, block,
-            pl.multiple_of,
-        )
+        block = rim_block(field, groups, (0,), 0, local, tile, block, pl.multiple_of)
+        block = rim_block(field, groups, (groups - 1,), groups - 2, local, tile, block, pl.multiple_of)
         rows = []
         for i in range(4):
             for h in range(tile // LANES):
@@ -561,25 +578,13 @@
     return (x - shifted_left(x, rim_x[rs, :])) + along_y[rs, :] - along_y[r + 1 : r + 1 + step, :]
 
 
-def tile_kernel(lines, tile_az, tile, columns, exchange, ids, *rest):
-    chunks = rest[: columns if exchange == "permute" else 1]
-    rest = rest[len(chunks) :]
-    tables, inverse = rest[:2], rest[2]
-    residual, shaped, weight_x, rim_x, weight_y, row_pair, row_next, col_pair, col_next = rest[3:12]
-    phase, gain, sides, ends, flux_x, flux_rim, flux_y = rest[12:]
-    own = ids[1]
-    pairs = table_pairs(tables)
-
-    for s in range(columns):
-        if exchange == "permute":
-            src, strip = chunks[s], own ^ s
-        else:
-            src, strip = chunks[0].at[s], s
-        row = strip * lines
-        if exchange == "permute":
-            row = pl.multiple_of(row, 8)
-        at = pl.ds(pl.multiple_of(strip * 8, 8), 8) if exchange == "permute" else pl.ds(strip * 8, 8)
-        if exchange == "permute":
+def edges_of(lines, count, tile, coded, sources, scratch, outs):
+    phase, gain, sides, ends = scratch
+    weight_x, flux_x, rim_x, flux_rim, weight_y, flux_y, weight_end, flux_end = outs
+    height = count * lines
+    for src, strip in sources:
+        if coded:
+            row, at = pl.multiple_of(strip * lines, 8), pl.ds(pl.multiple_of(strip * 8, 8), 8)
             phase[pl.ds(HALO + row, lines), :] = src[0:lines, :].astype(jnp.float32) + src[
                 lines : 2 * lines, :
             ].astype(jnp.float32)
@@ -587,22 +592,23 @@
             both = src[3 * lines :, :].astype(jnp.float32)
             block = both[0:8, :] + both[8:16, :]
         else:
+            row, at = strip * lines, pl.ds(strip * 8, 8)
             phase[pl.ds(HALO + row, lines), :] = src[0:lines, :]
             gain[pl.ds(HALO + row, lines), :] = src[lines : 2 * lines, :]
             block = src[2 * lines : 2 * lines + 8, :]
         sides[at, :] = block[:, 0:LANES]
         ends[at, :] = block[:, LANES : 2 * LANES]
-    last = 8 * (columns - 1)
+    last = 8 * (count - 1)
     for h in range(tile // LANES):
         cs = slice(h * LANES, (h + 1) * LANES)
         phase[HALO - 1 : HALO, cs] = ends[h : h + 1, :]
         gain[HALO - 1 : HALO, cs] = ends[4 + h : 5 + h, :]
-        phase[HALO + tile_az : HALO + tile_az + 1, cs] = ends[last + 2 + h : last + 3 + h, :]
-        gain[HALO + tile_az : HALO + tile_az + 1, cs] = ends[last + 6 + h : last + 7 + h, :]
-
-    step = min(tile_az, 32)
+        phase[HALO + height : HALO + height + 1, cs] = ends[last + 2 + h : last + 3 + h, :]
+        gain[HALO + height : HALO + height + 1, cs] = ends[last + 6 + h : last + 7 + h, :]
+
+    step = min(height, 32)
     groups = lines // 8
-    for r in range(0, tile_az, step):
+    for r in range(0, height, step):
         rs = slice(r, r + step)
         b = HALO + r
         p, g = phase[b : b + step, :], gain[b : b + step, :]
@@ -617,22 +623,58 @@
                     shift = ((0 if side == 0 else LANES - 1) - source_lane) % LANES
                     parts.append(pltpu.roll(block, shift, 1) if shift else block)
                 halo.append(jnp.concatenate(parts, axis=0) if len(parts) > 1 else parts[0])
-        w, f = edge(shifted_right(p, halo[0]), shifted_right(g, halo[2]), p, g)
-        weight_x[rs, :] = w
-        flux_x[rs, :] = f
-        w, f = edge(p[:, tile - LANES :], g[:, tile - LANES :], halo[1], halo[3])
-        rim_x[rs, :] = w
-        flux_rim[rs, :] = f
-        w, f = edge(phase[b - 1 : b - 1 + step, :], gain[b - 1 : b - 1 + step, :], p, g)
-        weight_y[rs, :] = w
-        flux_y[rs, :] = f
-    b = HALO + tile_az
-    w, f = edge(
-        phase[b - 1 : b, :], gain[b - 1 : b, :], phase[b : b + 1, :], gain[b : b + 1, :]
+        weight_x[rs, :], flux_x[rs, :] = edge(shifted_right(p, halo[0]), shifted_right(g, halo[2]), p, g)
+        rim_x[rs, :], flux_rim[rs, :] = edge(p[:, tile - LANES :], g[:, tile - LANES :], halo[1], halo[3])
+        weight_y[rs, :], flux_y[rs, :] = edge(phase[b - 1 : b - 1 + step, :], gain[b - 1 : b - 1 + step, :], p, g)
+    b = HALO + height
+    w, f = edge(phase[b - 1 : b, :], gain[b - 1 : b, :], phase[b : b + 1, :], gain[b : b + 1, :])
+    weight_end[...] = jnp.broadcast_to(w, (8, tile))
+    flux_end[...] = jnp.broadcast_to(f, (8, tile))
+
+
+def far_kernel(lines, tile, columns, ids, *rest):
+    half = columns // 2
+    own = ids[1]
+    sources = [(rest[n], (own ^ n) & (half - 1)) for n in range(half)]
+    edges_of(lines, half, tile, True, sources, rest[half + 8 :], rest[half : half + 8])
+
+
+def tile_kernel(lines, tile_az, tile, columns, exchange, ids, *rest):
+    coded = exchange == "permute"
+    half = columns // 2
+    own = ids[1]
+    count = half if coded else columns
+    if coded:
+        sources = [(rest[s], (own ^ s) & (half - 1)) for s in range(half)]
+        far, rest = rest[half : half + 8], rest[half + 8 :]
+    else:
+        sources = [(rest[0].at[s], s) for s in range(columns)]
+        rest = rest[1:]
+    tables, inverse = rest[:2], rest[2]
+    residual, shaped, weight_x, rim_x, weight_y, row_pair, row_next, col_pair, col_next = rest[3:12]
+    phase, gain, sides, ends, flux_x, flux_rim, flux_y, weight_end, flux_end = rest[12:]
+    pairs = table_pairs(tables)
+    height = count * lines
+    whole = (weight_x, flux_x, rim_x, flux_rim, weight_y, flux_y)
+    if coded:
+        lower = (own & half) // half
+        at = pl.ds(pl.multiple_of(lower * height, 8), height)
+        outs = [ref.at[at, :] for ref in whole]
+    else:
+        outs = [ref.at[pl.ds(0, height), :] for ref in whole]
+    edges_of(
+        lines, count, tile, coded, sources, (phase, gain, sides, ends), (*outs, weight_end, flux_end)
     )
-    weight_y[tile_az : tile_az + 8, :] = jnp.broadcast_to(w, (8, tile))
-    flux_y[tile_az : tile_az + 8, :] = jnp.broadcast_to(f, (8, tile))
-
+    w, f = weight_end[...], flux_end[...]
+    if coded:
+        at = pl.ds(pl.multiple_of((1 - lower) * height, 8), height)
+        for source, ref in zip(far, whole):
+            ref[at, :] = source[...]
+        w, f = jnp.where(lower == 1, w, far[6][...]), jnp.where(lower == 1, f, far[7][...])
+    weight_y[tile_az : tile_az + 8, :] = w
+    flux_y[tile_az : tile_az + 8, :] = f
+
+    step = min(tile_az, 32)
     for r in range(0, tile_az, step):
         residual[r : r + step, :] = TURN * divergence(tile_az, step, flux_x, flux_rim, flux_y, r)
     shaped[...] = precondition(residual[...], pairs, inverse)
@@ -869,28 +911,34 @@
     if exchange == "permute":
         half = columns // 2
         span = half * tile + 2 * LANES
+        smoothing = jnp.asarray(np.concatenate(two_parts(range_table(4 * LANES, 2 * LANES)), axis=0))
         sent = [None] * columns
         sources = (first_slc, second_slc)
         for across in (True, False):
-            ranged, codes, rims = interior(
+            ranged, inner, codes, rims = interior(
                 functools.partial(interior_kernel, lines, width, tile, columns, across),
-                [((4, lines, span), f32), ((3, lines - 2 * EDGE, span), bf16), ((half, 8, LANES), f32)],
-                (ids, *sources),
+                [
+                    ((4, lines, span), f32),
+                    ((2, lines - 2 * HALO, span), f32),
+                    ((3, lines - 2 * EDGE, span), bf16),
+                    ((half, 8, LANES), f32),
+                ],
+                (ids, *sources, smoothing),
                 [
                     pltpu.VMEM((2, 2, lines, span + 2 * LANES), bf16),
-                    pltpu.VMEM((4, 16, span + 2 * LANES), f32),
-                    pltpu.VMEM((2, lines - 2 * EDGE, span), f32),
+                    pltpu.VMEM((4 * lines, span + 2 * LANES), bf16),
+                    pltpu.VMEM((4 * lines, span + 2 * LANES), bf16),
                     pltpu.SemaphoreType.DMA((lines // 8,)),
                 ],
             )
             part = call(
                 functools.partial(border_kernel, lines, width, tile, columns, across),
                 [((3 * lines + 16, tile), bf16)] * half,
-                (ids, ranged, codes, rims, from_pair, from_next),
+                (ids, ranged, inner, codes, rims, from_pair, from_next),
                 [
                     pltpu.VMEM((4, HALO, width + 4 * LANES), f32),
-                    pltpu.VMEM((2, 4, EDGE + 2 * HALO, span), f32),
-                    pltpu.VMEM((2, 2 * EDGE, span), f32),
+                    pltpu.VMEM((2, 4, 3 * HALO, span), f32),
+                    pltpu.VMEM((2, 2 * HALO, span), f32),
                     pltpu.VMEM((8, span), f32),
                 ],
                 "borders",
@@ -932,11 +980,39 @@
         pltpu.VMEM((tile_az, LANES), f32),
         pltpu.VMEM((tile_az + 8, tile), f32),
     ]
+    edge_rows = tile_az
+    if exchange == "permute":
+        edge_rows = half * lines
+        part = ((edge_rows, tile), f32)
+        side = ((edge_rows, LANES), f32)
+        last = ((8, tile), f32)
+        far = call(
+            functools.partial(far_kernel, lines, tile, columns),
+            [part, part, side, side, part, part, last, last],
+            (ids, *arrived[half:]),
+            [
+                pltpu.VMEM((edge_rows + 2 * HALO, tile), f32),
+                pltpu.VMEM((edge_rows + 2 * HALO, tile), f32),
+                pltpu.VMEM((8 * half, LANES), f32),
+                pltpu.VMEM((8 * half, LANES), f32),
+            ],
+            "far",
+        )
+        arrived = [*arrived[:half], *far]
+    gathered_lines = pltpu.VMEM((edge_rows + 2 * HALO, tile), f32)
     residual, shaped, weight_x, rim_x, weight_y, row_pair, row_next, col_pair, col_next = call(
         functools.partial(tile_kernel, lines, tile_az, tile, columns, exchange),
         [whole, whole, whole, ((tile_az, LANES), f32), ((tile_az + 8, tile), f32), block, block, block, block],
         (ids, *arrived, *tables, inverse),
-        [padded, padded, pltpu.VMEM((8 * columns, LANES), f32), pltpu.VMEM((8 * columns, LANES), f32), *fluxes],
+        [
+            gathered_lines,
+            gathered_lines,
+            pltpu.VMEM((8 * columns, LANES), f32),
+            pltpu.VMEM((8 * columns, LANES), f32),
+            *fluxes,
+            pltpu.VMEM((8, tile), f32),
+            pltpu.VMEM((8, tile), f32),
+        ],
         "tiles",
     )
     rims = (

time: 71.9 us -> 70.5 us (0.981)
  Pallas kernels: 27.2 us -> 24.8 us
  starting transfers between devices: 22 us -> 20.8 us
  local copies, waits for them, and re-layouts: 1.17 us -> 2.21 us
  waiting for transfers between devices: 9.66 us -> 10.6 us
    pallas_call x2, Pallas kernels: 10.5 us -> 8.42 us  [interior(): pl.pallas_call(body, out_shape=[jax.ShapeDtypeStruct(s, d) for s, d in ou...]
    ppermute x7, starting transfers between devices: 10.9 us -> 9.38 us  [shards(): lax.ppermute(sent[s], 'col', [(i, i ^ s) for i in range(columns)])]
    unnamed x10 -> x14, local copies, waits for them, and re-layouts: 0.03 us -> 1.07 us
    ppermute x7, waiting for transfers between devices: 4.64 us -> 5.66 us  [shards(): lax.ppermute(sent[s], 'col', [(i, i ^ s) for i in range(columns)])]
    pallas_call x5 -> x6, Pallas kernels: 16.8 us -> 16.4 us  [call(): pl.pallas_call(body, out_shape=[jax.ShapeDtypeStruct(s, d) for s, d in ou...]
  transfers between devices with their start and end apart: 13 -> 13, of which waited for: 6 -> 6; matrix products, arithmetic and copies ran while one was open for 0% -> 0% of each run, Pallas kernels for 18% -> 17%
where the time goes in v3:
time: 70.5 us; the launch traced here: 70.3 us
  Pallas kernels  24.8 us (35%)
  starting transfers between devices  20.8 us (30%)
  blocking collectives  10.9 us (15%)
  waiting for transfers between devices  10.6 us (15%)
  local copies, waits for them, and re-layouts  2.21 us (3%)
  between operations  0.95 us (1%)
    pallas_call x6, Pallas kernels, call(): pl.pallas_call(body, out_shape=[jax.ShapeDtypeStruct(s, d) for s, d in ou...  16.4 us
    ppermute x6, starting transfers between devices, swapped(): return lax.ppermute(value, axis, pairs)  11.4 us
    all_to_all x1, blocking collectives, shards(): gathered = lax.all_to_all(spread, axes, 0, 0, tiled=True)  10.9 us
    ppermute x7, starting transfers between devices, shards(): lax.ppermute(sent[s], 'col', [(i, i ^ s) for i in range(columns)])  9.38 us
    pallas_call x2, Pallas kernels, interior(): pl.pallas_call(body, out_shape=[jax.ShapeDtypeStruct(s, d) for s, d in ou...  8.42 us
    ppermute x7, waiting for transfers between devices, shards(): lax.ppermute(sent[s], 'col', [(i, i ^ s) for i in range(columns)])  5.66 us
    ppermute x6, waiting for transfers between devices, swapped(): return lax.ppermute(value, axis, pairs)  4.92 us
  transfers between devices with their start and end apart: 13, of which 6 were waited for; matrix products, arithmetic and copies ran while one was open for 0% of the time, Pallas kernels for 17%

profile of v3, /device:TPU:0, one launch (start us, length us, event | category | flops | bytes accessed | tf_op | source)
XLA Modules:
  0.0 70.3 jit_solution(4800317878032852211)
XLA Ops:
  0.7 1.0 %fusion = (bf16[2,8,2048]{2,1,0:T(8,128)(2,1)S(1)}, bf16[2,8,2048]{2,1,0:T(8,128)(2,1)S(1)}, bf16[2,8,2048]{2,1,0:T(8,128)(2,1)S(1)}, bf16[2,8,2048]{2,1,0:T(8,128)(2,1)S(1)}) fusion(bf16[2,64,2048]{2,1,0:T(8,128)(2,1)} %first.2, bf16[2,64,2048]{2,1,0:T(8,128)(2,1)} %second.2), kind=kLoop, calls=%fused_computation.4 | loop fusion | bytes 524288 | tf_op jit(solution)/shard_map/slice | solution.py:905
  1.7 6.4 %collective-permute-start.1 = (bf16[4,8,2048]{2,1,0:T(8,128)(2,1)S(1)}, bf16[4,8,2048]{2,1,0:T(8,128)(2,1)S(1)}, u32[]{:S(2)}, u32[]{:S(2)}) collective-permute-start(bf16[4,8,2048]{2,1,0:T(8,128)(2,1)S(1)} %get-tuple-element.94), channel_id=1, source_target_pairs={{0,31},{1,2},{2,1},{3,4},{4,3},{5,6},{6,5},{7,8},{8,7},{9,10},{10,... | collective-permute-start | bytes 393224 | tf_op jit(solution)/shard_map/ppermute | solution.py:892
  8.3 1.0 %copy-done.3 = bf16[1024,256]{1,0:T(8,128)(2,1)S(1)} copy-done((bf16[1024,256]{1,0:T(8,128)(2,1)S(1)}, bf16[1024,256]{1,0:T(8,128)(2,1)}, u32[]{:S(2)}) %copy-start.3) | copy-done | bytes 524312
  9.3 4.1 %interior.2 = (f32[4,64,1280]{2,1,0:T(8,128)S(1)}, f32[2,48,1280]{2,1,0:T(8,128)S(1)}, bf16[3,32,1280]{2,1,0:T(8,128)(2,1)S(1)}, f32[4,8,128]{2,1,0:T(8,128)S(1)}) custom-call(s32[6]{0:T(128)S(1)} %stack.23.ids, bf16[2,64,2048]{2,1,0:T(8,128)(2,1)S(1)} %copy-done.1, bf16[2,64,2048]{2,1,0:T(8,128)(2,1)S(1)} %copy-done.2, bf16[1024,256]{1,0:T(8,128)(2,1)S(1)} %copy-done.3), custom_call_target="tpu_custom_call" | custom-call | flops 8000000 | bytes 4000000 | tf_op jit(solution)/shard_map/interior/pallas_call | solution.py:151
  13.5 1.5 %collective-permute-done.from_pair = bf16[4,8,2048]{2,1,0:T(8,128)(2,1)S(1)} collective-permute-done((bf16[4,8,2048]{2,1,0:T(8,128)(2,1)S(1)}, bf16[4,8,2048]{2,1,0:T(8,128)(2,1)S(1)}, u32[]{:S(2)}, u32[]{:S(2)}) %collective-permute-start) | collective-permute-done | bytes 131104 | tf_op jit(solution)/shard_map/ppermute | solution.py:892
  15.0 2.2 %borders.2 = (bf16[208,256]{1,0:T(8,128)(2,1)S(1)}, bf16[208,256]{1,0:T(8,128)(2,1)S(1)}, bf16[208,256]{1,0:T(8,128)(2,1)S(1)}, bf16[208,256]{1,0:T(8,128)(2,1)S(1)}) custom-call(s32[6]{0:T(128)S(1)} %stack.23.ids, f32[4,64,1280]{2,1,0:T(8,128)S(1)} %get-tuple-element.46.ranged, f32[2,48,1280]{2,1,0:T(8,128)S(1)} %get-tuple-element.47.inside_field, ...), custom_call_target="tpu_custom_call" | custom-call | flops 1000000 | bytes 4000000 | tf_op jit(solution)/shard_map/borders/pallas_call | solution.py:138
  17.3 2.9 %collective-permute-start.6 = (bf16[208,256]{1,0:T(8,128)(2,1)S(1)}, bf16[208,256]{1,0:T(8,128)(2,1)S(1)}, u32[]{:S(2)}, u32[]{:S(2)}) collective-permute-start(bf16[208,256]{1,0:T(8,128)(2,1)S(1)} %get-tuple-element.65), channel_id=1, source_target_pairs={{0,5},{1,4},{2,7},{3,6},{4,1},{5,0},{6,3},{7,2},{8,13},{9,12},{10,... | collective-permute-start | bytes 319496 | tf_op jit(solution)/shard_map/ppermute | solution.py:954
  20.1 1.7 %collective-permute-start.7 = (bf16[208,256]{1,0:T(8,128)(2,1)S(1)}, bf16[208,256]{1,0:T(8,128)(2,1)S(1)}, u32[]{:S(2)}, u32[]{:S(2)}) collective-permute-start(bf16[208,256]{1,0:T(8,128)(2,1)S(1)} %get-tuple-element.66), channel_id=1, source_target_pairs={{0,6},{1,7},{2,4},{3,5},{4,2},{5,3},{6,0},{7,1},{8,14},{9,15},{10,... | collective-permute-start | bytes 319496 | tf_op jit(solution)/shard_map/ppermute | solution.py:954
  21.8 3.1 %collective-permute-start.8 = (bf16[208,256]{1,0:T(8,128)(2,1)S(1)}, bf16[208,256]{1,0:T(8,128)(2,1)S(1)}, u32[]{:S(2)}, u32[]{:S(2)}) collective-permute-start(bf16[208,256]{1,0:T(8,128)(2,1)S(1)} %get-tuple-element.67), channel_id=1, source_target_pairs={{0,7},{1,6},{2,5},{3,4},{4,3},{5,2},{6,1},{7,0},{8,15},{9,14},{10,... | collective-permute-start | bytes 319496 | tf_op jit(solution)/shard_map/ppermute | solution.py:954
  24.9 4.3 %interior.3 = (f32[4,64,1280]{2,1,0:T(8,128)S(1)}, f32[2,48,1280]{2,1,0:T(8,128)S(1)}, bf16[3,32,1280]{2,1,0:T(8,128)(2,1)S(1)}, f32[4,8,128]{2,1,0:T(8,128)S(1)}) custom-call(s32[6]{0:T(128)S(1)} %stack.23.ids, bf16[2,64,2048]{2,1,0:T(8,128)(2,1)S(1)} %copy-done.1, bf16[2,64,2048]{2,1,0:T(8,128)(2,1)S(1)} %copy-done.2, bf16[1024,256]{1,0:T(8,128)(2,1)S(1)} %copy-done.4), custom_call_target="tpu_custom_call" | custom-call | flops 8000000 | bytes 4000000 | tf_op jit(solution)/shard_map/interior/pallas_call | solution.py:151
  29.2 2.2 %borders.3 = (bf16[208,256]{1,0:T(8,128)(2,1)S(1)}, bf16[208,256]{1,0:T(8,128)(2,1)S(1)}, bf16[208,256]{1,0:T(8,128)(2,1)S(1)}, bf16[208,256]{1,0:T(8,128)(2,1)S(1)}) custom-call(s32[6]{0:T(128)S(1)} %stack.23.ids, f32[4,64,1280]{2,1,0:T(8,128)S(1)} %get-tuple-element.56.ranged, f32[2,48,1280]{2,1,0:T(8,128)S(1)} %get-tuple-element.57.inside_field, ...), custom_call_target="tpu_custom_call" | custom-call | flops 1000000 | bytes 4000000 | tf_op jit(solution)/shard_map/borders/pallas_call | solution.py:138
  31.5 0.6 collective-permute-start.2
  32.1 1.9 %collective-permute-done.6.rest_1_ = bf16[208,256]{1,0:T(8,128)(2,1)S(1)} collective-permute-done((bf16[208,256]{1,0:T(8,128)(2,1)S(1)}, bf16[208,256]{1,0:T(8,128)(2,1)S(1)}, u32[]{:S(2)}, u32[]{:S(2)}) %collective-permute-start.6) | collective-permute-done | bytes 106528 | tf_op jit(solution)/shard_map/ppermute | solution.py:954
  33.9 1.1 %collective-permute-start.4 = (bf16[208,256]{1,0:T(8,128)(2,1)S(1)}, bf16[208,256]{1,0:T(8,128)(2,1)S(1)}, u32[]{:S(2)}, u32[]{:S(2)}) collective-permute-start(bf16[208,256]{1,0:T(8,128)(2,1)S(1)} %get-tuple-element.63), channel_id=1, source_target_pairs={{0,3},{1,2},{2,1},{3,0},{4,7},{5,6},{6,5},{7,4},{8,11},{9,10},{10,... | collective-permute-start | bytes 319496 | tf_op jit(solution)/shard_map/ppermute | solution.py:954
  35.0 1.2 %far.1 = (f32[256,256]{1,0:T(8,128)S(1)}, f32[256,256]{1,0:T(8,128)S(1)}, f32[256,128]{1,0:T(8,128)S(1)}, f32[256,128]{1,0:T(8,128)S(1)}, f32[256,256]{1,0:T(8,1...) custom-call(s32[6]{0:T(128)S(1)} %stack.23.ids, ...), custom_call_target="tpu_custom_call" | custom-call | flops 1000000 | bytes 4000000 | tf_op jit(solution)/shard_map/far/pallas_call | solution.py:138
  36.2 1.4 %collective-permute-done.3.rest_2_ = bf16[208,256]{1,0:T(8,128)(2,1)S(1)} collective-permute-done((bf16[208,256]{1,0:T(8,128)(2,1)S(1)}, bf16[208,256]{1,0:T(8,128)(2,1)S(1)}, u32[]{:S(2)}, u32[]{:S(2)}) %collective-permute-start.3) | collective-permute-done | bytes 106528 | tf_op jit(solution)/shard_map/ppermute | solution.py:954
  37.6 2.3 %collective-permute-done.4.rest_3_ = bf16[208,256]{1,0:T(8,128)(2,1)S(1)} collective-permute-done((bf16[208,256]{1,0:T(8,128)(2,1)S(1)}, bf16[208,256]{1,0:T(8,128)(2,1)S(1)}, u32[]{:S(2)}, u32[]{:S(2)}) %collective-permute-start.4) | collective-permute-done | bytes 106528 | tf_op jit(solution)/shard_map/ppermute | solution.py:954
  40.0 4.1 %tiles.1 = (f32[512,256]{1,0:T(8,128)S(1)}, f32[512,256]{1,0:T(8,128)S(1)}, f32[512,256]{1,0:T(8,128)S(1)}, f32[512,128]{1,0:T(8,128)S(1)}, f32[520,256]{1,0:T(8...) custom-call(s32[6]{0:T(128)S(1)} %stack.23.ids, ...), custom_call_target="tpu_custom_call" | custom-call | flops 1000000 | bytes 4000000 | tf_op jit(solution)/shard_map/tiles/pallas_call | solution.py:138
  44.2 1.8 %collective-permute-start.10 = (f32[8,128]{1,0:T(8,128)S(1)}, f32[8,128]{1,0:T(8,128)S(1)}, u32[]{:S(2)}, u32[]{:S(2)}) collective-permute-start(f32[8,128]{1,0:T(8,128)S(1)} %get-tuple-element.82), channel_id=1, source_target_pairs={{0,24},{8,16},{16,8},{24,0},{1,25},{9,17},{17,9},{25,1},{2,26},{10... | collective-permute-start | bytes 12296 | tf_op jit(solution)/shard_map/ppermute | solution.py:892
  46.2 2.9 %collective-permute-start.12 = (f32[8,128]{1,0:T(8,128)S(1)}, f32[8,128]{1,0:T(8,128)S(1)}, u32[]{:S(2)}, u32[]{:S(2)}) collective-permute-start(f32[8,128]{1,0:T(8,128)S(1)} %get-tuple-element.84), channel_id=1, source_target_pairs={{0,7},{1,2},{2,1},{3,4},{4,3},{5,6},{6,5},{7,0},{8,15},{9,10},{10,... | collective-permute-start | bytes 12296 | tf_op jit(solution)/shard_map/ppermute | solution.py:892
  49.6 2.9 %collective-permute-done.12.col_next = f32[8,128]{1,0:T(8,128)S(1)} collective-permute-done((f32[8,128]{1,0:T(8,128)S(1)}, f32[8,128]{1,0:T(8,128)S(1)}, u32[]{:S(2)}, u32[]{:S(2)}) %collective-permute-start.12) | collective-permute-done | bytes 4128 | tf_op jit(solution)/shard_map/ppermute | solution.py:892
  52.5 4.6 %operator.1 = (f32[512,256]{1,0:T(8,128)S(1)}, f32[512,256]{1,0:T(8,128)S(1)}, f32[512,256]{1,0:T(8,128)S(1)}, bf16[16,128]{1,0:T(8,128)(2,1)S(1)}, f32[16,128]{1,0:T(8,128)S(1)}) custom-call(s32[6]{0:T(128)S(1)} %stack.23.ids, f32[512,256]{1,0:T(8,128)S(1)} %get-tuple-element.76.residual, f32[512,256]{1,0:T(8,128)S(1)} %get-tuple-element.77.shaped, ...), custom_call_target="tpu_custom_call" | custom-call | flops 1000000 | bytes 4000000 | tf_op jit(solution)/shard_map/operator/pallas_call | solution.py:138
  57.1 10.9 %all_to_all.5.gathered = bf16[32,16,128]{2,1,0:T(8,128)(2,1)S(1)} all-to-all(bf16[32,16,128]{2,1,0:T(8,128)(2,1)S(1)} %broadcast_in_dim.2), channel_id=1, replica_groups=mesh['row'=4,'col'=8] {'row','col'}, dimensions={0} | all-to-all | bytes 262144 | tf_op jit(solution)/shard_map/all_to_all | solution.py:1032
  68.0 2.1 %finish.1 = (f32[512,256]{1,0:T(8,128)}, f32[512,256]{1,0:T(8,128)}) custom-call(s32[6]{0:T(128)S(1)} %stack.23.ids, bf16[32,16,128]{2,1,0:T(8,128)(2,1)S(1)} %all_to_all.5.gathered, f32[512,256]{1,0:T(8,128)S(1)} %get-tuple-element.76.residual, f32[512,256]{1,0:T(8,128)S(1)} %get-tuple-element.77.shaped, f32[512,256]{1,0:T(8,128)S(1)} %get-tuple-element.86.operated, ...), custom_call_target="tpu_custom_call" | custom-call | flops 1000000 | bytes 4000000 | tf_op jit(solution)/shard_map/finish/pallas_call | solution.py:138
  (29 shorter events, 1.1 us)
Async XLA Ops:
  0.6 7.6 %copy-start.2 = (bf16[2,64,2048]{2,1,0:T(8,128)(2,1)S(1)}, bf16[2,64,2048]{2,1,0:T(8,128)(2,1)}, u32[]{:S(2)}) copy-start(bf16[2,64,2048]{2,1,0:T(8,128)(2,1)} %second.2) | copy-start | bytes 1572868
  0.6 7.6 %copy-start.1 = (bf16[2,64,2048]{2,1,0:T(8,128)(2,1)S(1)}, bf16[2,64,2048]{2,1,0:T(8,128)(2,1)}, u32[]{:S(2)}) copy-start(bf16[2,64,2048]{2,1,0:T(8,128)(2,1)} %first.2) | copy-start | bytes 1572868
  1.7 11.7 %collective-permute-start.1 = (bf16[4,8,2048]{2,1,0:T(8,128)(2,1)S(1)}, bf16[4,8,2048]{2,1,0:T(8,128)(2,1)S(1)}, u32[]{:S(2)}, u32[]{:S(2)}) collective-permute-start(bf16[4,8,2048]{2,1,0:T(8,128)(2,1)S(1)} %get-tuple-element.94), channel_id=1, source_target_pairs={{0,31},{1,2},{2,1},{3,4},{4,3},{5,6},{6,5},{7,8},{8,7},{9,10},{10,... | collective-permute-start | bytes 393224 | tf_op jit(solution)/shard_map/ppermute | solution.py:892
  8.2 6.8 %collective-permute-start = (bf16[4,8,2048]{2,1,0:T(8,128)(2,1)S(1)}, bf16[4,8,2048]{2,1,0:T(8,128)(2,1)S(1)}, u32[]{:S(2)}, u32[]{:S(2)}) collective-permute-start(bf16[4,8,2048]{2,1,0:T(8,128)(2,1)S(1)} %get-tuple-element.95), channel_id=1, source_target_pairs={{0,1},{1,0},{2,3},{3,2},{4,5},{5,4},{6,7},{7,6},{8,9},{9,8},{10,11... | collective-permute-start | bytes 393224 | tf_op jit(solution)/shard_map/ppermute | solution.py:892
  8.3 1.0 %copy-start.3 = (bf16[1024,256]{1,0:T(8,128)(2,1)S(1)}, bf16[1024,256]{1,0:T(8,128)(2,1)}, u32[]{:S(2)}) copy-start(bf16[1024,256]{1,0:T(8,128)(2,1)} %constant.40.clone.table) | copy-start | bytes 1572868
  13.4 11.5 %copy-start.4 = (bf16[1024,256]{1,0:T(8,128)(2,1)S(1)}, bf16[1024,256]{1,0:T(8,128)(2,1)}, u32[]{:S(2)}) copy-start(bf16[1024,256]{1,0:T(8,128)(2,1)} %constant.40.clone.table) | copy-start | bytes 1572868
  17.2 14.9 %collective-permute-start.5 = (bf16[208,256]{1,0:T(8,128)(2,1)S(1)}, bf16[208,256]{1,0:T(8,128)(2,1)S(1)}, u32[]{:S(2)}, u32[]{:S(2)}) collective-permute-start(bf16[208,256]{1,0:T(8,128)(2,1)S(1)} %get-tuple-element.64), channel_id=1, source_target_pairs={{0,4},{1,5},{2,6},{3,7},{4,0},{5,1},{6,2},{7,3},{8,12},{9,13},{10,... | collective-permute-start | bytes 319496 | tf_op jit(solution)/shard_map/ppermute | solution.py:954
  17.3 16.7 %collective-permute-start.6 = (bf16[208,256]{1,0:T(8,128)(2,1)S(1)}, bf16[208,256]{1,0:T(8,128)(2,1)S(1)}, u32[]{:S(2)}, u32[]{:S(2)}) collective-permute-start(bf16[208,256]{1,0:T(8,128)(2,1)S(1)} %get-tuple-element.65), channel_id=1, source_target_pairs={{0,5},{1,4},{2,7},{3,6},{4,1},{5,0},{6,3},{7,2},{8,13},{9,12},{10,... | collective-permute-start | bytes 319496 | tf_op jit(solution)/shard_map/ppermute | solution.py:954
  20.1 14.9 %collective-permute-start.7 = (bf16[208,256]{1,0:T(8,128)(2,1)S(1)}, bf16[208,256]{1,0:T(8,128)(2,1)S(1)}, u32[]{:S(2)}, u32[]{:S(2)}) collective-permute-start(bf16[208,256]{1,0:T(8,128)(2,1)S(1)} %get-tuple-element.66), channel_id=1, source_target_pairs={{0,6},{1,7},{2,4},{3,5},{4,2},{5,3},{6,0},{7,1},{8,14},{9,15},{10,... | collective-permute-start | bytes 319496 | tf_op jit(solution)/shard_map/ppermute | solution.py:954
  21.8 13.2 %collective-permute-start.8 = (bf16[208,256]{1,0:T(8,128)(2,1)S(1)}, bf16[208,256]{1,0:T(8,128)(2,1)S(1)}, u32[]{:S(2)}, u32[]{:S(2)}) collective-permute-start(bf16[208,256]{1,0:T(8,128)(2,1)S(1)} %get-tuple-element.67), channel_id=1, source_target_pairs={{0,7},{1,6},{2,5},{3,4},{4,3},{5,2},{6,1},{7,0},{8,15},{9,14},{10,... | collective-permute-start | bytes 319496 | tf_op jit(solution)/shard_map/ppermute | solution.py:954
  24.9 15.1 %copy-start.6 = (bf16[1024,256]{1,0:T(8,128)(2,1)S(1)}, bf16[1024,256]{1,0:T(8,128)(2,1)}, u32[]{:S(2)}) copy-start(bf16[1024,256]{1,0:T(8,128)(2,1)} %constant.42.clone.rest_13_.rest_1_) | copy-start | bytes 1572868
  29.2 10.8 %copy-start = (bf16[2048,512]{1,0:T(8,128)(2,1)S(1)}, bf16[2048,512]{1,0:T(8,128)(2,1)}, u32[]{:S(2)}) copy-start(bf16[2048,512]{1,0:T(8,128)(2,1)} %constant.41.clone.rest_12_.rest_0_) | copy-start | bytes 6291460
  29.2 10.8 %copy-start.5 = (f32[512,256]{1,0:T(8,128)S(1)}, f32[512,256]{1,0:T(8,128)}, u32[]{:S(2)}) copy-start(f32[512,256]{1,0:T(8,128)} %constant.43.clone.rest_14_.rest_2_) | copy-start | bytes 1572868
  31.5 4.8 %collective-permute-start.2 = (bf16[208,256]{1,0:T(8,128)(2,1)S(1)}, bf16[208,256]{1,0:T(8,128)(2,1)S(1)}, u32[]{:S(2)}, u32[]{:S(2)}) collective-permute-start(bf16[208,256]{1,0:T(8,128)(2,1)S(1)} %get-tuple-element.61), channel_id=1, source_target_pairs={{0,1},{1,0},{2,3},{3,2},{4,5},{5,4},{6,7},{7,6},{8,9},{9,8},{10,11... | collective-permute-start | bytes 319496 | tf_op jit(solution)/shard_map/ppermute | solution.py:954
  32.1 5.6 %collective-permute-start.3 = (bf16[208,256]{1,0:T(8,128)(2,1)S(1)}, bf16[208,256]{1,0:T(8,128)(2,1)S(1)}, u32[]{:S(2)}, u32[]{:S(2)}) collective-permute-start(bf16[208,256]{1,0:T(8,128)(2,1)S(1)} %get-tuple-element.62), channel_id=1, source_target_pairs={{0,2},{1,3},{2,0},{3,1},{4,6},{5,7},{6,4},{7,5},{8,10},{9,11},{10,... | collective-permute-start | bytes 319496 | tf_op jit(solution)/shard_map/ppermute | solution.py:954
  33.9 6.0 %collective-permute-start.4 = (bf16[208,256]{1,0:T(8,128)(2,1)S(1)}, bf16[208,256]{1,0:T(8,128)(2,1)S(1)}, u32[]{:S(2)}, u32[]{:S(2)}) collective-permute-start(bf16[208,256]{1,0:T(8,128)(2,1)S(1)} %get-tuple-element.63), channel_id=1, source_target_pairs={{0,3},{1,2},{2,1},{3,0},{4,7},{5,6},{6,5},{7,4},{8,11},{9,10},{10,... | collective-permute-start | bytes 319496 | tf_op jit(solution)/shard_map/ppermute | solution.py:954
  44.1 5.0 %collective-permute-start.9 = (f32[8,128]{1,0:T(8,128)S(1)}, f32[8,128]{1,0:T(8,128)S(1)}, u32[]{:S(2)}, u32[]{:S(2)}) collective-permute-start(f32[8,128]{1,0:T(8,128)S(1)} %get-tuple-element.81), channel_id=1, source_target_pairs={{0,8},{8,0},{16,24},{24,16},{1,9},{9,1},{17,25},{25,17},{2,10},{10... | collective-permute-start | bytes 12296 | tf_op jit(solution)/shard_map/ppermute | solution.py:892
  44.2 4.9 %collective-permute-start.10 = (f32[8,128]{1,0:T(8,128)S(1)}, f32[8,128]{1,0:T(8,128)S(1)}, u32[]{:S(2)}, u32[]{:S(2)}) collective-permute-start(f32[8,128]{1,0:T(8,128)S(1)} %get-tuple-element.82), channel_id=1, source_target_pairs={{0,24},{8,16},{16,8},{24,0},{1,25},{9,17},{17,9},{25,1},{2,26},{10... | collective-permute-start | bytes 12296 | tf_op jit(solution)/shard_map/ppermute | solution.py:892
  46.0 3.6 %collective-permute-start.11 = (f32[8,128]{1,0:T(8,128)S(1)}, f32[8,128]{1,0:T(8,128)S(1)}, u32[]{:S(2)}, u32[]{:S(2)}) collective-permute-start(f32[8,128]{1,0:T(8,128)S(1)} %get-tuple-element.83), channel_id=1, source_target_pairs={{0,1},{1,0},{2,3},{3,2},{4,5},{5,4},{6,7},{7,6},{8,9},{9,8},{10,11... | collective-permute-start | bytes 12296 | tf_op jit(solution)/shard_map/ppermute | solution.py:892
  46.2 6.3 %collective-permute-start.12 = (f32[8,128]{1,0:T(8,128)S(1)}, f32[8,128]{1,0:T(8,128)S(1)}, u32[]{:S(2)}, u32[]{:S(2)}) collective-permute-start(f32[8,128]{1,0:T(8,128)S(1)} %get-tuple-element.84), channel_id=1, source_target_pairs={{0,7},{1,2},{2,1},{3,4},{4,3},{5,6},{6,5},{7,0},{8,15},{9,10},{10,... | collective-permute-start | bytes 12296 | tf_op jit(solution)/shard_map/ppermute | solution.py:892

commit v4 on v3

--- a/solution.py
+++ b/solution.py
@@ -340,6 +340,7 @@
             else:
                 seg[e, f, own_rows:, :] = total
                 seg[e, f, 0:own_rows, :] = ranged[f, lines - own_rows :, :]
+    border = []
     for e in range(2):
         ref = seg.at[e]
         for c in range(0, span, LANES):
@@ -350,13 +351,17 @@
             field[1, e * HALO : (e + 1) * HALO, cs] = gain
         low, high = end_weights(e == 0)
         r = 0 if e == 0 else own_rows - HALO
-        smoothed = [
-            jnp.sum(low * ref[f, r : r + HALO, :] + high * ref[f, r + HALO : r + 2 * HALO, :], axis=0, keepdims=True)
-            for f in range(4)
-        ]
-        phase, gain = phase_gain(smoothed)
-        ends[e : e + 1, :] = phase
-        ends[2 + e : 3 + e, :] = gain * inside[e]
+        border.append(
+            [
+                jnp.sum(low * ref[f, r : r + HALO, :] + high * ref[f, r + HALO : r + 2 * HALO, :], axis=0, keepdims=True)
+                for f in range(4)
+            ]
+        )
+    phase, gain = phase_gain([jnp.concatenate(pair, axis=0) for pair in zip(*border)])
+    ends[0:2, :] = phase
+    ends[2:4, :] = gain
+    for e in range(2):
+        ends[2 + e : 3 + e, :] = ends[2 + e : 3 + e, :] * inside[e]
     groups = lines // 8
     inner = lines - 2 * EDGE
     for n, s in enumerate(range(half, columns) if across else range(half)):
@@ -719,7 +724,7 @@
 
 
 def second_kernel(
-    tile_az, tile, ids, residual, shaped, weight_x, rim_x, weight_y, row_pair, row_next, col_pair, col_next, *rest
+    tile_az, tile, ids, residual, shaped, weight_x, rim_x, weight_y, col_next, col_pair, row_next, row_pair, *rest
 ):
     tables, inverse = rest[:2], rest[2]
     operated, shaped2, operated2, chunk, roots = rest[3:8]
@@ -1015,12 +1020,11 @@
         ],
         "tiles",
     )
-    rims = (
-        swapped(row_pair, "row", rows, 0),
-        swapped(row_next, "row", rows, 1),
-        swapped(col_pair, "col", columns, 0),
-        swapped(col_next, "col", columns, 1),
-    )
+    col_next = swapped(col_next, "col", columns, 1)
+    col_pair = swapped(col_pair, "col", columns, 0)
+    row_next = swapped(row_next, "row", rows, 1)
+    row_pair = swapped(row_pair, "row", rows, 0)
+    rims = (col_next, col_pair, row_next, row_pair)
     operated, shaped2, operated2, chunk, roots = call(
         functools.partial(second_kernel, tile_az, tile),
         [whole, whole, whole, ((16, LANES), bf16), ((16, LANES), f32)],

time: 70.5 us -> 68.9 us (0.977)
  waiting for transfers between devices: 10.6 us -> 8.82 us
    ppermute x6, waiting for transfers between devices: 4.92 us -> 3.12 us  [swapped(): return lax.ppermute(value, axis, pairs)]
where the time goes in v4:
time: 68.9 us; the launch traced here: 68.7 us
  Pallas kernels  24.7 us (36%)
  starting transfers between devices  20.6 us (30%)
  blocking collectives  11.4 us (17%)
  waiting for transfers between devices  8.82 us (13%)
  local copies, waits for them, and re-layouts  2.21 us (3%)
  between operations  0.94 us (1%)
    pallas_call x6, Pallas kernels, call(): pl.pallas_call(body, out_shape=[jax.ShapeDtypeStruct(s, d) for s, d in ou...  16.3 us
    all_to_all x1, blocking collectives, shards(): gathered = lax.all_to_all(spread, axes, 0, 0, tiled=True)  11.4 us
    ppermute x6, starting transfers between devices, swapped(): return lax.ppermute(value, axis, pairs)  11.3 us
    ppermute x7, starting transfers between devices, shards(): lax.ppermute(sent[s], 'col', [(i, i ^ s) for i in range(columns)])  9.34 us
    pallas_call x2, Pallas kernels, interior(): pl.pallas_call(body, out_shape=[jax.ShapeDtypeStruct(s, d) for s, d in ou...  8.42 us
    ppermute x7, waiting for transfers between devices, shards(): lax.ppermute(sent[s], 'col', [(i, i ^ s) for i in range(columns)])  5.7 us
    ppermute x6, waiting for transfers between devices, swapped(): return lax.ppermute(value, axis, pairs)  3.12 us
  transfers between devices with their start and end apart: 13, of which 6 were waited for; matrix products, arithmetic and copies ran while one was open for 0% of the time, Pallas kernels for 17%

profile of v4, /device:TPU:0, one launch (start us, length us, event | category | flops | bytes accessed | tf_op | source)
XLA Modules:
  0.0 68.7 jit_solution(3016176125240581959)
XLA Ops:
  0.7 1.0 %fusion = (bf16[2,8,2048]{2,1,0:T(8,128)(2,1)S(1)}, bf16[2,8,2048]{2,1,0:T(8,128)(2,1)S(1)}, bf16[2,8,2048]{2,1,0:T(8,128)(2,1)S(1)}, bf16[2,8,2048]{2,1,0:T(8,128)(2,1)S(1)}) fusion(bf16[2,64,2048]{2,1,0:T(8,128)(2,1)} %first.2, bf16[2,64,2048]{2,1,0:T(8,128)(2,1)} %second.2), kind=kLoop, calls=%fused_computation.4 | loop fusion | bytes 524288 | tf_op jit(solution)/shard_map/slice | solution.py:910
  1.7 6.4 %collective-permute-start.1 = (bf16[4,8,2048]{2,1,0:T(8,128)(2,1)S(1)}, bf16[4,8,2048]{2,1,0:T(8,128)(2,1)S(1)}, u32[]{:S(2)}, u32[]{:S(2)}) collective-permute-start(bf16[4,8,2048]{2,1,0:T(8,128)(2,1)S(1)} %get-tuple-element.94), channel_id=1, source_target_pairs={{0,31},{1,2},{2,1},{3,4},{4,3},{5,6},{6,5},{7,8},{8,7},{9,10},{10,... | collective-permute-start | bytes 393224 | tf_op jit(solution)/shard_map/ppermute | solution.py:897
  8.3 1.0 %copy-done.3 = bf16[1024,256]{1,0:T(8,128)(2,1)S(1)} copy-done((bf16[1024,256]{1,0:T(8,128)(2,1)S(1)}, bf16[1024,256]{1,0:T(8,128)(2,1)}, u32[]{:S(2)}) %copy-start.3) | copy-done | bytes 524312
  9.3 4.1 %interior.2 = (f32[4,64,1280]{2,1,0:T(8,128)S(1)}, f32[2,48,1280]{2,1,0:T(8,128)S(1)}, bf16[3,32,1280]{2,1,0:T(8,128)(2,1)S(1)}, f32[4,8,128]{2,1,0:T(8,128)S(1)}) custom-call(s32[6]{0:T(128)S(1)} %stack.23.ids, bf16[2,64,2048]{2,1,0:T(8,128)(2,1)S(1)} %copy-done.1, bf16[2,64,2048]{2,1,0:T(8,128)(2,1)S(1)} %copy-done.2, bf16[1024,256]{1,0:T(8,128)(2,1)S(1)} %copy-done.3), custom_call_target="tpu_custom_call" | custom-call | flops 8000000 | bytes 4000000 | tf_op jit(solution)/shard_map/interior/pallas_call | solution.py:151
  13.5 1.5 %collective-permute-done.from_pair = bf16[4,8,2048]{2,1,0:T(8,128)(2,1)S(1)} collective-permute-done((bf16[4,8,2048]{2,1,0:T(8,128)(2,1)S(1)}, bf16[4,8,2048]{2,1,0:T(8,128)(2,1)S(1)}, u32[]{:S(2)}, u32[]{:S(2)}) %collective-permute-start) | collective-permute-done | bytes 131104 | tf_op jit(solution)/shard_map/ppermute | solution.py:897
  15.0 2.2 %borders.2 = (bf16[208,256]{1,0:T(8,128)(2,1)S(1)}, bf16[208,256]{1,0:T(8,128)(2,1)S(1)}, bf16[208,256]{1,0:T(8,128)(2,1)S(1)}, bf16[208,256]{1,0:T(8,128)(2,1)S(1)}) custom-call(s32[6]{0:T(128)S(1)} %stack.23.ids, f32[4,64,1280]{2,1,0:T(8,128)S(1)} %get-tuple-element.46.ranged, f32[2,48,1280]{2,1,0:T(8,128)S(1)} %get-tuple-element.47.inside_field, ...), custom_call_target="tpu_custom_call" | custom-call | flops 1000000 | bytes 4000000 | tf_op jit(solution)/shard_map/borders/pallas_call | solution.py:138
  17.2 2.9 %collective-permute-start.6 = (bf16[208,256]{1,0:T(8,128)(2,1)S(1)}, bf16[208,256]{1,0:T(8,128)(2,1)S(1)}, u32[]{:S(2)}, u32[]{:S(2)}) collective-permute-start(bf16[208,256]{1,0:T(8,128)(2,1)S(1)} %get-tuple-element.65), channel_id=1, source_target_pairs={{0,5},{1,4},{2,7},{3,6},{4,1},{5,0},{6,3},{7,2},{8,13},{9,12},{10,... | collective-permute-start | bytes 319496 | tf_op jit(solution)/shard_map/ppermute | solution.py:959
  20.1 1.7 %collective-permute-start.7 = (bf16[208,256]{1,0:T(8,128)(2,1)S(1)}, bf16[208,256]{1,0:T(8,128)(2,1)S(1)}, u32[]{:S(2)}, u32[]{:S(2)}) collective-permute-start(bf16[208,256]{1,0:T(8,128)(2,1)S(1)} %get-tuple-element.66), channel_id=1, source_target_pairs={{0,6},{1,7},{2,4},{3,5},{4,2},{5,3},{6,0},{7,1},{8,14},{9,15},{10,... | collective-permute-start | bytes 319496 | tf_op jit(solution)/shard_map/ppermute | solution.py:959
  21.8 3.1 %collective-permute-start.8 = (bf16[208,256]{1,0:T(8,128)(2,1)S(1)}, bf16[208,256]{1,0:T(8,128)(2,1)S(1)}, u32[]{:S(2)}, u32[]{:S(2)}) collective-permute-start(bf16[208,256]{1,0:T(8,128)(2,1)S(1)} %get-tuple-element.67), channel_id=1, source_target_pairs={{0,7},{1,6},{2,5},{3,4},{4,3},{5,2},{6,1},{7,0},{8,15},{9,14},{10,... | collective-permute-start | bytes 319496 | tf_op jit(solution)/shard_map/ppermute | solution.py:959
  24.9 4.3 %interior.3 = (f32[4,64,1280]{2,1,0:T(8,128)S(1)}, f32[2,48,1280]{2,1,0:T(8,128)S(1)}, bf16[3,32,1280]{2,1,0:T(8,128)(2,1)S(1)}, f32[4,8,128]{2,1,0:T(8,128)S(1)}) custom-call(s32[6]{0:T(128)S(1)} %stack.23.ids, bf16[2,64,2048]{2,1,0:T(8,128)(2,1)S(1)} %copy-done.1, bf16[2,64,2048]{2,1,0:T(8,128)(2,1)S(1)} %copy-done.2, bf16[1024,256]{1,0:T(8,128)(2,1)S(1)} %copy-done.4), custom_call_target="tpu_custom_call" | custom-call | flops 8000000 | bytes 4000000 | tf_op jit(solution)/shard_map/interior/pallas_call | solution.py:151
  29.2 2.2 %borders.3 = (bf16[208,256]{1,0:T(8,128)(2,1)S(1)}, bf16[208,256]{1,0:T(8,128)(2,1)S(1)}, bf16[208,256]{1,0:T(8,128)(2,1)S(1)}, bf16[208,256]{1,0:T(8,128)(2,1)S(1)}) custom-call(s32[6]{0:T(128)S(1)} %stack.23.ids, f32[4,64,1280]{2,1,0:T(8,128)S(1)} %get-tuple-element.56.ranged, f32[2,48,1280]{2,1,0:T(8,128)S(1)} %get-tuple-element.57.inside_field, ...), custom_call_target="tpu_custom_call" | custom-call | flops 1000000 | bytes 4000000 | tf_op jit(solution)/shard_map/borders/pallas_call | solution.py:138
  32.0 1.9 %collective-permute-done.6.rest_1_ = bf16[208,256]{1,0:T(8,128)(2,1)S(1)} collective-permute-done((bf16[208,256]{1,0:T(8,128)(2,1)S(1)}, bf16[208,256]{1,0:T(8,128)(2,1)S(1)}, u32[]{:S(2)}, u32[]{:S(2)}) %collective-permute-start.6) | collective-permute-done | bytes 106528 | tf_op jit(solution)/shard_map/ppermute | solution.py:959
  33.9 1.0 %collective-permute-start.4 = (bf16[208,256]{1,0:T(8,128)(2,1)S(1)}, bf16[208,256]{1,0:T(8,128)(2,1)S(1)}, u32[]{:S(2)}, u32[]{:S(2)}) collective-permute-start(bf16[208,256]{1,0:T(8,128)(2,1)S(1)} %get-tuple-element.63), channel_id=1, source_target_pairs={{0,3},{1,2},{2,1},{3,0},{4,7},{5,6},{6,5},{7,4},{8,11},{9,10},{10,... | collective-permute-start | bytes 319496 | tf_op jit(solution)/shard_map/ppermute | solution.py:959
  35.0 1.2 %far.1 = (f32[256,256]{1,0:T(8,128)S(1)}, f32[256,256]{1,0:T(8,128)S(1)}, f32[256,128]{1,0:T(8,128)S(1)}, f32[256,128]{1,0:T(8,128)S(1)}, f32[256,256]{1,0:T(8,1...) custom-call(s32[6]{0:T(128)S(1)} %stack.23.ids, ...), custom_call_target="tpu_custom_call" | custom-call | flops 1000000 | bytes 4000000 | tf_op jit(solution)/shard_map/far/pallas_call | solution.py:138
  36.2 1.4 %collective-permute-done.3.rest_2_ = bf16[208,256]{1,0:T(8,128)(2,1)S(1)} collective-permute-done((bf16[208,256]{1,0:T(8,128)(2,1)S(1)}, bf16[208,256]{1,0:T(8,128)(2,1)S(1)}, u32[]{:S(2)}, u32[]{:S(2)}) %collective-permute-start.3) | collective-permute-done | bytes 106528 | tf_op jit(solution)/shard_map/ppermute | solution.py:959
  37.5 2.4 %collective-permute-done.4.rest_3_ = bf16[208,256]{1,0:T(8,128)(2,1)S(1)} collective-permute-done((bf16[208,256]{1,0:T(8,128)(2,1)S(1)}, bf16[208,256]{1,0:T(8,128)(2,1)S(1)}, u32[]{:S(2)}, u32[]{:S(2)}) %collective-permute-start.4) | collective-permute-done | bytes 106528 | tf_op jit(solution)/shard_map/ppermute | solution.py:959
  39.9 4.1 %tiles.1 = (f32[512,256]{1,0:T(8,128)S(1)}, f32[512,256]{1,0:T(8,128)S(1)}, f32[512,256]{1,0:T(8,128)S(1)}, f32[512,128]{1,0:T(8,128)S(1)}, f32[520,256]{1,0:T(8...) custom-call(s32[6]{0:T(128)S(1)} %stack.23.ids, ...), custom_call_target="tpu_custom_call" | custom-call | flops 1000000 | bytes 4000000 | tf_op jit(solution)/shard_map/tiles/pallas_call | solution.py:138
  44.0 2.4 %collective-permute-start.9 = (f32[8,128]{1,0:T(8,128)S(1)}, f32[8,128]{1,0:T(8,128)S(1)}, u32[]{:S(2)}, u32[]{:S(2)}) collective-permute-start(f32[8,128]{1,0:T(8,128)S(1)} %get-tuple-element.81), channel_id=1, source_target_pairs={{0,7},{1,2},{2,1},{3,4},{4,3},{5,6},{6,5},{7,0},{8,15},{9,10},{10,... | collective-permute-start | bytes 12296 | tf_op jit(solution)/shard_map/ppermute | solution.py:897
  46.4 1.1 %collective-permute-start.10 = (f32[8,128]{1,0:T(8,128)S(1)}, f32[8,128]{1,0:T(8,128)S(1)}, u32[]{:S(2)}, u32[]{:S(2)}) collective-permute-start(f32[8,128]{1,0:T(8,128)S(1)} %get-tuple-element.82), channel_id=1, source_target_pairs={{0,1},{1,0},{2,3},{3,2},{4,5},{5,4},{6,7},{7,6},{8,9},{9,8},{10,11... | collective-permute-start | bytes 12296 | tf_op jit(solution)/shard_map/ppermute | solution.py:897
  47.5 1.3 %collective-permute-start.12 = (f32[8,128]{1,0:T(8,128)S(1)}, f32[8,128]{1,0:T(8,128)S(1)}, u32[]{:S(2)}, u32[]{:S(2)}) collective-permute-start(f32[8,128]{1,0:T(8,128)S(1)} %get-tuple-element.84), channel_id=1, source_target_pairs={{0,8},{8,0},{16,24},{24,16},{1,9},{9,1},{17,25},{25,17},{2,10},{10... | collective-permute-start | bytes 12296 | tf_op jit(solution)/shard_map/ppermute | solution.py:897
  48.9 1.5 %collective-permute-done.9.col_next = f32[8,128]{1,0:T(8,128)S(1)} collective-permute-done((f32[8,128]{1,0:T(8,128)S(1)}, f32[8,128]{1,0:T(8,128)S(1)}, u32[]{:S(2)}, u32[]{:S(2)}) %collective-permute-start.9) | collective-permute-done | bytes 4128 | tf_op jit(solution)/shard_map/ppermute | solution.py:897
  50.5 4.6 %operator.1 = (f32[512,256]{1,0:T(8,128)S(1)}, f32[512,256]{1,0:T(8,128)S(1)}, f32[512,256]{1,0:T(8,128)S(1)}, bf16[16,128]{1,0:T(8,128)(2,1)S(1)}, f32[16,128]{1,0:T(8,128)S(1)}) custom-call(s32[6]{0:T(128)S(1)} %stack.23.ids, f32[512,256]{1,0:T(8,128)S(1)} %get-tuple-element.76.residual, f32[512,256]{1,0:T(8,128)S(1)} %get-tuple-element.77.shaped, ...), custom_call_target="tpu_custom_call" | custom-call | flops 1000000 | bytes 4000000 | tf_op jit(solution)/shard_map/operator/pallas_call | solution.py:138
  55.1 11.4 %all_to_all.5.gathered = bf16[32,16,128]{2,1,0:T(8,128)(2,1)S(1)} all-to-all(bf16[32,16,128]{2,1,0:T(8,128)(2,1)S(1)} %broadcast_in_dim.2), channel_id=1, replica_groups=mesh['row'=4,'col'=8] {'row','col'}, dimensions={0} | all-to-all | bytes 262144 | tf_op jit(solution)/shard_map/all_to_all | solution.py:1036
  66.5 2.1 %finish.1 = (f32[512,256]{1,0:T(8,128)}, f32[512,256]{1,0:T(8,128)}) custom-call(s32[6]{0:T(128)S(1)} %stack.23.ids, bf16[32,16,128]{2,1,0:T(8,128)(2,1)S(1)} %all_to_all.5.gathered, f32[512,256]{1,0:T(8,128)S(1)} %get-tuple-element.76.residual, f32[512,256]{1,0:T(8,128)S(1)} %get-tuple-element.77.shaped, f32[512,256]{1,0:T(8,128)S(1)} %get-tuple-element.86.operated, ...), custom_call_target="tpu_custom_call" | custom-call | flops 1000000 | bytes 4000000 | tf_op jit(solution)/shard_map/finish/pallas_call | solution.py:138
  (29 shorter events, 1.0 us)
Async XLA Ops:
  0.6 7.6 %copy-start.2 = (bf16[2,64,2048]{2,1,0:T(8,128)(2,1)S(1)}, bf16[2,64,2048]{2,1,0:T(8,128)(2,1)}, u32[]{:S(2)}) copy-start(bf16[2,64,2048]{2,1,0:T(8,128)(2,1)} %second.2) | copy-start | bytes 1572868
  0.6 7.6 %copy-start.1 = (bf16[2,64,2048]{2,1,0:T(8,128)(2,1)S(1)}, bf16[2,64,2048]{2,1,0:T(8,128)(2,1)}, u32[]{:S(2)}) copy-start(bf16[2,64,2048]{2,1,0:T(8,128)(2,1)} %first.2) | copy-start | bytes 1572868
  1.7 11.7 %collective-permute-start.1 = (bf16[4,8,2048]{2,1,0:T(8,128)(2,1)S(1)}, bf16[4,8,2048]{2,1,0:T(8,128)(2,1)S(1)}, u32[]{:S(2)}, u32[]{:S(2)}) collective-permute-start(bf16[4,8,2048]{2,1,0:T(8,128)(2,1)S(1)} %get-tuple-element.94), channel_id=1, source_target_pairs={{0,31},{1,2},{2,1},{3,4},{4,3},{5,6},{6,5},{7,8},{8,7},{9,10},{10,... | collective-permute-start | bytes 393224 | tf_op jit(solution)/shard_map/ppermute | solution.py:897
  8.2 6.8 %collective-permute-start = (bf16[4,8,2048]{2,1,0:T(8,128)(2,1)S(1)}, bf16[4,8,2048]{2,1,0:T(8,128)(2,1)S(1)}, u32[]{:S(2)}, u32[]{:S(2)}) collective-permute-start(bf16[4,8,2048]{2,1,0:T(8,128)(2,1)S(1)} %get-tuple-element.95), channel_id=1, source_target_pairs={{0,1},{1,0},{2,3},{3,2},{4,5},{5,4},{6,7},{7,6},{8,9},{9,8},{10,11... | collective-permute-start | bytes 393224 | tf_op jit(solution)/shard_map/ppermute | solution.py:897
  8.3 1.0 %copy-start.3 = (bf16[1024,256]{1,0:T(8,128)(2,1)S(1)}, bf16[1024,256]{1,0:T(8,128)(2,1)}, u32[]{:S(2)}) copy-start(bf16[1024,256]{1,0:T(8,128)(2,1)} %constant.40.clone.table) | copy-start | bytes 1572868
  13.4 11.4 %copy-start.4 = (bf16[1024,256]{1,0:T(8,128)(2,1)S(1)}, bf16[1024,256]{1,0:T(8,128)(2,1)}, u32[]{:S(2)}) copy-start(bf16[1024,256]{1,0:T(8,128)(2,1)} %constant.40.clone.table) | copy-start | bytes 1572868
  17.2 14.8 %collective-permute-start.5 = (bf16[208,256]{1,0:T(8,128)(2,1)S(1)}, bf16[208,256]{1,0:T(8,128)(2,1)S(1)}, u32[]{:S(2)}, u32[]{:S(2)}) collective-permute-start(bf16[208,256]{1,0:T(8,128)(2,1)S(1)} %get-tuple-element.64), channel_id=1, source_target_pairs={{0,4},{1,5},{2,6},{3,7},{4,0},{5,1},{6,2},{7,3},{8,12},{9,13},{10,... | collective-permute-start | bytes 319496 | tf_op jit(solution)/shard_map/ppermute | solution.py:959
  17.2 16.7 %collective-permute-start.6 = (bf16[208,256]{1,0:T(8,128)(2,1)S(1)}, bf16[208,256]{1,0:T(8,128)(2,1)S(1)}, u32[]{:S(2)}, u32[]{:S(2)}) collective-permute-start(bf16[208,256]{1,0:T(8,128)(2,1)S(1)} %get-tuple-element.65), channel_id=1, source_target_pairs={{0,5},{1,4},{2,7},{3,6},{4,1},{5,0},{6,3},{7,2},{8,13},{9,12},{10,... | collective-permute-start | bytes 319496 | tf_op jit(solution)/shard_map/ppermute | solution.py:959
  20.1 14.8 %collective-permute-start.7 = (bf16[208,256]{1,0:T(8,128)(2,1)S(1)}, bf16[208,256]{1,0:T(8,128)(2,1)S(1)}, u32[]{:S(2)}, u32[]{:S(2)}) collective-permute-start(bf16[208,256]{1,0:T(8,128)(2,1)S(1)} %get-tuple-element.66), channel_id=1, source_target_pairs={{0,6},{1,7},{2,4},{3,5},{4,2},{5,3},{6,0},{7,1},{8,14},{9,15},{10,... | collective-permute-start | bytes 319496 | tf_op jit(solution)/shard_map/ppermute | solution.py:959
  21.8 13.2 %collective-permute-start.8 = (bf16[208,256]{1,0:T(8,128)(2,1)S(1)}, bf16[208,256]{1,0:T(8,128)(2,1)S(1)}, u32[]{:S(2)}, u32[]{:S(2)}) collective-permute-start(bf16[208,256]{1,0:T(8,128)(2,1)S(1)} %get-tuple-element.67), channel_id=1, source_target_pairs={{0,7},{1,6},{2,5},{3,4},{4,3},{5,2},{6,1},{7,0},{8,15},{9,14},{10,... | collective-permute-start | bytes 319496 | tf_op jit(solution)/shard_map/ppermute | solution.py:959
  24.9 15.0 %copy-start.6 = (bf16[1024,256]{1,0:T(8,128)(2,1)S(1)}, bf16[1024,256]{1,0:T(8,128)(2,1)}, u32[]{:S(2)}) copy-start(bf16[1024,256]{1,0:T(8,128)(2,1)} %constant.42.clone.rest_13_.rest_1_) | copy-start | bytes 1572868
  29.2 10.7 %copy-start = (bf16[2048,512]{1,0:T(8,128)(2,1)S(1)}, bf16[2048,512]{1,0:T(8,128)(2,1)}, u32[]{:S(2)}) copy-start(bf16[2048,512]{1,0:T(8,128)(2,1)} %constant.41.clone.rest_12_.rest_0_) | copy-start | bytes 6291460
  29.2 10.7 %copy-start.5 = (f32[512,256]{1,0:T(8,128)S(1)}, f32[512,256]{1,0:T(8,128)}, u32[]{:S(2)}) copy-start(f32[512,256]{1,0:T(8,128)} %constant.43.clone.rest_14_.rest_2_) | copy-start | bytes 1572868
  31.4 4.8 %collective-permute-start.2 = (bf16[208,256]{1,0:T(8,128)(2,1)S(1)}, bf16[208,256]{1,0:T(8,128)(2,1)S(1)}, u32[]{:S(2)}, u32[]{:S(2)}) collective-permute-start(bf16[208,256]{1,0:T(8,128)(2,1)S(1)} %get-tuple-element.61), channel_id=1, source_target_pairs={{0,1},{1,0},{2,3},{3,2},{4,5},{5,4},{6,7},{7,6},{8,9},{9,8},{10,11... | collective-permute-start | bytes 319496 | tf_op jit(solution)/shard_map/ppermute | solution.py:959
  32.0 5.5 %collective-permute-start.3 = (bf16[208,256]{1,0:T(8,128)(2,1)S(1)}, bf16[208,256]{1,0:T(8,128)(2,1)S(1)}, u32[]{:S(2)}, u32[]{:S(2)}) collective-permute-start(bf16[208,256]{1,0:T(8,128)(2,1)S(1)} %get-tuple-element.62), channel_id=1, source_target_pairs={{0,2},{1,3},{2,0},{3,1},{4,6},{5,7},{6,4},{7,5},{8,10},{9,11},{10,... | collective-permute-start | bytes 319496 | tf_op jit(solution)/shard_map/ppermute | solution.py:959
  33.9 6.0 %collective-permute-start.4 = (bf16[208,256]{1,0:T(8,128)(2,1)S(1)}, bf16[208,256]{1,0:T(8,128)(2,1)S(1)}, u32[]{:S(2)}, u32[]{:S(2)}) collective-permute-start(bf16[208,256]{1,0:T(8,128)(2,1)S(1)} %get-tuple-element.63), channel_id=1, source_target_pairs={{0,3},{1,2},{2,1},{3,0},{4,7},{5,6},{6,5},{7,4},{8,11},{9,10},{10,... | collective-permute-start | bytes 319496 | tf_op jit(solution)/shard_map/ppermute | solution.py:959
  44.0 6.4 %collective-permute-start.9 = (f32[8,128]{1,0:T(8,128)S(1)}, f32[8,128]{1,0:T(8,128)S(1)}, u32[]{:S(2)}, u32[]{:S(2)}) collective-permute-start(f32[8,128]{1,0:T(8,128)S(1)} %get-tuple-element.81), channel_id=1, source_target_pairs={{0,7},{1,2},{2,1},{3,4},{4,3},{5,6},{6,5},{7,0},{8,15},{9,10},{10,... | collective-permute-start | bytes 12296 | tf_op jit(solution)/shard_map/ppermute | solution.py:897
  46.4 4.0 %collective-permute-start.10 = (f32[8,128]{1,0:T(8,128)S(1)}, f32[8,128]{1,0:T(8,128)S(1)}, u32[]{:S(2)}, u32[]{:S(2)}) collective-permute-start(f32[8,128]{1,0:T(8,128)S(1)} %get-tuple-element.82), channel_id=1, source_target_pairs={{0,1},{1,0},{2,3},{3,2},{4,5},{5,4},{6,7},{7,6},{8,9},{9,8},{10,11... | collective-permute-start | bytes 12296 | tf_op jit(solution)/shard_map/ppermute | solution.py:897
  47.4 3.0 %collective-permute-start.11 = (f32[8,128]{1,0:T(8,128)S(1)}, f32[8,128]{1,0:T(8,128)S(1)}, u32[]{:S(2)}, u32[]{:S(2)}) collective-permute-start(f32[8,128]{1,0:T(8,128)S(1)} %get-tuple-element.83), channel_id=1, source_target_pairs={{0,24},{8,16},{16,8},{24,0},{1,25},{9,17},{17,9},{25,1},{2,26},{10... | collective-permute-start | bytes 12296 | tf_op jit(solution)/shard_map/ppermute | solution.py:897
  47.5 2.9 %collective-permute-start.12 = (f32[8,128]{1,0:T(8,128)S(1)}, f32[8,128]{1,0:T(8,128)S(1)}, u32[]{:S(2)}, u32[]{:S(2)}) collective-permute-start(f32[8,128]{1,0:T(8,128)S(1)} %get-tuple-element.84), channel_id=1, source_target_pairs={{0,8},{8,0},{16,24},{24,16},{1,9},{9,1},{17,25},{25,17},{2,10},{10... | collective-permute-start | bytes 12296 | tf_op jit(solution)/shard_map/ppermute | solution.py:897

commit v5 on v4

--- a/solution.py
+++ b/solution.py
@@ -650,7 +650,7 @@
     own = ids[1]
     count = half if coded else columns
     if coded:
-        sources = [(rest[s], (own ^ s) & (half - 1)) for s in range(half)]
+        sources = [(rest[half - 1 - s], (own ^ s) & (half - 1)) for s in range(half)]
         far, rest = rest[half : half + 8], rest[half + 8 :]
     else:
         sources = [(rest[0].at[s], s) for s in range(columns)]
@@ -1003,7 +1003,7 @@
             ],
             "far",
         )
-        arrived = [*arrived[:half], *far]
+        arrived = [*arrived[:half][::-1], *far]
     gathered_lines = pltpu.VMEM((edge_rows + 2 * HALO, tile), f32)
     residual, shaped, weight_x, rim_x, weight_y, row_pair, row_next, col_pair, col_next = call(
         functools.partial(tile_kernel, lines, tile_az, tile, columns, exchange),

time: 68.9 us -> 68.1 us (0.988)
  waiting for transfers between devices: 8.82 us -> 8.11 us
    ppermute x7, waiting for transfers between devices: 5.7 us -> 3.92 us  [shards(): lax.ppermute(sent[s], 'col', [(i, i ^ s) for i in range(columns)])]
    ppermute x7, starting transfers between devices: 9.34 us -> 10.8 us  [shards(): lax.ppermute(sent[s], 'col', [(i, i ^ s) for i in range(columns)])]
    ppermute x6, starting transfers between devices: 11.3 us -> 10.1 us  [swapped(): return lax.ppermute(value, axis, pairs)]
    ppermute x6, waiting for transfers between devices: 3.12 us -> 4.19 us  [swapped(): return lax.ppermute(value, axis, pairs)]
  transfers between devices with their start and end apart: 13 -> 13, of which waited for: 6 -> 5; matrix products, arithmetic and copies ran while one was open for 0% -> 0% of each run, Pallas kernels for 17% -> 17%
where the time goes in v5:
time: 68.1 us; the launch traced here: 67.9 us
  Pallas kernels  24.8 us (36%)
  starting transfers between devices  20.9 us (31%)
  blocking collectives  10.9 us (16%)
  waiting for transfers between devices  8.11 us (12%)
  local copies, waits for them, and re-layouts  2.21 us (3%)
  between operations  0.96 us (1%)
    pallas_call x6, Pallas kernels, call(): pl.pallas_call(body, out_shape=[jax.ShapeDtypeStruct(s, d) for s, d in ou...  16.3 us
    all_to_all x1, blocking collectives, shards(): gathered = lax.all_to_all(spread, axes, 0, 0, tiled=True)  10.9 us
    ppermute x7, starting transfers between devices, shards(): lax.ppermute(sent[s], 'col', [(i, i ^ s) for i in range(columns)])  10.8 us
    ppermute x6, starting transfers between devices, swapped(): return lax.ppermute(value, axis, pairs)  10.1 us
    pallas_call x2, Pallas kernels, interior(): pl.pallas_call(body, out_shape=[jax.ShapeDtypeStruct(s, d) for s, d in ou...  8.42 us
    ppermute x6, waiting for transfers between devices, swapped(): return lax.ppermute(value, axis, pairs)  4.19 us
    ppermute x7, waiting for transfers between devices, shards(): lax.ppermute(sent[s], 'col', [(i, i ^ s) for i in range(columns)])  3.92 us
  transfers between devices with their start and end apart: 13, of which 5 were waited for; matrix products, arithmetic and copies ran while one was open for 0% of the time, Pallas kernels for 17%

profile of v5, /device:TPU:0, one launch (start us, length us, event | category | flops | bytes accessed | tf_op | source)
XLA Modules:
  0.0 67.9 jit_solution(8093092220729292317)
XLA Ops:
  0.7 1.0 %fusion = (bf16[2,8,2048]{2,1,0:T(8,128)(2,1)S(1)}, bf16[2,8,2048]{2,1,0:T(8,128)(2,1)S(1)}, bf16[2,8,2048]{2,1,0:T(8,128)(2,1)S(1)}, bf16[2,8,2048]{2,1,0:T(8,128)(2,1)S(1)}) fusion(bf16[2,64,2048]{2,1,0:T(8,128)(2,1)} %first.2, bf16[2,64,2048]{2,1,0:T(8,128)(2,1)} %second.2), kind=kLoop, calls=%fused_computation.4 | loop fusion | bytes 524288 | tf_op jit(solution)/shard_map/slice | solution.py:910
  1.7 6.4 %collective-permute-start.1 = (bf16[4,8,2048]{2,1,0:T(8,128)(2,1)S(1)}, bf16[4,8,2048]{2,1,0:T(8,128)(2,1)S(1)}, u32[]{:S(2)}, u32[]{:S(2)}) collective-permute-start(bf16[4,8,2048]{2,1,0:T(8,128)(2,1)S(1)} %get-tuple-element.94), channel_id=1, source_target_pairs={{0,31},{1,2},{2,1},{3,4},{4,3},{5,6},{6,5},{7,8},{8,7},{9,10},{10,... | collective-permute-start | bytes 393224 | tf_op jit(solution)/shard_map/ppermute | solution.py:897
  8.3 1.0 %copy-done.3 = bf16[1024,256]{1,0:T(8,128)(2,1)S(1)} copy-done((bf16[1024,256]{1,0:T(8,128)(2,1)S(1)}, bf16[1024,256]{1,0:T(8,128)(2,1)}, u32[]{:S(2)}) %copy-start.3) | copy-done | bytes 524312
  9.3 4.1 %interior.2 = (f32[4,64,1280]{2,1,0:T(8,128)S(1)}, f32[2,48,1280]{2,1,0:T(8,128)S(1)}, bf16[3,32,1280]{2,1,0:T(8,128)(2,1)S(1)}, f32[4,8,128]{2,1,0:T(8,128)S(1)}) custom-call(s32[6]{0:T(128)S(1)} %stack.23.ids, bf16[2,64,2048]{2,1,0:T(8,128)(2,1)S(1)} %copy-done.1, bf16[2,64,2048]{2,1,0:T(8,128)(2,1)S(1)} %copy-done.2, bf16[1024,256]{1,0:T(8,128)(2,1)S(1)} %copy-done.3), custom_call_target="tpu_custom_call" | custom-call | flops 8000000 | bytes 4000000 | tf_op jit(solution)/shard_map/interior/pallas_call | solution.py:151
  13.5 1.5 %collective-permute-done.from_pair = bf16[4,8,2048]{2,1,0:T(8,128)(2,1)S(1)} collective-permute-done((bf16[4,8,2048]{2,1,0:T(8,128)(2,1)S(1)}, bf16[4,8,2048]{2,1,0:T(8,128)(2,1)S(1)}, u32[]{:S(2)}, u32[]{:S(2)}) %collective-permute-start) | collective-permute-done | bytes 131104 | tf_op jit(solution)/shard_map/ppermute | solution.py:897
  15.0 2.2 %borders.2 = (bf16[208,256]{1,0:T(8,128)(2,1)S(1)}, bf16[208,256]{1,0:T(8,128)(2,1)S(1)}, bf16[208,256]{1,0:T(8,128)(2,1)S(1)}, bf16[208,256]{1,0:T(8,128)(2,1)S(1)}) custom-call(s32[6]{0:T(128)S(1)} %stack.23.ids, f32[4,64,1280]{2,1,0:T(8,128)S(1)} %get-tuple-element.46.ranged, f32[2,48,1280]{2,1,0:T(8,128)S(1)} %get-tuple-element.47.inside_field, ...), custom_call_target="tpu_custom_call" | custom-call | flops 1000000 | bytes 4000000 | tf_op jit(solution)/shard_map/borders/pallas_call | solution.py:138
  17.2 2.9 %collective-permute-start.6 = (bf16[208,256]{1,0:T(8,128)(2,1)S(1)}, bf16[208,256]{1,0:T(8,128)(2,1)S(1)}, u32[]{:S(2)}, u32[]{:S(2)}) collective-permute-start(bf16[208,256]{1,0:T(8,128)(2,1)S(1)} %get-tuple-element.65), channel_id=1, source_target_pairs={{0,5},{1,4},{2,7},{3,6},{4,1},{5,0},{6,3},{7,2},{8,13},{9,12},{10,... | collective-permute-start | bytes 319496 | tf_op jit(solution)/shard_map/ppermute | solution.py:959
  20.1 1.7 %collective-permute-start.7 = (bf16[208,256]{1,0:T(8,128)(2,1)S(1)}, bf16[208,256]{1,0:T(8,128)(2,1)S(1)}, u32[]{:S(2)}, u32[]{:S(2)}) collective-permute-start(bf16[208,256]{1,0:T(8,128)(2,1)S(1)} %get-tuple-element.66), channel_id=1, source_target_pairs={{0,6},{1,7},{2,4},{3,5},{4,2},{5,3},{6,0},{7,1},{8,14},{9,15},{10,... | collective-permute-start | bytes 319496 | tf_op jit(solution)/shard_map/ppermute | solution.py:959
  21.8 3.1 %collective-permute-start.8 = (bf16[208,256]{1,0:T(8,128)(2,1)S(1)}, bf16[208,256]{1,0:T(8,128)(2,1)S(1)}, u32[]{:S(2)}, u32[]{:S(2)}) collective-permute-start(bf16[208,256]{1,0:T(8,128)(2,1)S(1)} %get-tuple-element.67), channel_id=1, source_target_pairs={{0,7},{1,6},{2,5},{3,4},{4,3},{5,2},{6,1},{7,0},{8,15},{9,14},{10,... | collective-permute-start | bytes 319496 | tf_op jit(solution)/shard_map/ppermute | solution.py:959
  24.9 4.3 %interior.3 = (f32[4,64,1280]{2,1,0:T(8,128)S(1)}, f32[2,48,1280]{2,1,0:T(8,128)S(1)}, bf16[3,32,1280]{2,1,0:T(8,128)(2,1)S(1)}, f32[4,8,128]{2,1,0:T(8,128)S(1)}) custom-call(s32[6]{0:T(128)S(1)} %stack.23.ids, bf16[2,64,2048]{2,1,0:T(8,128)(2,1)S(1)} %copy-done.1, bf16[2,64,2048]{2,1,0:T(8,128)(2,1)S(1)} %copy-done.2, bf16[1024,256]{1,0:T(8,128)(2,1)S(1)} %copy-done.4), custom_call_target="tpu_custom_call" | custom-call | flops 8000000 | bytes 4000000 | tf_op jit(solution)/shard_map/interior/pallas_call | solution.py:151
  29.2 2.2 %borders.3 = (bf16[208,256]{1,0:T(8,128)(2,1)S(1)}, bf16[208,256]{1,0:T(8,128)(2,1)S(1)}, bf16[208,256]{1,0:T(8,128)(2,1)S(1)}, bf16[208,256]{1,0:T(8,128)(2,1)S(1)}) custom-call(s32[6]{0:T(128)S(1)} %stack.23.ids, f32[4,64,1280]{2,1,0:T(8,128)S(1)} %get-tuple-element.56.ranged, f32[2,48,1280]{2,1,0:T(8,128)S(1)} %get-tuple-element.57.inside_field, ...), custom_call_target="tpu_custom_call" | custom-call | flops 1000000 | bytes 4000000 | tf_op jit(solution)/shard_map/borders/pallas_call | solution.py:138
  31.5 2.0 %collective-permute-start.3 = (bf16[208,256]{1,0:T(8,128)(2,1)S(1)}, bf16[208,256]{1,0:T(8,128)(2,1)S(1)}, u32[]{:S(2)}, u32[]{:S(2)}) collective-permute-start(bf16[208,256]{1,0:T(8,128)(2,1)S(1)} %get-tuple-element.61), channel_id=1, source_target_pairs={{0,2},{1,3},{2,0},{3,1},{4,6},{5,7},{6,4},{7,5},{8,10},{9,11},{10,... | collective-permute-start | bytes 319496 | tf_op jit(solution)/shard_map/ppermute | solution.py:959
  33.9 1.0 %collective-permute-start.4 = (bf16[208,256]{1,0:T(8,128)(2,1)S(1)}, bf16[208,256]{1,0:T(8,128)(2,1)S(1)}, u32[]{:S(2)}, u32[]{:S(2)}) collective-permute-start(bf16[208,256]{1,0:T(8,128)(2,1)S(1)} %get-tuple-element.62), channel_id=1, source_target_pairs={{0,1},{1,0},{2,3},{3,2},{4,5},{5,4},{6,7},{7,6},{8,9},{9,8},{10,11... | collective-permute-start | bytes 319496 | tf_op jit(solution)/shard_map/ppermute | solution.py:959
  35.0 1.2 %far.1 = (f32[256,256]{1,0:T(8,128)S(1)}, f32[256,256]{1,0:T(8,128)S(1)}, f32[256,128]{1,0:T(8,128)S(1)}, f32[256,128]{1,0:T(8,128)S(1)}, f32[256,256]{1,0:T(8,1...) custom-call(s32[6]{0:T(128)S(1)} %stack.23.ids, ...), custom_call_target="tpu_custom_call" | custom-call | flops 1000000 | bytes 4000000 | tf_op jit(solution)/shard_map/far/pallas_call | solution.py:138
  36.2 1.3 %collective-permute-done.2.rest_0_ = bf16[208,256]{1,0:T(8,128)(2,1)S(1)} collective-permute-done((bf16[208,256]{1,0:T(8,128)(2,1)S(1)}, bf16[208,256]{1,0:T(8,128)(2,1)S(1)}, u32[]{:S(2)}, u32[]{:S(2)}) %collective-permute-start.2) | collective-permute-done | bytes 106528 | tf_op jit(solution)/shard_map/ppermute | solution.py:959
  37.4 2.2 %collective-permute-done.4.rest_2_ = bf16[208,256]{1,0:T(8,128)(2,1)S(1)} collective-permute-done((bf16[208,256]{1,0:T(8,128)(2,1)S(1)}, bf16[208,256]{1,0:T(8,128)(2,1)S(1)}, u32[]{:S(2)}, u32[]{:S(2)}) %collective-permute-start.4) | collective-permute-done | bytes 106528 | tf_op jit(solution)/shard_map/ppermute | solution.py:959
  39.6 4.1 %tiles.1 = (f32[512,256]{1,0:T(8,128)S(1)}, f32[512,256]{1,0:T(8,128)S(1)}, f32[512,256]{1,0:T(8,128)S(1)}, f32[512,128]{1,0:T(8,128)S(1)}, f32[520,256]{1,0:T(8...) custom-call(s32[6]{0:T(128)S(1)} %stack.23.ids, ...), custom_call_target="tpu_custom_call" | custom-call | flops 1000000 | bytes 4000000 | tf_op jit(solution)/shard_map/tiles/pallas_call | solution.py:138
  43.7 2.0 %collective-permute-start.9 = (f32[8,128]{1,0:T(8,128)S(1)}, f32[8,128]{1,0:T(8,128)S(1)}, u32[]{:S(2)}, u32[]{:S(2)}) collective-permute-start(f32[8,128]{1,0:T(8,128)S(1)} %get-tuple-element.81), channel_id=1, source_target_pairs={{0,7},{1,2},{2,1},{3,4},{4,3},{5,6},{6,5},{7,0},{8,15},{9,10},{10,... | collective-permute-start | bytes 12296 | tf_op jit(solution)/shard_map/ppermute | solution.py:897
  45.7 0.5 collective-permute-start.10
  46.3 1.1 %collective-permute-start.12 = (f32[8,128]{1,0:T(8,128)S(1)}, f32[8,128]{1,0:T(8,128)S(1)}, u32[]{:S(2)}, u32[]{:S(2)}) collective-permute-start(f32[8,128]{1,0:T(8,128)S(1)} %get-tuple-element.84), channel_id=1, source_target_pairs={{0,8},{8,0},{16,24},{24,16},{1,9},{9,1},{17,25},{25,17},{2,10},{10... | collective-permute-start | bytes 12296 | tf_op jit(solution)/shard_map/ppermute | solution.py:897
  47.4 2.7 %collective-permute-done.9.col_next = f32[8,128]{1,0:T(8,128)S(1)} collective-permute-done((f32[8,128]{1,0:T(8,128)S(1)}, f32[8,128]{1,0:T(8,128)S(1)}, u32[]{:S(2)}, u32[]{:S(2)}) %collective-permute-start.9) | collective-permute-done | bytes 4128 | tf_op jit(solution)/shard_map/ppermute | solution.py:897
  50.1 4.6 %operator.1 = (f32[512,256]{1,0:T(8,128)S(1)}, f32[512,256]{1,0:T(8,128)S(1)}, f32[512,256]{1,0:T(8,128)S(1)}, bf16[16,128]{1,0:T(8,128)(2,1)S(1)}, f32[16,128]{1,0:T(8,128)S(1)}) custom-call(s32[6]{0:T(128)S(1)} %stack.23.ids, f32[512,256]{1,0:T(8,128)S(1)} %get-tuple-element.76.residual, f32[512,256]{1,0:T(8,128)S(1)} %get-tuple-element.77.shaped, ...), custom_call_target="tpu_custom_call" | custom-call | flops 1000000 | bytes 4000000 | tf_op jit(solution)/shard_map/operator/pallas_call | solution.py:138
  54.7 10.9 %all_to_all.5.gathered = bf16[32,16,128]{2,1,0:T(8,128)(2,1)S(1)} all-to-all(bf16[32,16,128]{2,1,0:T(8,128)(2,1)S(1)} %broadcast_in_dim.2), channel_id=1, replica_groups=mesh['row'=4,'col'=8] {'row','col'}, dimensions={0} | all-to-all | bytes 262144 | tf_op jit(solution)/shard_map/all_to_all | solution.py:1036
  65.6 2.1 %finish.1 = (f32[512,256]{1,0:T(8,128)}, f32[512,256]{1,0:T(8,128)}) custom-call(s32[6]{0:T(128)S(1)} %stack.23.ids, bf16[32,16,128]{2,1,0:T(8,128)(2,1)S(1)} %all_to_all.5.gathered, f32[512,256]{1,0:T(8,128)S(1)} %get-tuple-element.76.residual, f32[512,256]{1,0:T(8,128)S(1)} %get-tuple-element.77.shaped, f32[512,256]{1,0:T(8,128)S(1)} %get-tuple-element.86.operated, ...), custom_call_target="tpu_custom_call" | custom-call | flops 1000000 | bytes 4000000 | tf_op jit(solution)/shard_map/finish/pallas_call | solution.py:138
  (29 shorter events, 0.9 us)
Async XLA Ops:
  0.6 7.6 %copy-start.2 = (bf16[2,64,2048]{2,1,0:T(8,128)(2,1)S(1)}, bf16[2,64,2048]{2,1,0:T(8,128)(2,1)}, u32[]{:S(2)}) copy-start(bf16[2,64,2048]{2,1,0:T(8,128)(2,1)} %second.2) | copy-start | bytes 1572868
  0.6 7.6 %copy-start.1 = (bf16[2,64,2048]{2,1,0:T(8,128)(2,1)S(1)}, bf16[2,64,2048]{2,1,0:T(8,128)(2,1)}, u32[]{:S(2)}) copy-start(bf16[2,64,2048]{2,1,0:T(8,128)(2,1)} %first.2) | copy-start | bytes 1572868
  1.7 11.7 %collective-permute-start.1 = (bf16[4,8,2048]{2,1,0:T(8,128)(2,1)S(1)}, bf16[4,8,2048]{2,1,0:T(8,128)(2,1)S(1)}, u32[]{:S(2)}, u32[]{:S(2)}) collective-permute-start(bf16[4,8,2048]{2,1,0:T(8,128)(2,1)S(1)} %get-tuple-element.94), channel_id=1, source_target_pairs={{0,31},{1,2},{2,1},{3,4},{4,3},{5,6},{6,5},{7,8},{8,7},{9,10},{10,... | collective-permute-start | bytes 393224 | tf_op jit(solution)/shard_map/ppermute | solution.py:897
  8.2 6.8 %collective-permute-start = (bf16[4,8,2048]{2,1,0:T(8,128)(2,1)S(1)}, bf16[4,8,2048]{2,1,0:T(8,128)(2,1)S(1)}, u32[]{:S(2)}, u32[]{:S(2)}) collective-permute-start(bf16[4,8,2048]{2,1,0:T(8,128)(2,1)S(1)} %get-tuple-element.95), channel_id=1, source_target_pairs={{0,1},{1,0},{2,3},{3,2},{4,5},{5,4},{6,7},{7,6},{8,9},{9,8},{10,11... | collective-permute-start | bytes 393224 | tf_op jit(solution)/shard_map/ppermute | solution.py:897
  8.3 1.0 %copy-start.3 = (bf16[1024,256]{1,0:T(8,128)(2,1)S(1)}, bf16[1024,256]{1,0:T(8,128)(2,1)}, u32[]{:S(2)}) copy-start(bf16[1024,256]{1,0:T(8,128)(2,1)} %constant.40.clone.table) | copy-start | bytes 1572868
  13.4 11.4 %copy-start.4 = (bf16[1024,256]{1,0:T(8,128)(2,1)S(1)}, bf16[1024,256]{1,0:T(8,128)(2,1)}, u32[]{:S(2)}) copy-start(bf16[1024,256]{1,0:T(8,128)(2,1)} %constant.40.clone.table) | copy-start | bytes 1572868
  17.2 14.3 %collective-permute-start.5 = (bf16[208,256]{1,0:T(8,128)(2,1)S(1)}, bf16[208,256]{1,0:T(8,128)(2,1)S(1)}, u32[]{:S(2)}, u32[]{:S(2)}) collective-permute-start(bf16[208,256]{1,0:T(8,128)(2,1)S(1)} %get-tuple-element.64), channel_id=1, source_target_pairs={{0,4},{1,5},{2,6},{3,7},{4,0},{5,1},{6,2},{7,3},{8,12},{9,13},{10,... | collective-permute-start | bytes 319496 | tf_op jit(solution)/shard_map/ppermute | solution.py:959
  17.2 16.7 %collective-permute-start.6 = (bf16[208,256]{1,0:T(8,128)(2,1)S(1)}, bf16[208,256]{1,0:T(8,128)(2,1)S(1)}, u32[]{:S(2)}, u32[]{:S(2)}) collective-permute-start(bf16[208,256]{1,0:T(8,128)(2,1)S(1)} %get-tuple-element.65), channel_id=1, source_target_pairs={{0,5},{1,4},{2,7},{3,6},{4,1},{5,0},{6,3},{7,2},{8,13},{9,12},{10,... | collective-permute-start | bytes 319496 | tf_op jit(solution)/shard_map/ppermute | solution.py:959
  20.1 14.8 %collective-permute-start.7 = (bf16[208,256]{1,0:T(8,128)(2,1)S(1)}, bf16[208,256]{1,0:T(8,128)(2,1)S(1)}, u32[]{:S(2)}, u32[]{:S(2)}) collective-permute-start(bf16[208,256]{1,0:T(8,128)(2,1)S(1)} %get-tuple-element.66), channel_id=1, source_target_pairs={{0,6},{1,7},{2,4},{3,5},{4,2},{5,3},{6,0},{7,1},{8,14},{9,15},{10,... | collective-permute-start | bytes 319496 | tf_op jit(solution)/shard_map/ppermute | solution.py:959
  21.8 13.2 %collective-permute-start.8 = (bf16[208,256]{1,0:T(8,128)(2,1)S(1)}, bf16[208,256]{1,0:T(8,128)(2,1)S(1)}, u32[]{:S(2)}, u32[]{:S(2)}) collective-permute-start(bf16[208,256]{1,0:T(8,128)(2,1)S(1)} %get-tuple-element.67), channel_id=1, source_target_pairs={{0,7},{1,6},{2,5},{3,4},{4,3},{5,2},{6,1},{7,0},{8,15},{9,14},{10,... | collective-permute-start | bytes 319496 | tf_op jit(solution)/shard_map/ppermute | solution.py:959
  24.9 14.7 %copy-start.6 = (bf16[1024,256]{1,0:T(8,128)(2,1)S(1)}, bf16[1024,256]{1,0:T(8,128)(2,1)}, u32[]{:S(2)}) copy-start(bf16[1024,256]{1,0:T(8,128)(2,1)} %constant.42.clone.rest_13_.rest_1_) | copy-start | bytes 1572868
  29.2 10.4 %copy-start = (bf16[2048,512]{1,0:T(8,128)(2,1)S(1)}, bf16[2048,512]{1,0:T(8,128)(2,1)}, u32[]{:S(2)}) copy-start(bf16[2048,512]{1,0:T(8,128)(2,1)} %constant.41.clone.rest_12_.rest_0_) | copy-start | bytes 6291460
  29.2 10.4 %copy-start.5 = (f32[512,256]{1,0:T(8,128)S(1)}, f32[512,256]{1,0:T(8,128)}, u32[]{:S(2)}) copy-start(f32[512,256]{1,0:T(8,128)} %constant.43.clone.rest_14_.rest_2_) | copy-start | bytes 1572868
  31.4 6.0 %collective-permute-start.2 = (bf16[208,256]{1,0:T(8,128)(2,1)S(1)}, bf16[208,256]{1,0:T(8,128)(2,1)S(1)}, u32[]{:S(2)}, u32[]{:S(2)}) collective-permute-start(bf16[208,256]{1,0:T(8,128)(2,1)S(1)} %get-tuple-element.60), channel_id=1, source_target_pairs={{0,3},{1,2},{2,1},{3,0},{4,7},{5,6},{6,5},{7,4},{8,11},{9,10},{10,... | collective-permute-start | bytes 319496 | tf_op jit(solution)/shard_map/ppermute | solution.py:959
  31.5 5.9 %collective-permute-start.3 = (bf16[208,256]{1,0:T(8,128)(2,1)S(1)}, bf16[208,256]{1,0:T(8,128)(2,1)S(1)}, u32[]{:S(2)}, u32[]{:S(2)}) collective-permute-start(bf16[208,256]{1,0:T(8,128)(2,1)S(1)} %get-tuple-element.61), channel_id=1, source_target_pairs={{0,2},{1,3},{2,0},{3,1},{4,6},{5,7},{6,4},{7,5},{8,10},{9,11},{10,... | collective-permute-start | bytes 319496 | tf_op jit(solution)/shard_map/ppermute | solution.py:959
  33.9 5.7 %collective-permute-start.4 = (bf16[208,256]{1,0:T(8,128)(2,1)S(1)}, bf16[208,256]{1,0:T(8,128)(2,1)S(1)}, u32[]{:S(2)}, u32[]{:S(2)}) collective-permute-start(bf16[208,256]{1,0:T(8,128)(2,1)S(1)} %get-tuple-element.62), channel_id=1, source_target_pairs={{0,1},{1,0},{2,3},{3,2},{4,5},{5,4},{6,7},{7,6},{8,9},{9,8},{10,11... | collective-permute-start | bytes 319496 | tf_op jit(solution)/shard_map/ppermute | solution.py:959
  43.7 6.4 %collective-permute-start.9 = (f32[8,128]{1,0:T(8,128)S(1)}, f32[8,128]{1,0:T(8,128)S(1)}, u32[]{:S(2)}, u32[]{:S(2)}) collective-permute-start(f32[8,128]{1,0:T(8,128)S(1)} %get-tuple-element.81), channel_id=1, source_target_pairs={{0,7},{1,2},{2,1},{3,4},{4,3},{5,6},{6,5},{7,0},{8,15},{9,10},{10,... | collective-permute-start | bytes 12296 | tf_op jit(solution)/shard_map/ppermute | solution.py:897
  45.7 4.4 %collective-permute-start.10 = (f32[8,128]{1,0:T(8,128)S(1)}, f32[8,128]{1,0:T(8,128)S(1)}, u32[]{:S(2)}, u32[]{:S(2)}) collective-permute-start(f32[8,128]{1,0:T(8,128)S(1)} %get-tuple-element.82), channel_id=1, source_target_pairs={{0,1},{1,0},{2,3},{3,2},{4,5},{5,4},{6,7},{7,6},{8,9},{9,8},{10,11... | collective-permute-start | bytes 12296 | tf_op jit(solution)/shard_map/ppermute | solution.py:897
  46.1 3.9 %collective-permute-start.11 = (f32[8,128]{1,0:T(8,128)S(1)}, f32[8,128]{1,0:T(8,128)S(1)}, u32[]{:S(2)}, u32[]{:S(2)}) collective-permute-start(f32[8,128]{1,0:T(8,128)S(1)} %get-tuple-element.83), channel_id=1, source_target_pairs={{0,24},{8,16},{16,8},{24,0},{1,25},{9,17},{17,9},{25,1},{2,26},{10... | collective-permute-start | bytes 12296 | tf_op jit(solution)/shard_map/ppermute | solution.py:897
  46.3 3.8 %collective-permute-start.12 = (f32[8,128]{1,0:T(8,128)S(1)}, f32[8,128]{1,0:T(8,128)S(1)}, u32[]{:S(2)}, u32[]{:S(2)}) collective-permute-start(f32[8,128]{1,0:T(8,128)S(1)} %get-tuple-element.84), channel_id=1, source_target_pairs={{0,8},{8,0},{16,24},{24,16},{1,9},{9,1},{17,25},{25,17},{2,10},{10... | collective-permute-start | bytes 12296 | tf_op jit(solution)/shard_map/ppermute | solution.py:897

commit v6 on v5

--- a/solution.py
+++ b/solution.py
@@ -304,7 +304,7 @@
     return block
 
 
-def border_kernel(lines, width, tile, columns, across, ids, ranged, inside_field, codes, rims, from_pair, from_next, *rest):
+def border_kernel(lines, width, tile, columns, across, ids, ranged, inside_field, codes, rims, from_next, from_pair, *rest):
     half = columns // 2
     outs, (prod, seg, field, ends) = rest[:half], rest[half:]
     own = ids[1]
@@ -939,7 +939,7 @@
             part = call(
                 functools.partial(border_kernel, lines, width, tile, columns, across),
                 [((3 * lines + 16, tile), bf16)] * half,
-                (ids, ranged, inner, codes, rims, from_pair, from_next),
+                (ids, ranged, inner, codes, rims, from_next, from_pair),
                 [
                     pltpu.VMEM((4, HALO, width + 4 * LANES), f32),
                     pltpu.VMEM((2, 4, 3 * HALO, span), f32),

time: 68.1 us -> 67.4 us (0.990)
  waiting for transfers between devices: 8.11 us -> 5.75 us
  starting transfers between devices: 20.9 us -> 21.9 us
  blocking collectives: 10.9 us -> 11.6 us
    ppermute x6, waiting for transfers between devices: 4.19 us -> 2.17 us  [swapped(): return lax.ppermute(value, axis, pairs)]
    ppermute x6, starting transfers between devices: 10.1 us -> 11.6 us  [swapped(): return lax.ppermute(value, axis, pairs)]
    all_to_all x1, blocking collectives: 10.9 us -> 11.6 us  [shards(): gathered = lax.all_to_all(spread, axes, 0, 0, tiled=True)]
  transfers between devices with their start and end apart: 13 -> 13, of which waited for: 5 -> 7; matrix products, arithmetic and copies ran while one was open for 0% -> 0% of each run, Pallas kernels for 17% -> 18%
where the time goes in v6:
time: 67.4 us; the launch traced here: 67.2 us
  Pallas kernels  24.7 us (37%)
  starting transfers between devices  21.9 us (32%)
  blocking collectives  11.6 us (17%)
  waiting for transfers between devices  5.75 us (9%)
  local copies, waits for them, and re-layouts  2.21 us (3%)
  between operations  0.96 us (1%)
    pallas_call x6, Pallas kernels, call(): pl.pallas_call(body, out_shape=[jax.ShapeDtypeStruct(s, d) for s, d in ou...  16.3 us
    all_to_all x1, blocking collectives, shards(): gathered = lax.all_to_all(spread, axes, 0, 0, tiled=True)  11.6 us
    ppermute x6, starting transfers between devices, swapped(): return lax.ppermute(value, axis, pairs)  11.6 us
    ppermute x7, starting transfers between devices, shards(): lax.ppermute(sent[s], 'col', [(i, i ^ s) for i in range(columns)])  10.3 us
    pallas_call x2, Pallas kernels, interior(): pl.pallas_call(body, out_shape=[jax.ShapeDtypeStruct(s, d) for s, d in ou...  8.41 us
    ppermute x7, waiting for transfers between devices, shards(): lax.ppermute(sent[s], 'col', [(i, i ^ s) for i in range(columns)])  3.59 us
    ppermute x6, waiting for transfers between devices, swapped(): return lax.ppermute(value, axis, pairs)  2.17 us
  transfers between devices with their start and end apart: 13, of which 7 were waited for; matrix products, arithmetic and copies ran while one was open for 0% of the time, Pallas kernels for 18%

profile of v6, /device:TPU:0, one launch (start us, length us, event | category | flops | bytes accessed | tf_op | source)
XLA Modules:
  0.0 67.2 jit_solution(9293495554089720046)
XLA Ops:
  0.7 1.0 %fusion = (bf16[2,8,2048]{2,1,0:T(8,128)(2,1)S(1)}, bf16[2,8,2048]{2,1,0:T(8,128)(2,1)S(1)}, bf16[2,8,2048]{2,1,0:T(8,128)(2,1)S(1)}, bf16[2,8,2048]{2,1,0:T(8,128)(2,1)S(1)}) fusion(bf16[2,64,2048]{2,1,0:T(8,128)(2,1)} %first.2, bf16[2,64,2048]{2,1,0:T(8,128)(2,1)} %second.2), kind=kLoop, calls=%fused_computation.4 | loop fusion | bytes 524288 | tf_op jit(solution)/shard_map/slice | solution.py:911
  1.7 3.0 %collective-permute-start.1 = (bf16[4,8,2048]{2,1,0:T(8,128)(2,1)S(1)}, bf16[4,8,2048]{2,1,0:T(8,128)(2,1)S(1)}, u32[]{:S(2)}, u32[]{:S(2)}) collective-permute-start(bf16[4,8,2048]{2,1,0:T(8,128)(2,1)S(1)} %get-tuple-element.94), channel_id=1, source_target_pairs={{0,1},{1,0},{2,3},{3,2},{4,5},{5,4},{6,7},{7,6},{8,9},{9,8},{10,11... | collective-permute-start | bytes 393224 | tf_op jit(solution)/shard_map/ppermute | solution.py:897
  4.8 3.6 %collective-permute-start = (bf16[4,8,2048]{2,1,0:T(8,128)(2,1)S(1)}, bf16[4,8,2048]{2,1,0:T(8,128)(2,1)S(1)}, u32[]{:S(2)}, u32[]{:S(2)}) collective-permute-start(bf16[4,8,2048]{2,1,0:T(8,128)(2,1)S(1)} %get-tuple-element.95), channel_id=1, source_target_pairs={{0,31},{1,2},{2,1},{3,4},{4,3},{5,6},{6,5},{7,8},{8,7},{9,10},{10,... | collective-permute-start | bytes 393224 | tf_op jit(solution)/shard_map/ppermute | solution.py:897
  8.5 1.0 %copy-done.3 = bf16[1024,256]{1,0:T(8,128)(2,1)S(1)} copy-done((bf16[1024,256]{1,0:T(8,128)(2,1)S(1)}, bf16[1024,256]{1,0:T(8,128)(2,1)}, u32[]{:S(2)}) %copy-start.3) | copy-done | bytes 524312
  9.5 4.1 %interior.2 = (f32[4,64,1280]{2,1,0:T(8,128)S(1)}, f32[2,48,1280]{2,1,0:T(8,128)S(1)}, bf16[3,32,1280]{2,1,0:T(8,128)(2,1)S(1)}, f32[4,8,128]{2,1,0:T(8,128)S(1)}) custom-call(s32[6]{0:T(128)S(1)} %stack.23.ids, bf16[2,64,2048]{2,1,0:T(8,128)(2,1)S(1)} %copy-done.1, bf16[2,64,2048]{2,1,0:T(8,128)(2,1)S(1)} %copy-done.2, bf16[1024,256]{1,0:T(8,128)(2,1)S(1)} %copy-done.3), custom_call_target="tpu_custom_call" | custom-call | flops 8000000 | bytes 4000000 | tf_op jit(solution)/shard_map/interior/pallas_call | solution.py:151
  13.9 2.2 %borders.2 = (bf16[208,256]{1,0:T(8,128)(2,1)S(1)}, bf16[208,256]{1,0:T(8,128)(2,1)S(1)}, bf16[208,256]{1,0:T(8,128)(2,1)S(1)}, bf16[208,256]{1,0:T(8,128)(2,1)S(1)}) custom-call(s32[6]{0:T(128)S(1)} %stack.23.ids, f32[4,64,1280]{2,1,0:T(8,128)S(1)} %get-tuple-element.46.ranged, f32[2,48,1280]{2,1,0:T(8,128)S(1)} %get-tuple-element.47.inside_field, ...), custom_call_target="tpu_custom_call" | custom-call | flops 1000000 | bytes 4000000 | tf_op jit(solution)/shard_map/borders/pallas_call | solution.py:138
  16.2 1.5 %collective-permute-start.6 = (bf16[208,256]{1,0:T(8,128)(2,1)S(1)}, bf16[208,256]{1,0:T(8,128)(2,1)S(1)}, u32[]{:S(2)}, u32[]{:S(2)}) collective-permute-start(bf16[208,256]{1,0:T(8,128)(2,1)S(1)} %get-tuple-element.65), channel_id=1, source_target_pairs={{0,5},{1,4},{2,7},{3,6},{4,1},{5,0},{6,3},{7,2},{8,13},{9,12},{10,... | collective-permute-start | bytes 319496 | tf_op jit(solution)/shard_map/ppermute | solution.py:959
  17.7 3.8 %collective-permute-start.7 = (bf16[208,256]{1,0:T(8,128)(2,1)S(1)}, bf16[208,256]{1,0:T(8,128)(2,1)S(1)}, u32[]{:S(2)}, u32[]{:S(2)}) collective-permute-start(bf16[208,256]{1,0:T(8,128)(2,1)S(1)} %get-tuple-element.66), channel_id=1, source_target_pairs={{0,6},{1,7},{2,4},{3,5},{4,2},{5,3},{6,0},{7,1},{8,14},{9,15},{10,... | collective-permute-start | bytes 319496 | tf_op jit(solution)/shard_map/ppermute | solution.py:959
  21.5 2.3 %collective-permute-start.8 = (bf16[208,256]{1,0:T(8,128)(2,1)S(1)}, bf16[208,256]{1,0:T(8,128)(2,1)S(1)}, u32[]{:S(2)}, u32[]{:S(2)}) collective-permute-start(bf16[208,256]{1,0:T(8,128)(2,1)S(1)} %get-tuple-element.67), channel_id=1, source_target_pairs={{0,7},{1,6},{2,5},{3,4},{4,3},{5,2},{6,1},{7,0},{8,15},{9,14},{10,... | collective-permute-start | bytes 319496 | tf_op jit(solution)/shard_map/ppermute | solution.py:959
  23.8 4.3 %interior.3 = (f32[4,64,1280]{2,1,0:T(8,128)S(1)}, f32[2,48,1280]{2,1,0:T(8,128)S(1)}, bf16[3,32,1280]{2,1,0:T(8,128)(2,1)S(1)}, f32[4,8,128]{2,1,0:T(8,128)S(1)}) custom-call(s32[6]{0:T(128)S(1)} %stack.23.ids, bf16[2,64,2048]{2,1,0:T(8,128)(2,1)S(1)} %copy-done.1, bf16[2,64,2048]{2,1,0:T(8,128)(2,1)S(1)} %copy-done.2, bf16[1024,256]{1,0:T(8,128)(2,1)S(1)} %copy-done.4), custom_call_target="tpu_custom_call" | custom-call | flops 8000000 | bytes 4000000 | tf_op jit(solution)/shard_map/interior/pallas_call | solution.py:151
  28.2 2.2 %borders.3 = (bf16[208,256]{1,0:T(8,128)(2,1)S(1)}, bf16[208,256]{1,0:T(8,128)(2,1)S(1)}, bf16[208,256]{1,0:T(8,128)(2,1)S(1)}, bf16[208,256]{1,0:T(8,128)(2,1)S(1)}) custom-call(s32[6]{0:T(128)S(1)} %stack.23.ids, f32[4,64,1280]{2,1,0:T(8,128)S(1)} %get-tuple-element.56.ranged, f32[2,48,1280]{2,1,0:T(8,128)S(1)} %get-tuple-element.57.inside_field, ...), custom_call_target="tpu_custom_call" | custom-call | flops 1000000 | bytes 4000000 | tf_op jit(solution)/shard_map/borders/pallas_call | solution.py:138
  30.4 0.6 collective-permute-start.3
  31.1 0.9 %collective-permute-done.6.rest_1_ = bf16[208,256]{1,0:T(8,128)(2,1)S(1)} collective-permute-done((bf16[208,256]{1,0:T(8,128)(2,1)S(1)}, bf16[208,256]{1,0:T(8,128)(2,1)S(1)}, u32[]{:S(2)}, u32[]{:S(2)}) %collective-permute-start.6) | collective-permute-done | bytes 106528 | tf_op jit(solution)/shard_map/ppermute | solution.py:959
  32.0 1.9 %collective-permute-start.4 = (bf16[208,256]{1,0:T(8,128)(2,1)S(1)}, bf16[208,256]{1,0:T(8,128)(2,1)S(1)}, u32[]{:S(2)}, u32[]{:S(2)}) collective-permute-start(bf16[208,256]{1,0:T(8,128)(2,1)S(1)} %get-tuple-element.62), channel_id=1, source_target_pairs={{0,1},{1,0},{2,3},{3,2},{4,5},{5,4},{6,7},{7,6},{8,9},{9,8},{10,11... | collective-permute-start | bytes 319496 | tf_op jit(solution)/shard_map/ppermute | solution.py:959
  33.9 1.2 %far.1 = (f32[256,256]{1,0:T(8,128)S(1)}, f32[256,256]{1,0:T(8,128)S(1)}, f32[256,128]{1,0:T(8,128)S(1)}, f32[256,128]{1,0:T(8,128)S(1)}, f32[256,256]{1,0:T(8,1...) custom-call(s32[6]{0:T(128)S(1)} %stack.23.ids, ...), custom_call_target="tpu_custom_call" | custom-call | flops 1000000 | bytes 4000000 | tf_op jit(solution)/shard_map/far/pallas_call | solution.py:138
  35.1 1.0 %collective-permute-done.2.rest_0_ = bf16[208,256]{1,0:T(8,128)(2,1)S(1)} collective-permute-done((bf16[208,256]{1,0:T(8,128)(2,1)S(1)}, bf16[208,256]{1,0:T(8,128)(2,1)S(1)}, u32[]{:S(2)}, u32[]{:S(2)}) %collective-permute-start.2) | collective-permute-done | bytes 106528 | tf_op jit(solution)/shard_map/ppermute | solution.py:959
  36.3 1.4 %collective-permute-done.4.rest_2_ = bf16[208,256]{1,0:T(8,128)(2,1)S(1)} collective-permute-done((bf16[208,256]{1,0:T(8,128)(2,1)S(1)}, bf16[208,256]{1,0:T(8,128)(2,1)S(1)}, u32[]{:S(2)}, u32[]{:S(2)}) %collective-permute-start.4) | collective-permute-done | bytes 106528 | tf_op jit(solution)/shard_map/ppermute | solution.py:959
  37.8 4.1 %tiles.1 = (f32[512,256]{1,0:T(8,128)S(1)}, f32[512,256]{1,0:T(8,128)S(1)}, f32[512,256]{1,0:T(8,128)S(1)}, f32[512,128]{1,0:T(8,128)S(1)}, f32[520,256]{1,0:T(8...) custom-call(s32[6]{0:T(128)S(1)} %stack.23.ids, ...), custom_call_target="tpu_custom_call" | custom-call | flops 1000000 | bytes 4000000 | tf_op jit(solution)/shard_map/tiles/pallas_call | solution.py:138
  41.9 3.2 %collective-permute-start.9 = (f32[8,128]{1,0:T(8,128)S(1)}, f32[8,128]{1,0:T(8,128)S(1)}, u32[]{:S(2)}, u32[]{:S(2)}) collective-permute-start(f32[8,128]{1,0:T(8,128)S(1)} %get-tuple-element.81), channel_id=1, source_target_pairs={{0,7},{1,2},{2,1},{3,4},{4,3},{5,6},{6,5},{7,0},{8,15},{9,10},{10,... | collective-permute-start | bytes 12296 | tf_op jit(solution)/shard_map/ppermute | solution.py:897
  45.4 1.3 %collective-permute-start.12 = (f32[8,128]{1,0:T(8,128)S(1)}, f32[8,128]{1,0:T(8,128)S(1)}, u32[]{:S(2)}, u32[]{:S(2)}) collective-permute-start(f32[8,128]{1,0:T(8,128)S(1)} %get-tuple-element.84), channel_id=1, source_target_pairs={{0,8},{8,0},{16,24},{24,16},{1,9},{9,1},{17,25},{25,17},{2,10},{10... | collective-permute-start | bytes 12296 | tf_op jit(solution)/shard_map/ppermute | solution.py:897
  46.8 1.4 %collective-permute-done.9.col_next = f32[8,128]{1,0:T(8,128)S(1)} collective-permute-done((f32[8,128]{1,0:T(8,128)S(1)}, f32[8,128]{1,0:T(8,128)S(1)}, u32[]{:S(2)}, u32[]{:S(2)}) %collective-permute-start.9) | collective-permute-done | bytes 4128 | tf_op jit(solution)/shard_map/ppermute | solution.py:897
  48.7 4.6 %operator.1 = (f32[512,256]{1,0:T(8,128)S(1)}, f32[512,256]{1,0:T(8,128)S(1)}, f32[512,256]{1,0:T(8,128)S(1)}, bf16[16,128]{1,0:T(8,128)(2,1)S(1)}, f32[16,128]{1,0:T(8,128)S(1)}) custom-call(s32[6]{0:T(128)S(1)} %stack.23.ids, f32[512,256]{1,0:T(8,128)S(1)} %get-tuple-element.76.residual, f32[512,256]{1,0:T(8,128)S(1)} %get-tuple-element.77.shaped, ...), custom_call_target="tpu_custom_call" | custom-call | flops 1000000 | bytes 4000000 | tf_op jit(solution)/shard_map/operator/pallas_call | solution.py:138
  53.3 11.6 %all_to_all.5.gathered = bf16[32,16,128]{2,1,0:T(8,128)(2,1)S(1)} all-to-all(bf16[32,16,128]{2,1,0:T(8,128)(2,1)S(1)} %broadcast_in_dim.2), channel_id=1, replica_groups=mesh['row'=4,'col'=8] {'row','col'}, dimensions={0} | all-to-all | bytes 262144 | tf_op jit(solution)/shard_map/all_to_all | solution.py:1036
  64.9 2.1 %finish.1 = (f32[512,256]{1,0:T(8,128)}, f32[512,256]{1,0:T(8,128)}) custom-call(s32[6]{0:T(128)S(1)} %stack.23.ids, bf16[32,16,128]{2,1,0:T(8,128)(2,1)S(1)} %all_to_all.5.gathered, f32[512,256]{1,0:T(8,128)S(1)} %get-tuple-element.76.residual, f32[512,256]{1,0:T(8,128)S(1)} %get-tuple-element.77.shaped, f32[512,256]{1,0:T(8,128)S(1)} %get-tuple-element.86.operated, ...), custom_call_target="tpu_custom_call" | custom-call | flops 1000000 | bytes 4000000 | tf_op jit(solution)/shard_map/finish/pallas_call | solution.py:138
  (29 shorter events, 1.6 us)
Async XLA Ops:
  0.6 7.9 %copy-start.2 = (bf16[2,64,2048]{2,1,0:T(8,128)(2,1)S(1)}, bf16[2,64,2048]{2,1,0:T(8,128)(2,1)}, u32[]{:S(2)}) copy-start(bf16[2,64,2048]{2,1,0:T(8,128)(2,1)} %second.2) | copy-start | bytes 1572868
  0.6 7.9 %copy-start.1 = (bf16[2,64,2048]{2,1,0:T(8,128)(2,1)S(1)}, bf16[2,64,2048]{2,1,0:T(8,128)(2,1)}, u32[]{:S(2)}) copy-start(bf16[2,64,2048]{2,1,0:T(8,128)(2,1)} %first.2) | copy-start | bytes 1572868
  1.7 11.9 %collective-permute-start.1 = (bf16[4,8,2048]{2,1,0:T(8,128)(2,1)S(1)}, bf16[4,8,2048]{2,1,0:T(8,128)(2,1)S(1)}, u32[]{:S(2)}, u32[]{:S(2)}) collective-permute-start(bf16[4,8,2048]{2,1,0:T(8,128)(2,1)S(1)} %get-tuple-element.94), channel_id=1, source_target_pairs={{0,1},{1,0},{2,3},{3,2},{4,5},{5,4},{6,7},{7,6},{8,9},{9,8},{10,11... | collective-permute-start | bytes 393224 | tf_op jit(solution)/shard_map/ppermute | solution.py:897
  4.8 9.2 %collective-permute-start = (bf16[4,8,2048]{2,1,0:T(8,128)(2,1)S(1)}, bf16[4,8,2048]{2,1,0:T(8,128)(2,1)S(1)}, u32[]{:S(2)}, u32[]{:S(2)}) collective-permute-start(bf16[4,8,2048]{2,1,0:T(8,128)(2,1)S(1)} %get-tuple-element.95), channel_id=1, source_target_pairs={{0,31},{1,2},{2,1},{3,4},{4,3},{5,6},{6,5},{7,8},{8,7},{9,10},{10,... | collective-permute-start | bytes 393224 | tf_op jit(solution)/shard_map/ppermute | solution.py:897
  8.5 1.0 %copy-start.3 = (bf16[1024,256]{1,0:T(8,128)(2,1)S(1)}, bf16[1024,256]{1,0:T(8,128)(2,1)}, u32[]{:S(2)}) copy-start(bf16[1024,256]{1,0:T(8,128)(2,1)} %constant.40.clone.table) | copy-start | bytes 1572868
  13.7 10.2 %copy-start.4 = (bf16[1024,256]{1,0:T(8,128)(2,1)S(1)}, bf16[1024,256]{1,0:T(8,128)(2,1)}, u32[]{:S(2)}) copy-start(bf16[1024,256]{1,0:T(8,128)(2,1)} %constant.40.clone.table) | copy-start | bytes 1572868
  16.1 14.3 %collective-permute-start.5 = (bf16[208,256]{1,0:T(8,128)(2,1)S(1)}, bf16[208,256]{1,0:T(8,128)(2,1)S(1)}, u32[]{:S(2)}, u32[]{:S(2)}) collective-permute-start(bf16[208,256]{1,0:T(8,128)(2,1)S(1)} %get-tuple-element.64), channel_id=1, source_target_pairs={{0,4},{1,5},{2,6},{3,7},{4,0},{5,1},{6,2},{7,3},{8,12},{9,13},{10,... | collective-permute-start | bytes 319496 | tf_op jit(solution)/shard_map/ppermute | solution.py:959
  16.2 15.8 %collective-permute-start.6 = (bf16[208,256]{1,0:T(8,128)(2,1)S(1)}, bf16[208,256]{1,0:T(8,128)(2,1)S(1)}, u32[]{:S(2)}, u32[]{:S(2)}) collective-permute-start(bf16[208,256]{1,0:T(8,128)(2,1)S(1)} %get-tuple-element.65), channel_id=1, source_target_pairs={{0,5},{1,4},{2,7},{3,6},{4,1},{5,0},{6,3},{7,2},{8,13},{9,12},{10,... | collective-permute-start | bytes 319496 | tf_op jit(solution)/shard_map/ppermute | solution.py:959
  17.7 16.2 %collective-permute-start.7 = (bf16[208,256]{1,0:T(8,128)(2,1)S(1)}, bf16[208,256]{1,0:T(8,128)(2,1)S(1)}, u32[]{:S(2)}, u32[]{:S(2)}) collective-permute-start(bf16[208,256]{1,0:T(8,128)(2,1)S(1)} %get-tuple-element.66), channel_id=1, source_target_pairs={{0,6},{1,7},{2,4},{3,5},{4,2},{5,3},{6,0},{7,1},{8,14},{9,15},{10,... | collective-permute-start | bytes 319496 | tf_op jit(solution)/shard_map/ppermute | solution.py:959
  21.5 12.4 %collective-permute-start.8 = (bf16[208,256]{1,0:T(8,128)(2,1)S(1)}, bf16[208,256]{1,0:T(8,128)(2,1)S(1)}, u32[]{:S(2)}, u32[]{:S(2)}) collective-permute-start(bf16[208,256]{1,0:T(8,128)(2,1)S(1)} %get-tuple-element.67), channel_id=1, source_target_pairs={{0,7},{1,6},{2,5},{3,4},{4,3},{5,2},{6,1},{7,0},{8,15},{9,14},{10,... | collective-permute-start | bytes 319496 | tf_op jit(solution)/shard_map/ppermute | solution.py:959
  23.8 13.9 %copy-start.6 = (bf16[1024,256]{1,0:T(8,128)(2,1)S(1)}, bf16[1024,256]{1,0:T(8,128)(2,1)}, u32[]{:S(2)}) copy-start(bf16[1024,256]{1,0:T(8,128)(2,1)} %constant.42.clone.rest_13_.rest_1_) | copy-start | bytes 1572868
  28.1 9.6 %copy-start = (bf16[2048,512]{1,0:T(8,128)(2,1)S(1)}, bf16[2048,512]{1,0:T(8,128)(2,1)}, u32[]{:S(2)}) copy-start(bf16[2048,512]{1,0:T(8,128)(2,1)} %constant.41.clone.rest_12_.rest_0_) | copy-start | bytes 6291460
  28.2 9.6 %copy-start.5 = (f32[512,256]{1,0:T(8,128)S(1)}, f32[512,256]{1,0:T(8,128)}, u32[]{:S(2)}) copy-start(f32[512,256]{1,0:T(8,128)} %constant.43.clone.rest_14_.rest_2_) | copy-start | bytes 1572868
  30.4 5.8 %collective-permute-start.2 = (bf16[208,256]{1,0:T(8,128)(2,1)S(1)}, bf16[208,256]{1,0:T(8,128)(2,1)S(1)}, u32[]{:S(2)}, u32[]{:S(2)}) collective-permute-start(bf16[208,256]{1,0:T(8,128)(2,1)S(1)} %get-tuple-element.60), channel_id=1, source_target_pairs={{0,3},{1,2},{2,1},{3,0},{4,7},{5,6},{6,5},{7,4},{8,11},{9,10},{10,... | collective-permute-start | bytes 319496 | tf_op jit(solution)/shard_map/ppermute | solution.py:959
  30.4 5.9 %collective-permute-start.3 = (bf16[208,256]{1,0:T(8,128)(2,1)S(1)}, bf16[208,256]{1,0:T(8,128)(2,1)S(1)}, u32[]{:S(2)}, u32[]{:S(2)}) collective-permute-start(bf16[208,256]{1,0:T(8,128)(2,1)S(1)} %get-tuple-element.61), channel_id=1, source_target_pairs={{0,2},{1,3},{2,0},{3,1},{4,6},{5,7},{6,4},{7,5},{8,10},{9,11},{10,... | collective-permute-start | bytes 319496 | tf_op jit(solution)/shard_map/ppermute | solution.py:959
  32.0 5.7 %collective-permute-start.4 = (bf16[208,256]{1,0:T(8,128)(2,1)S(1)}, bf16[208,256]{1,0:T(8,128)(2,1)S(1)}, u32[]{:S(2)}, u32[]{:S(2)}) collective-permute-start(bf16[208,256]{1,0:T(8,128)(2,1)S(1)} %get-tuple-element.62), channel_id=1, source_target_pairs={{0,1},{1,0},{2,3},{3,2},{4,5},{5,4},{6,7},{7,6},{8,9},{9,8},{10,11... | collective-permute-start | bytes 319496 | tf_op jit(solution)/shard_map/ppermute | solution.py:959
  41.9 6.4 %collective-permute-start.9 = (f32[8,128]{1,0:T(8,128)S(1)}, f32[8,128]{1,0:T(8,128)S(1)}, u32[]{:S(2)}, u32[]{:S(2)}) collective-permute-start(f32[8,128]{1,0:T(8,128)S(1)} %get-tuple-element.81), channel_id=1, source_target_pairs={{0,7},{1,2},{2,1},{3,4},{4,3},{5,6},{6,5},{7,0},{8,15},{9,10},{10,... | collective-permute-start | bytes 12296 | tf_op jit(solution)/shard_map/ppermute | solution.py:897
  45.1 3.6 %collective-permute-start.10 = (f32[8,128]{1,0:T(8,128)S(1)}, f32[8,128]{1,0:T(8,128)S(1)}, u32[]{:S(2)}, u32[]{:S(2)}) collective-permute-start(f32[8,128]{1,0:T(8,128)S(1)} %get-tuple-element.82), channel_id=1, source_target_pairs={{0,1},{1,0},{2,3},{3,2},{4,5},{5,4},{6,7},{7,6},{8,9},{9,8},{10,11... | collective-permute-start | bytes 12296 | tf_op jit(solution)/shard_map/ppermute | solution.py:897
  45.1 3.6 %collective-permute-start.11 = (f32[8,128]{1,0:T(8,128)S(1)}, f32[8,128]{1,0:T(8,128)S(1)}, u32[]{:S(2)}, u32[]{:S(2)}) collective-permute-start(f32[8,128]{1,0:T(8,128)S(1)} %get-tuple-element.83), channel_id=1, source_target_pairs={{0,24},{8,16},{16,8},{24,0},{1,25},{9,17},{17,9},{25,1},{2,26},{10... | collective-permute-start | bytes 12296 | tf_op jit(solution)/shard_map/ppermute | solution.py:897
  45.4 3.3 %collective-permute-start.12 = (f32[8,128]{1,0:T(8,128)S(1)}, f32[8,128]{1,0:T(8,128)S(1)}, u32[]{:S(2)}, u32[]{:S(2)}) collective-permute-start(f32[8,128]{1,0:T(8,128)S(1)} %get-tuple-element.84), channel_id=1, source_target_pairs={{0,8},{8,0},{16,24},{24,16},{1,9},{9,1},{17,25},{25,17},{2,10},{10... | collective-permute-start | bytes 12296 | tf_op jit(solution)/shard_map/ppermute | solution.py:897
